TPU v7x, 32 devices: a whole 2x2x4 slice. The times are simulated.
32 devices in a mesh: dp: 8 (over z, y), blk: 4 (over x, core).
Axes of the slice: x: 2, y: 2, z: 4, core: 2. Of those that a mesh axis runs over, the one named last changes fastest.
Arguments:
- embedded: bfloat16 [16, 2048, 768], P('dp', 'blk'), may hold values from -6 to 6
- species_flag: int32 [16], P('dp'), may hold values 0 or 1
- gene_ids: int32 [16, 2048], P('dp', 'blk'), may hold values from 0 to 35999, as said below
- species_table: float32 [2, 768], replicated, may hold values from -3 to 3
- norm_gain: float32 [2, 2, 768], replicated, may hold values from 0.1 to 1.9
- norm_bias: float32 [2, 2, 768], replicated, may hold values from -1.8 to 1.8
- w_qkv: bfloat16 [2, 768, 2304], replicated, may hold values from -0.3125 to 0.3125
- w_out: bfloat16 [2, 768, 768], replicated, may hold values from -0.875 to 0.875
- w_up: bfloat16 [2, 768, 3072], replicated, may hold values from -0.21875 to 0.21875
- w_down: bfloat16 [2, 3072, 768], replicated, may hold values from -0.109375 to 0.109375
- out_cotangent: bfloat16 [16, 2048, 768], P('dp', 'blk'), may hold values from -6 to 6
Outputs:
- hidden_out: float32 [16, 2048, 768], P('dp', 'blk')
- embed_grad: float32 [16, 2048, 768], P('dp', 'blk')
- species_grad: float32 [2, 768], replicated
- gain_grad: float32 [2, 2, 768], replicated
- bias_grad: float32 [2, 2, 768], replicated
- w_qkv_grad: float32 [2, 768, 2304], P(None, 'dp', 'blk')
- w_out_grad: float32 [2, 768, 768], P(None, 'dp', 'blk')
- w_up_grad: float32 [2, 768, 3072], P(None, 'dp', 'blk')
- w_down_grad: float32 [2, 3072, 768], P(None, 'dp', 'blk')
Inputs may be any that keep to these rules, and one draw needn't show every extreme that they name: `gene_ids`: in each cell the nonzero ids form a leading run of one or more positions and all later positions are 0 (padding); in each group of 2 consecutive cells one cell has no padding.
All inputs are finite; a program needn't handle non-finite values. No bound on the sum of `species_flag` on one device may be relied on, other than what follows from the above.
Results may differ from a plain program's by a relative error of at most 0.017.
Values may be sent and summed in bfloat16 or wider, within the bound.
No kernel may reach another device: no remote copies, remote signals or barrier semaphores. Data moves between devices by JAX's collectives and lax.ppermute only.
A program may use at most 704 MiB of HBM per device.

v0:
```python
import math

import jax
import jax.numpy as jnp
from jax import lax
from jax.sharding import PartitionSpec as P

HEADS = 12
HEAD_DIM = 64
LAYERS = 2


def layer_norm(value, gain, bias):
    mean = jnp.mean(value, axis=-1, keepdims=True)
    centred = value - mean
    variance = jnp.mean(centred * centred, axis=-1, keepdims=True)
    return centred * lax.rsqrt(variance + 1e-05) * gain + bias


def gelu_exact(value):
    return jax.nn.gelu(value, approximate=False)


def matmul(left, right):
    return jnp.dot(left, right, preferred_element_type=jnp.float32)


def outer_product(left, right):
    return lax.dot_general(
        left, right, (((0,), (0,)), ((), ())), preferred_element_type=jnp.float32
    )


def contract(left, right):
    return lax.dot_general(
        left, right, (((1,), (1,)), ((), ())), preferred_element_type=jnp.float32
    )


def shards(
    embedded,
    species_flag,
    gene_ids,
    species_table,
    norm_gain,
    norm_bias,
    w_qkv,
    w_out,
    w_up,
    w_down,
    out_cotangent,
):
    cell_count, block_len, model_width = embedded.shape
    head_count = HEADS
    head_size = HEAD_DIM
    seq_len = block_len * lax.axis_size("blk")
    row_count = cell_count * block_len
    scale = 1.0 / math.sqrt(head_size)
    picked = (species_flag[:, None] == jnp.arange(2, dtype=jnp.int32)[None, :]).astype(jnp.float32)

    def embed(table):
        added = jnp.dot(picked, table, precision=lax.Precision.HIGHEST)
        return (embedded.astype(jnp.float32) + added[:, None, :]).reshape(row_count, model_width)

    state, embed_back = jax.vjp(embed, species_table)
    live = gene_ids != 0
    counts = jnp.sum(live.astype(jnp.float32), axis=1)
    lengths = lax.psum(counts, "blk")
    fixed_valid = jnp.arange(seq_len, dtype=jnp.float32)[None, :] < lengths[:, None]

    def share_keys(qkv):
        pairs = qkv.reshape(cell_count, block_len, 3 * model_width)[:, :, model_width:]
        return (lax.all_gather(pairs, "blk", axis=1, tiled=True), fixed_valid)

    def attend(qkv, pairs_all, valid):
        queries = qkv[:, :model_width].reshape(cell_count, block_len, head_count, head_size)
        keys_all = pairs_all[:, :, :model_width].reshape(cell_count, seq_len, head_count, head_size)
        values_all = pairs_all[:, :, model_width:].reshape(
            cell_count, seq_len, head_count, head_size
        )
        scores = (
            jnp.einsum("cqhd,ckhd->chqk", queries, keys_all, preferred_element_type=jnp.float32)
            * scale
        )
        scores = jnp.where(valid[:, None, None, :], scores, -1e30)
        shifted = jnp.exp(scores - jnp.max(scores, axis=-1, keepdims=True))
        probs = shifted / jnp.sum(shifted, axis=-1, keepdims=True)
        probs_low = probs.astype(jnp.bfloat16)
        attended = jnp.einsum(
            "chqk,ckhd->cqhd", probs_low, values_all, preferred_element_type=jnp.float32
        )
        attended = attended.reshape(row_count, model_width).astype(jnp.bfloat16)
        return (queries, keys_all, values_all, probs, probs_low, attended)

    inputs = []
    for layer in range(LAYERS):
        inputs.append(state)
        normed = layer_norm(state, norm_gain[layer, 0], norm_bias[layer, 0]).astype(jnp.bfloat16)
        qkv = matmul(normed, w_qkv[layer]).astype(jnp.bfloat16)
        pairs_all, valid = share_keys(qkv)
        attended = attend(qkv, pairs_all, valid)[5]
        middle = state + matmul(attended, w_out[layer])
        normed_two = layer_norm(middle, norm_gain[layer, 1], norm_bias[layer, 1]).astype(
            jnp.bfloat16
        )
        active = gelu_exact(matmul(normed_two, w_up[layer])).astype(jnp.bfloat16)
        state = middle + matmul(active, w_down[layer])
    hidden_out = state.reshape(cell_count, block_len, model_width)
    grad = out_cotangent.astype(jnp.float32).reshape(row_count, model_width)
    qkv_list, out_list, up_list, down_list, gain_list, bias_list = ([], [], [], [], [], [])
    for layer in reversed(range(LAYERS)):
        start_state = inputs[layer]
        normed_f, norm_back = jax.vjp(
            layer_norm, start_state, norm_gain[layer, 0], norm_bias[layer, 0]
        )
        normed = normed_f.astype(jnp.bfloat16)
        qkv = matmul(normed, w_qkv[layer]).astype(jnp.bfloat16)
        pairs_all, valid = share_keys(qkv)
        queries, keys_all, values_all, probs, probs_low, attended = attend(qkv, pairs_all, valid)
        middle = start_state + matmul(attended, w_out[layer])
        normed_two_f, norm_two_back = jax.vjp(
            layer_norm, middle, norm_gain[layer, 1], norm_bias[layer, 1]
        )
        normed_two = normed_two_f.astype(jnp.bfloat16)
        upward = matmul(normed_two, w_up[layer])
        active_f, gelu_back = jax.vjp(gelu_exact, upward)
        active = active_f.astype(jnp.bfloat16)
        grad_y = grad.astype(jnp.bfloat16)
        down_grad = outer_product(active, grad_y)
        d_up = gelu_back(contract(grad_y, w_down[layer]))[0].astype(jnp.bfloat16)
        up_grad = outer_product(normed_two, d_up)
        d_middle, gain_two, bias_two = norm_two_back(contract(d_up, w_up[layer]))
        d_middle = grad + d_middle
        grad_z = d_middle.astype(jnp.bfloat16)
        out_grad = outer_product(attended, grad_z)
        d_att = (
            contract(grad_z, w_out[layer])
            .astype(jnp.bfloat16)
            .reshape(cell_count, block_len, head_count, head_size)
        )
        d_probs = jnp.einsum(
            "cqhd,ckhd->chqk", d_att, values_all, preferred_element_type=jnp.float32
        )
        row_terms = jnp.sum(probs * d_probs, axis=-1, keepdims=True)
        d_scores = (probs * (d_probs - row_terms)).astype(jnp.bfloat16)
        d_queries = (
            jnp.einsum("chqk,ckhd->cqhd", d_scores, keys_all, preferred_element_type=jnp.float32)
            * scale
        )
        d_keys = (
            jnp.einsum("chqk,cqhd->ckhd", d_scores, queries, preferred_element_type=jnp.float32)
            * scale
        )
        d_values = jnp.einsum(
            "chqk,cqhd->ckhd", probs_low, d_att, preferred_element_type=jnp.float32
        )
        d_pairs = jnp.concatenate(
            [
                d_keys.reshape(cell_count, seq_len, model_width),
                d_values.reshape(cell_count, seq_len, model_width),
            ],
            axis=-1,
        )
        d_pairs = lax.psum_scatter(
            d_pairs.astype(jnp.bfloat16), "blk", scatter_dimension=1, tiled=True
        ).astype(jnp.float32)
        d_qkv = jnp.concatenate(
            [d_queries.reshape(cell_count, block_len, model_width), d_pairs], axis=-1
        )
        d_qkv = d_qkv.astype(jnp.bfloat16).reshape(row_count, 3 * model_width)
        qkv_grad = outer_product(normed, d_qkv)
        d_start, gain_one, bias_one = norm_back(contract(d_qkv, w_qkv[layer]))
        grad = d_middle + d_start
        qkv_list.insert(0, qkv_grad)
        out_list.insert(0, out_grad)
        up_list.insert(0, up_grad)
        down_list.insert(0, down_grad)
        gain_list.insert(0, jnp.stack([gain_one, gain_two]))
        bias_list.insert(0, jnp.stack([bias_one, bias_two]))
    embed_grad = grad.reshape(cell_count, block_len, model_width)
    table_grad = embed_back(grad)[0]
    species_grad, gain_grad, bias_grad = lax.psum(
        (table_grad, jnp.stack(gain_list), jnp.stack(bias_list)), ("dp", "blk")
    )
    qkv_sum = jnp.stack(qkv_list)
    out_sum = jnp.stack(out_list)
    up_sum = jnp.stack(up_list)
    down_sum = jnp.stack(down_list)
    qkv_part, out_part, up_part, down_part = (
        lax.psum_scatter(
            qkv_sum.astype(jnp.bfloat16), "dp", scatter_dimension=1, tiled=True
        ).astype(jnp.float32),
        lax.psum_scatter(
            out_sum.astype(jnp.bfloat16), "dp", scatter_dimension=1, tiled=True
        ).astype(jnp.float32),
        lax.psum_scatter(up_sum.astype(jnp.bfloat16), "dp", scatter_dimension=1, tiled=True).astype(
            jnp.float32
        ),
        lax.psum_scatter(
            down_sum.astype(jnp.bfloat16), "dp", scatter_dimension=1, tiled=True
        ).astype(jnp.float32),
    )
    qkv_fin, out_fin, up_fin, down_fin = (
        lax.psum_scatter(
            qkv_part.astype(jnp.bfloat16), "blk", scatter_dimension=2, tiled=True
        ).astype(jnp.float32),
        lax.psum_scatter(
            out_part.astype(jnp.bfloat16), "blk", scatter_dimension=2, tiled=True
        ).astype(jnp.float32),
        lax.psum_scatter(
            up_part.astype(jnp.bfloat16), "blk", scatter_dimension=2, tiled=True
        ).astype(jnp.float32),
        lax.psum_scatter(
            down_part.astype(jnp.bfloat16), "blk", scatter_dimension=2, tiled=True
        ).astype(jnp.float32),
    )
    return (
        hidden_out,
        embed_grad,
        species_grad,
        gain_grad,
        bias_grad,
        qkv_fin,
        out_fin,
        up_fin,
        down_fin,
    )


def solution(mesh):
    placed = (
        P("dp", "blk", None),
        P("dp"),
        P("dp", "blk"),
        P(),
        P(),
        P(),
        P(),
        P(),
        P(),
        P(),
        P("dp", "blk", None),
    )
    return jax.shard_map(
        shards,
        mesh=mesh,
        in_specs=placed,
        out_specs=(
            P("dp", "blk", None),
            P("dp", "blk", None),
            P(),
            P(),
            P(),
            P(None, "dp", "blk"),
            P(None, "dp", "blk"),
            P(None, "dp", "blk"),
            P(None, "dp", "blk"),
        ),
        check_vma=False,
    )
```

profile of v0, /device:TPU:0, one launch (start us, length us, event | category | flops | bytes accessed | tf_op | source)
XLA Modules:
  0.0 1930.6 jit_solution(6065221581644138115)
XLA Ops:
  40.0 72.3 %all-gather.3.cloned.1.call-done = bf16[2,2048,1536]{2,1,0:T(8,128)(2,1)} async-done(((bf16[2,512,1536]{2,1,0:T(8,128)(2,1)}), bf16[2,2048,1536]{2,1,0:T(8,128)(2,1)}) %all-gather.3.cloned.1.call-update) | async-done | bytes 12582928 | tf_op jit(solution)/shard_map/all_gather | solution.py:73
  139.9 39.5 %fusion.163 = (f32[2,12,512]{2,1,0:T(8,128)S(1)}, f32[2,12,512,2048]{3,2,1,0:T(8,128)}) fusion(pred[2,2048]{1,0:T(4,128)(4,1)S(1)} %iota_compare_fusion, bf16[2,2048,12,64]{1,3,2,0:T(8,128)(2,1)} %bitcast.206, bf16[2,512,12,64]{1,0,3,2:T(2,128)(2,1)S(1)} %reshape.326), kind=kOutput, calls=%fused_computation.254 | convolution fusion | flops 3321890816 | bytes 108580864 | tf_op jit(solution)/shard_map/sub | solution.py:86
  179.3 45.6 %fusion.97 = bf16[2,512,12,64]{1,3,2,0:T(8,128)(2,1)S(1)} fusion(bf16[2,2048,12,64]{1,3,2,0:T(8,128)(2,1)} %bitcast.213, f32[2,12,512,2048]{3,2,1,0:T(8,128)} %get-tuple-element.83, f32[2,12,512]{2,1,0:T(8,128)S(1)} %get-tuple-element.82), kind=kOutput, calls=%fused_computation.166 | convolution fusion | flops 3272343552 | bytes 108576768 | tf_op jit(solution)/shard_map/chqk,ckhd->cqhd/dot_general | solution.py:89
  231.3 35.1 %multiply_convert_fusion.5 = (bf16[1024,3072]{1,0:T(8,128)(2,1)}, f32[1024,3072]{1,0:T(8,128)}, f32[1024,3072]{1,0:T(8,128)}) fusion(bf16[2,768,3072]{2,1,0:T(8,128)(2,1)S(1)} %bitcast.243, f32[1024,768]{1,0:T(8,128)S(1)} %get-tuple-element.85, f32[768]{0:T(1024)S(1)} %copy-done.78, f32[768]{0:T(1024)S(1)} %copy-done.59, f32[1024]{0:T(1024)S(1)} %fusion.137, ...), kind=kOutput, calls=%fused_computation.51 | convolution fusion | flops 5040242688 | bytes 39337984 | tf_op jit(solution)/shard_map/dot_general | solution.py:25
  288.9 78.8 %all-gather.5.cloned.1.call-done = bf16[2,2048,1536]{2,1,0:T(8,128)(2,1)} async-done(((bf16[2,512,1536]{2,1,0:T(8,128)(2,1)}), bf16[2,2048,1536]{2,1,0:T(8,128)(2,1)}) %all-gather.5.cloned.1.call-update) | async-done | bytes 12582928 | tf_op jit(solution)/shard_map/all_gather | solution.py:73
  395.4 39.4 %fusion.170 = (f32[2,12,512]{2,1,0:T(8,128)S(1)}, f32[2,12,512,2048]{3,2,1,0:T(8,128)}) fusion(pred[2,2048]{1,0:T(4,128)(4,1)S(1)} %copy-done.75, bf16[2,2048,12,64]{1,3,2,0:T(8,128)(2,1)} %bitcast.208, bf16[2,512,12,64]{1,0,3,2:T(2,128)(2,1)S(1)} %reshape.330), kind=kOutput, calls=%fused_computation.257 | convolution fusion | flops 3321890816 | bytes 108580864 | tf_op jit(solution)/shard_map/sub | solution.py:86
  434.8 35.0 %fusion.94 = bf16[2,512,12,64]{1,3,2,0:T(8,128)(2,1)S(1)} fusion(bf16[2,2048,12,64]{1,3,2,0:T(8,128)(2,1)} %bitcast.215, f32[2,12,512,2048]{3,2,1,0:T(8,128)} %get-tuple-element.90, f32[2,12,512]{2,1,0:T(8,128)S(1)} %get-tuple-element.89), kind=kOutput, calls=%fused_computation.165 | convolution fusion | flops 3272343552 | bytes 108576768 | tf_op jit(solution)/shard_map/chqk,ckhd->cqhd/dot_general | solution.py:89
  476.1 35.3 %multiply_convert_fusion.4 = (bf16[1024,3072]{1,0:T(8,128)(2,1)}, f32[1024,3072]{1,0:T(8,128)}, f32[1024,3072]{1,0:T(8,128)}) fusion(bf16[2,768,3072]{2,1,0:T(8,128)(2,1)S(1)} %bitcast.245, f32[1024,768]{1,0:T(8,128)S(1)} %get-tuple-element.92, f32[768]{0:T(1024)S(1)} %copy-done.80, f32[768]{0:T(1024)S(1)} %copy-done.62, f32[1024]{0:T(1024)S(1)} %fusion.139, ...), kind=kOutput, calls=%fused_computation.38 | convolution fusion | flops 5040242688 | bytes 39337984 | tf_op jit(solution)/shard_map/dot_general | solution.py:25
  545.0 34.7 %fusion.51 = bf16[2,12,64,2048]{3,2,1,0:T(8,128)(2,1)} fusion(bf16[2,512,12,64]{1,0,3,2:T(2,128)(2,1)S(1)} %reshape.335, f32[2,12,512,2048]{3,2,1,0:T(8,128)} %get-tuple-element.90, f32[2,12,512]{2,1,0:T(8,128)S(1)} %get-tuple-element.89), kind=kOutput, calls=%fused_computation.100 | convolution fusion | flops 3274702848 | bytes 108576768 | tf_op jit(solution)/shard_map/chqk,cqhd->ckhd/dot_general | solution.py:154
  579.8 65.2 %multiply_reduce_fusion.1 = (f32[2,12,512]{2,1,0:T(8,128)S(1)}, f32[2,12,512,2048]{3,2,1,0:T(8,128)}) fusion(f32[2,12,512,2048]{3,2,1,0:T(8,128)} %get-tuple-element.90, f32[2,12,512]{2,1,0:T(8,128)S(1)} %get-tuple-element.89, bf16[2,2048,12,64]{1,3,2,0:T(8,128)(2,1)} %bitcast.216, bf16[2,512,12,64]{1,0,3,2:T(2,128)(2,1)S(1)} %reshape.335), kind=kOutput, calls=%fused_computation.5 | convolution fusion | flops 3296710656 | bytes 209289216 | tf_op jit(solution)/shard_map/cqhd,ckhd->chqk/dot_general | solution.py:141
  653.6 78.0 %multiply_convert_fusion.1 = bf16[2,12,512,2048]{3,2,1,0:T(8,128)(2,1)} fusion(f32[2,12,512,2048]{3,2,1,0:T(8,128)} %get-tuple-element.96, f32[2,12,512]{2,1,0:T(8,128)S(1)} %get-tuple-element.95, f32[2,12,512,2048]{3,2,1,0:T(8,128)} %get-tuple-element.90, f32[2,12,512]{2,1,0:T(8,128)S(1)} %get-tuple-element.89), kind=kLoop, calls=%fused_computation.4 | loop fusion | flops 100663296 | bytes 251756544 | tf_op jit(solution)/shard_map/convert_element_type | solution.py:145
  772.0 29.2 %fusion.92 = bf16[2,512,12,64]{1,3,2,0:T(8,128)(2,1)} fusion(bf16[2,2048,12,64]{1,3,2,0:T(8,128)(2,1)} %bitcast.209, bf16[2,12,512,2048]{3,2,1,0:T(8,128)(2,1)} %multiply_convert_fusion.1), kind=kOutput, calls=%fused_computation.163 | convolution fusion | flops 3222798336 | bytes 58195968 | tf_op jit(solution)/shard_map/chqk,ckhd->cqhd/dot_general | solution.py:147
  808.5 62.6 %reduce-scatter.14.cloned.1.call-done = bf16[2,512,1536]{2,1,0:T(8,128)(2,1)} async-done(((bf16[2,2048,1536]{2,1,0:T(8,128)(2,1)}), bf16[2,512,1536]{2,1,0:T(8,128)(2,1)}) %reduce-scatter.14.cloned.1.call-update) | async-done | bytes 3145744 | tf_op jit(solution)/shard_map/reduce_scatter | solution.py:164
  919.9 34.8 %fusion.48 = bf16[2,12,64,2048]{3,2,1,0:T(8,128)(2,1)} fusion(bf16[2,512,12,64]{1,0,3,2:T(2,128)(2,1)S(1)} %reshape.338, f32[2,12,512,2048]{3,2,1,0:T(8,128)} %get-tuple-element.83, f32[2,12,512]{2,1,0:T(8,128)S(1)} %copy-done.37), kind=kOutput, calls=%fused_computation.99 | convolution fusion | flops 3274702848 | bytes 108576768 | tf_op jit(solution)/shard_map/chqk,cqhd->ckhd/dot_general | solution.py:154
  954.7 65.3 %multiply_reduce_fusion = (f32[2,12,512]{2,1,0:T(8,128)S(1)}, f32[2,12,512,2048]{3,2,1,0:T(8,128)}) fusion(f32[2,12,512,2048]{3,2,1,0:T(8,128)} %get-tuple-element.83, f32[2,12,512]{2,1,0:T(8,128)S(1)} %copy-done.37, bf16[2,2048,12,64]{1,3,2,0:T(8,128)(2,1)} %bitcast.214, bf16[2,512,12,64]{1,0,3,2:T(2,128)(2,1)S(1)} %reshape.338), kind=kOutput, calls=%fused_computation.3 | convolution fusion | flops 3296710656 | bytes 209289216 | tf_op jit(solution)/shard_map/cqhd,ckhd->chqk/dot_general | solution.py:141
  1028.6 78.0 %multiply_convert_fusion = bf16[2,12,512,2048]{3,2,1,0:T(8,128)(2,1)} fusion(f32[2,12,512,2048]{3,2,1,0:T(8,128)} %get-tuple-element.100, f32[2,12,512]{2,1,0:T(8,128)S(1)} %get-tuple-element.99, f32[2,12,512,2048]{3,2,1,0:T(8,128)} %get-tuple-element.83, f32[2,12,512]{2,1,0:T(8,128)S(1)} %copy-done.37), kind=kLoop, calls=%fused_computation.2 | loop fusion | flops 100663296 | bytes 251756544 | tf_op jit(solution)/shard_map/convert_element_type | solution.py:145
  1215.9 22.9 %fusion.93 = bf16[2,512,12,64]{1,3,2,0:T(8,128)(2,1)S(1)} fusion(bf16[2,2048,12,64]{1,3,2,0:T(8,128)(2,1)} %bitcast.207, bf16[2,12,512,2048]{3,2,1,0:T(8,128)(2,1)} %multiply_convert_fusion), kind=kOutput, calls=%fused_computation.164 | convolution fusion | flops 3222798336 | bytes 58195968 | tf_op jit(solution)/shard_map/chqk,ckhd->cqhd/dot_general | solution.py:147
  1271.2 47.8 %reduce-scatter.20.cloned.1.call-done = bf16[2,96,768]{2,1,0:T(8,128)(2,1)} async-done(((bf16[2,768,768]{2,1,0:T(8,128)(2,1)}), bf16[2,96,768]{2,1,0:T(8,128)(2,1)}) %reduce-scatter.20.cloned.1.call-update) | async-done | bytes 294928 | tf_op jit(solution)/shard_map/reduce_scatter | solution.py:193
  1321.3 163.7 %reduce-scatter.26.cloned.1.call-done = bf16[2,384,768]{2,1,0:T(8,128)(2,1)} async-done(((bf16[2,3072,768]{2,1,0:T(8,128)(2,1)}), bf16[2,384,768]{2,1,0:T(8,128)(2,1)}) %reduce-scatter.26.cloned.1.call-update) | async-done | bytes 1179664 | tf_op jit(solution)/shard_map/reduce_scatter | solution.py:199
  1489.8 161.3 %reduce-scatter.22.cloned.1.call-done = bf16[2,96,3072]{2,1,0:T(8,128)(2,1)} async-done(((bf16[2,768,3072]{2,1,0:T(8,128)(2,1)}), bf16[2,96,3072]{2,1,0:T(8,128)(2,1)}) %reduce-scatter.22.cloned.1.call-update) | async-done | bytes 1179664 | tf_op jit(solution)/shard_map/reduce_scatter | solution.py:196
  1662.3 120.7 %reduce-scatter.18.cloned.1.call-done = bf16[2,96,2304]{2,1,0:T(8,128)(2,1)} async-done(((bf16[2,768,2304]{2,1,0:T(8,128)(2,1)}), bf16[2,96,2304]{2,1,0:T(8,128)(2,1)}) %reduce-scatter.18.cloned.1.call-update) | async-done | bytes 884752 | tf_op jit(solution)/shard_map/reduce_scatter | solution.py:190
  1807.9 37.9 %all-reduce.4.cloned.1.call-done = bf16[2,384,768]{1,0,2:T(2,128)(2,1)} async-done(((bf16[2,384,768]{1,0,2:T(2,128)(2,1)}), bf16[2,384,768]{1,0,2:T(2,128)(2,1)}) %all-reduce.4.cloned.1.call-update) | async-done | bytes 1179664
  1847.8 26.6 %reduce-scatter.24.cloned.1.call-done = bf16[2,96,768]{2,1,0:T(8,128)(2,1)} async-done(((bf16[2,96,3072]{2,1,0:T(8,128)(2,1)}), bf16[2,96,768]{2,1,0:T(8,128)(2,1)}) %reduce-scatter.24.cloned.1.call-update) | async-done | bytes 294928 | tf_op jit(solution)/shard_map/reduce_scatter | solution.py:210
  1880.9 40.5 %all-reduce.1 = (f32[2,768]{1,0:T(2,128)}, f32[2,2,768]{2,1,0:T(2,128)}, f32[2,2,768]{2,1,0:T(2,128)}) all-reduce(f32[2,768]{1,0:T(2,128)S(1)} %fusion.142, f32[2,2,768]{2,1,0:T(2,128)S(1)} %pad_maximum_fusion.12, f32[2,2,768]{2,1,0:T(2,128)S(1)} %pad_maximum_fusion.13), channel_id=1, replica_groups=mesh['dp'=8,'blk'=4] {'dp','blk'}, use_global_device_ids=true, to_apply=%region_27.28 | all-reduce | flops 7680 | bytes 61440 | tf_op jit(solution)/shard_map/psum | solution.py:182
  (371 shorter events, 463.8 us)
Async XLA Ops:
  7.2 105.1 %all-gather.3.cloned.1.call-start = ((), (), s32[]{:S(2)}) async-start(), calls=%async_computation.9 | async-start | bytes 15728640 | tf_op jit(solution)/shard_map/all_gather | solution.py:73
  27.3 340.4 %all-gather.5.cloned.1.call-start = ((), (), s32[]{:S(2)}) async-start(), calls=%async_computation.10 | async-start | bytes 15728640 | tf_op jit(solution)/shard_map/all_gather | solution.py:73
  39.9 99.9 %copy-start.24 = (bf16[2,512,12,64]{1,0,3,2:T(2,128)(2,1)}, bf16[2,512,12,64]{1,0,3,2:T(2,128)(2,1)S(1)}, u32[]{:S(2)}) copy-start(bf16[2,512,12,64]{1,0,3,2:T(2,128)(2,1)S(1)} %reshape.326) | copy-start | bytes 4718596
  40.0 99.9 %copy-start.74 = (pred[2,2048]{1,0:T(4,128)(4,1)}, pred[2,2048]{1,0:T(4,128)(4,1)S(1)}, u32[]{:S(2)}) copy-start(pred[2,2048]{1,0:T(4,128)(4,1)S(1)} %iota_compare_fusion) | copy-start | bytes 12292
  285.4 585.8 %reduce-scatter.14.cloned.1.call-start = ((), (), s32[]{:S(2)}) async-start(), calls=%async_computation.11 | async-start | bytes 15728640 | tf_op jit(solution)/shard_map/reduce_scatter | solution.py:164
  288.9 106.5 %copy-start.26 = (bf16[2,512,12,64]{1,0,3,2:T(2,128)(2,1)}, bf16[2,512,12,64]{1,0,3,2:T(2,128)(2,1)S(1)}, u32[]{:S(2)}) copy-start(bf16[2,512,12,64]{1,0,3,2:T(2,128)(2,1)S(1)} %reshape.330) | copy-start | bytes 4718596
  653.6 78.0 %copy-start.27 = (bf16[2,512,12,64]{1,0,3,2:T(2,128)(2,1)S(1)}, bf16[2,512,12,64]{1,0,3,2:T(2,128)(2,1)}, u32[]{:S(2)}) copy-start(bf16[2,512,12,64]{1,0,3,2:T(2,128)(2,1)} %copy-done.26) | copy-start | bytes 4718596
  772.0 480.0 %reduce-scatter.16.cloned.1.call-start = ((), (), s32[]{:S(2)}) async-start(), calls=%async_computation.12 | async-start | bytes 15728640 | tf_op jit(solution)/shard_map/reduce_scatter | solution.py:164
  1147.3 171.7 %reduce-scatter.20.cloned.1.call-start = ((), (), s32[]{:S(2)}) async-start(), calls=%async_computation.14 | async-start | bytes 2654208 | tf_op jit(solution)/shard_map/reduce_scatter | solution.py:193
  1153.9 331.0 %reduce-scatter.26.cloned.1.call-start = ((), (), s32[]{:S(2)}) async-start(), calls=%async_computation.17 | async-start | bytes 10616832 | tf_op jit(solution)/shard_map/reduce_scatter | solution.py:199
  1184.7 466.4 %reduce-scatter.22.cloned.1.call-start = ((), (), s32[]{:S(2)}) async-start(), calls=%async_computation.15 | async-start | bytes 10616832 | tf_op jit(solution)/shard_map/reduce_scatter | solution.py:196
  1215.3 567.7 %reduce-scatter.18.cloned.1.call-start = ((), (), s32[]{:S(2)}) async-start(), calls=%async_computation.13 | async-start | bytes 7962624 | tf_op jit(solution)/shard_map/reduce_scatter | solution.py:190
  1271.1 381.3 %copy-start.83 = (f32[768]{0:T(1024)S(1)}, f32[768]{0:T(1024)}, u32[]{:S(2)}) copy-start(f32[768]{0:T(1024)} %get-tuple-element.42) | copy-start | bytes 9220
  1271.1 381.3 %copy-start.82 = (f32[768]{0:T(1024)S(1)}, f32[768]{0:T(1024)}, u32[]{:S(2)}) copy-start(f32[768]{0:T(1024)} %get-tuple-element.47) | copy-start | bytes 9220
  1271.1 381.4 %copy-start.8 = (f32[1024,768]{1,0:T(8,128)S(1)}, f32[1024,768]{1,0:T(8,128)}, u32[]{:S(2)}) copy-start(f32[1024,768]{1,0:T(8,128)} %copy-done.6) | copy-start | bytes 9437188
  1271.1 535.0 %reduce-scatter.30.cloned.1.call-start = ((), (), s32[]{:S(2)}) async-start(), calls=%async_computation.19 | async-start | bytes 491520
  1321.2 330.0 %copy-start.95 = (u32[32]{0:T(128)S(1)}, u32[32]{0:T(128)}, u32[]{:S(2)}) copy-start(u32[32]{0:T(128)} %constant.101) | copy-start | bytes 388
  1321.2 524.6 %all-reduce.4.cloned.1.call-start = ((), (), s32[]{:S(2)}) async-start(), calls=%async_computation.20 | async-start | bytes 2359296
  1489.7 384.7 %reduce-scatter.24.cloned.1.call-start = ((), (), s32[]{:S(2)}) async-start(), calls=%async_computation.16 | async-start | bytes 1474560 | tf_op jit(solution)/shard_map/reduce_scatter | solution.py:210
  1651.1 270.2 %reduce-scatter.28.cloned.1.call-start = ((), (), s32[]{:S(2)}) async-start(), calls=%async_computation.18 | async-start | bytes 1474560
  1662.2 128.2 %copy-start.85 = (f32[768]{0:T(1024)S(1)}, f32[768]{0:T(1024)}, u32[]{:S(2)}) copy-start(f32[768]{0:T(1024)} %get-tuple-element.38) | copy-start | bytes 9220
  1662.2 128.2 %copy-start.84 = (f32[768]{0:T(1024)S(1)}, f32[768]{0:T(1024)}, u32[]{:S(2)}) copy-start(f32[768]{0:T(1024)} %get-tuple-element.45) | copy-start | bytes 9220
  1662.2 214.0 %copy-start.88 = (f32[768]{0:T(1024)S(1)}, f32[768]{0:T(1024)}, u32[]{:S(2)}) copy-start(f32[768]{0:T(1024)} %get-tuple-element.36) | copy-start | bytes 9220
  1662.2 214.1 %copy-start.17 = (f32[1024,768]{1,0:T(8,128)S(1)}, f32[1024,768]{1,0:T(8,128)}, u32[]{:S(2)}) copy-start(f32[1024,768]{1,0:T(8,128)} %copy-done.15) | copy-start | bytes 9437188
  (93 other events, 1349.8 us)
Sparse Core Ops, SparseCore 0:
  27.4 84.7 all-gather.2
  285.5 82.1 all-gather.4
  772.1 99.0 reduce-scatter.13
  1147.4 99.1 reduce-scatter.15
  1249.9 69.0 reduce-scatter.19
  1322.4 162.5 reduce-scatter.25
  1488.5 162.5 reduce-scatter.21
  1654.8 128.1 reduce-scatter.17
  1786.2 19.8 reduce-scatter.29
  1808.5 37.2 all-reduce.3
  1848.5 25.8 reduce-scatter.23
  1876.8 25.7 reduce-scatter.27
where the time goes:
time: 1930 us
  waiting for transfers between devices  787 us (41%)
  matrix products  694 us (36%)
  other arithmetic  227 us (12%)
  local copies, waits for them, and re-layouts  156 us (8%)
  blocking collectives  49.2 us (3%)
    reduce_scatter x1, waiting for transfers between devices, shards(): lax.psum_scatter(down_sum.astype(jnp.bfloat16), 'dp', scatter_dimension=1...  164 us
    reduce_scatter x1, waiting for transfers between devices, shards(): lax.psum_scatter(up_sum.astype(jnp.bfloat16), 'dp', scatter_dimension=1,...  161 us
    convert_element_type x2, other arithmetic, shards(): d_scores = (probs * (d_probs - row_terms)).astype(jnp.bfloat16)  156 us
    all_gather x2, waiting for transfers between devices, share_keys(): return (lax.all_gather(pairs, 'blk', axis=1, tiled=True), fixed_valid)  151 us
    dot_general x2, matrix products, shards(): jnp.einsum('cqhd,ckhd->chqk', d_att, values_all, preferred_element_type=j...  130 us
    reduce_scatter x1, waiting for transfers between devices, shards(): lax.psum_scatter(qkv_sum.astype(jnp.bfloat16), 'dp', scatter_dimension=1,...  121 us
    dot_general x8, matrix products, matmul(): return jnp.dot(left, right, preferred_element_type=jnp.float32)  105 us
    dot_general x2, matrix products, attend(): jnp.einsum('chqk,ckhd->cqhd', probs_low, values_all, preferred_element_ty...  80.6 us
  transfers between devices with their start and end apart: 12, of which 10 were waited for; matrix products, arithmetic and copies ran while one was open for 10% of the time, Pallas kernels for 0%

commit v1 on v0

v1 whole, which is shorter than its diff:
```python
import functools
import math

import jax
import jax.numpy as jnp
from jax import lax
from jax.experimental import pallas as pl
from jax.experimental.pallas import tpu as pltpu
from jax.sharding import PartitionSpec as P

HEADS = 12
HEAD_DIM = 64
LAYERS = 2
PAIR = 2 * HEAD_DIM
EPS = 1e-05
LOG2E = 1.4426950408889634
LN2 = 0.6931471805599453
SCALE = 1.0 / math.sqrt(HEAD_DIM)
MASKED = -1e30
MIB = 1024 * 1024

F32 = jnp.float32
BF16 = jnp.bfloat16


def mm(left, right):
    return jnp.dot(left, right, preferred_element_type=F32)


def mm_nt(left, right):
    return lax.dot_general(left, right, (((1,), (1,)), ((), ())), preferred_element_type=F32)


def mm_tn(left, right):
    return lax.dot_general(left, right, (((0,), (0,)), ((), ())), preferred_element_type=F32)


def pieced(product, left, right, axis):
    wide = right.shape[axis]
    pieces = [
        product(
            left[...],
            right[:, at : min(at + 256, wide)]
            if axis == 1
            else right[at : min(at + 256, wide), :],
        )
        for at in range(0, wide, 256)
    ]
    return pieces[0] if len(pieces) == 1 else jnp.concatenate(pieces, axis=1)


def normalise(value):
    mean = jnp.mean(value, axis=-1, keepdims=True)
    centred = value - mean
    variance = jnp.mean(centred * centred, axis=-1, keepdims=True)
    r = lax.rsqrt(variance + EPS)
    return centred * r, r


def norm_backward(n, r, e, gain):
    eg = e * gain
    first = jnp.mean(eg, axis=-1, keepdims=True)
    second = jnp.mean(eg * n, axis=-1, keepdims=True)
    return r * (eg - first - n * second)


def params(mib=64):
    return pltpu.CompilerParams(vmem_limit_bytes=mib * MIB)


def whole(shape):
    return pl.BlockSpec(shape, lambda i: (0,) * len(shape), pipeline_mode=pl.Buffered(1))


def rows_of(tile, width):
    return pl.BlockSpec((tile, width), lambda i: (i, 0))


def slabs_of(count, tile, width):
    return pl.BlockSpec((count, tile, width), lambda i: (0, i, 0))


def columns_of(width, tile):
    return pl.BlockSpec((width, tile), lambda i: (0, i))


def layer_of(stacked, layer):
    rest = stacked.shape[1:]
    return pl.BlockSpec(
        (None,) + rest, lambda i: (layer,) + (0,) * len(rest), pipeline_mode=pl.Buffered(1)
    )


def ordered(after):
    return [pl.BlockSpec(memory_space=pl.ANY)] * len(after)


def without(kernel, first, count):
    def run(*refs):
        return kernel(*refs[:first], *refs[first + count :])

    return run


def turned(value):
    return value.T.astype(BF16)


class Tokens:
    def __init__(self, arrays, shift=None):
        self.arrays = arrays
        self.shift = shift
        self.rows = sum(array.shape[0] for array in arrays)
        self.width = arrays[0].shape[1]

    def operands(self):
        return list(self.arrays) + ([] if self.shift is None else [self.shift])

    def specs(self, tile):
        tiles = self.arrays[0].shape[0] // tile
        if len(self.arrays) == 1:
            specs = [rows_of(tile, self.width)]
        else:
            specs = [
                pl.BlockSpec((tile, self.width), lambda i: (jnp.minimum(i, tiles - 1), 0)),
                pl.BlockSpec((tile, self.width), lambda i: (jnp.maximum(i - tiles, 0), 0)),
            ]
        return specs + ([] if self.shift is None else [whole((1, self.width))])

    def count(self):
        return len(self.operands())

    def read(self, tile, refs):
        value = refs[0][...].astype(F32)
        if tile == self.rows and len(self.arrays) == 2:
            value = jnp.concatenate([value, refs[1][...].astype(F32)], axis=0)
        elif len(self.arrays) == 2:
            first = pl.program_id(0) < self.arrays[0].shape[0] // tile
            value = jnp.where(first, value, refs[1][...].astype(F32))
        return value if self.shift is None else value + refs[-1][...]


def qkv_kernel(x, tile, *refs):
    gain_ref, bias_ref, w_ref, h_ref, q_ref, kv_ref = refs[x.count() :]
    width = x.width
    n, _ = normalise(x.read(tile, refs[: x.count()]))
    h = n * gain_ref[0:1, :] + bias_ref[0:1, :]
    h_ref[...] = turned(h)
    h = h.astype(BF16)
    kv_ref[...] = mm(h, w_ref[:, width:]).astype(BF16)
    q_ref[...] = (mm(h, w_ref[:, :width]) * (SCALE * LOG2E)).astype(BF16)


def qkv_forward(layer, x, gain, bias, w, after):
    rows, width = x.rows, x.width
    tile = min(256, rows // 2)
    return pl.pallas_call(
        without(functools.partial(qkv_kernel, x, tile), x.count() + 3, len(after)),
        grid=(rows // tile,),
        in_specs=x.specs(tile)
        + [layer_of(value, layer) for value in (gain, bias, w)]
        + ordered(after),
        out_specs=[columns_of(width, tile), rows_of(tile, width), rows_of(tile, 2 * width)],
        out_shape=[
            jax.ShapeDtypeStruct((width, rows), BF16),
            jax.ShapeDtypeStruct((rows, width), BF16),
            jax.ShapeDtypeStruct((rows, 2 * width), BF16),
        ],
        compiler_params=params(),
        cost_estimate=pl.CostEstimate(
            flops=6 * rows * width * width, bytes_accessed=12 * rows * width, transcendentals=0
        ),
        name="norm_qkv",
    )(*x.operands(), gain, bias, w, *after)


def lanes_like(shape):
    lane = lax.broadcasted_iota(jnp.int32, shape, 1)
    return lane < HEAD_DIM, lane & (HEAD_DIM - 1)


def three_parts(value, sub, fourth):
    high = value.astype(BF16).astype(F32)
    rest = value - high
    middle = rest.astype(BF16).astype(F32)
    least = rest - middle
    return jnp.where(
        sub == 0,
        high,
        jnp.where(sub == 1, middle, jnp.where(sub == 2, least, jnp.where(sub == 3, fourth, 0.0))),
    )


def attend_kernel(parts, *refs):
    q_ref = refs[0]
    k_refs = refs[1 : 1 + parts]
    v_refs = refs[1 + parts : 1 + 2 * parts]
    dead_refs = refs[1 + 2 * parts : 1 + 3 * parts]
    o_ref, inverse_ref, p_ref, ka, kb, va, vb = refs[1 + 3 * parts :]
    rows = k_refs[0].shape[0]

    @pl.when(pl.program_id(1) == 0)
    def _():
        low, sub = lanes_like((rows, PAIR))
        for part in range(parts):
            own = slice(part * rows, (part + 1) * rows)
            k = k_refs[part][...].astype(F32)
            v = v_refs[part][...].astype(F32)
            extra = jnp.where(sub == 3, dead_refs[part][...].astype(F32), 0.0)
            ka[own, :] = jnp.where(low, k, extra).astype(BF16)
            kb[own, :] = jnp.where(low, extra, k).astype(BF16)
            va[own, :] = jnp.where(low, v, 1.0).astype(BF16)
            vb[own, :] = jnp.where(low, 1.0, v).astype(BF16)

    low, sub = lanes_like(q_ref.shape)
    fourth = jnp.where(sub == 3, 1.0, 0.0)
    q = q_ref[...].astype(F32)
    sa = mm_nt(jnp.where(low, q, fourth).astype(BF16), ka[...])
    sb = mm_nt(jnp.where(low, fourth, q).astype(BF16), kb[...])
    pa = jnp.exp2(sa - jnp.max(sa, axis=-1, keepdims=True)).astype(BF16)
    p_ref[0] = pa
    oa = mm(pa, va[...])
    pb = jnp.exp2(sb - jnp.max(sb, axis=-1, keepdims=True)).astype(BF16)
    p_ref[1] = pb
    ob = mm(pb, vb[...])
    inverse = 1.0 / pltpu.roll(jnp.where(low, ob, oa), HEAD_DIM, 1)
    inverse_ref[...] = inverse
    o_ref[...] = (jnp.where(low, oa, ob) * inverse).astype(BF16)


def attend(q, kv_parts, dead_parts):
    rows, width = q.shape
    parts = len(kv_parts)
    pairs = width // PAIR
    tile = min(512, rows)
    keys = parts * rows
    some = pl.BlockSpec((tile, PAIR), lambda j, i: (i, j))
    first = pl.BlockSpec((rows, PAIR), lambda j, i: (0, j))
    second = pl.BlockSpec((rows, PAIR), lambda j, i: (0, pairs + j))
    fixed = pl.BlockSpec((rows, PAIR), lambda j, i: (0, 0))
    scratch = pltpu.VMEM((keys, PAIR), BF16)
    return pl.pallas_call(
        functools.partial(attend_kernel, parts),
        grid=(pairs, rows // tile),
        in_specs=[some] + [first] * parts + [second] * parts + [fixed] * parts,
        out_specs=[some, some, pl.BlockSpec((2, tile, keys), lambda j, i: (j, i, 0))],
        out_shape=[
            jax.ShapeDtypeStruct((rows, width), BF16),
            jax.ShapeDtypeStruct((rows, width), F32),
            jax.ShapeDtypeStruct((2 * pairs, rows, keys), BF16),
        ],
        scratch_shapes=[scratch] * 4,
        compiler_params=params(),
        cost_estimate=pl.CostEstimate(
            flops=16 * rows * keys * width,
            bytes_accessed=4 * pairs * rows * keys,
            transcendentals=HEADS * rows * keys,
        ),
        name="attend",
    )(q, *kv_parts, *kv_parts, *dead_parts)


def attend_back_kernel(parts, *refs):
    q_ref, inverse_ref, att_ref, datt_ref, p_ref = refs[:5]
    k_refs = refs[5 : 5 + parts]
    v_refs = refs[5 + parts : 5 + 2 * parts]
    rest = refs[5 + 2 * parts :]
    dq_ref = rest[0]
    dkv_refs = rest[1 : 1 + parts]
    ks, va, vb, dk_turned, dv_turned = rest[1 + parts :]
    rows = k_refs[0].shape[0]
    index = pl.program_id(1)

    @pl.when(index == 0)
    def _():
        low, sub = lanes_like((rows, PAIR))
        ones = jnp.where(sub < 3, 1.0, 0.0)
        for part in range(parts):
            own = slice(part * rows, (part + 1) * rows)
            ks[own, :] = k_refs[part][...]
            v = v_refs[part][...].astype(F32)
            va[own, :] = jnp.where(low, v, ones).astype(BF16)
            vb[own, :] = jnp.where(low, ones, v).astype(BF16)
        dk_turned[...] = jnp.zeros_like(dk_turned)
        dv_turned[...] = jnp.zeros_like(dv_turned)

    low, sub = lanes_like(q_ref.shape)
    q_turned = turned(q_ref[...].astype(F32))
    datt = datt_ref[...].astype(F32) * inverse_ref[...]
    datt_turned = turned(datt)
    product = datt * att_ref[...].astype(F32)
    term_a = jnp.sum(jnp.where(low, product, 0.0), axis=-1, keepdims=True)
    term_b = jnp.sum(jnp.where(low, 0.0, product), axis=-1, keepdims=True)
    extra = three_parts(-jnp.where(low, term_b, term_a), sub, 0.0)
    ta = mm_nt(jnp.where(low, datt, extra).astype(BF16), va[...])
    tb = mm_nt(jnp.where(low, extra, datt).astype(BF16), vb[...])
    first, second = slice(0, HEAD_DIM), slice(HEAD_DIM, PAIR)
    pa, pb = p_ref[0], p_ref[1]
    dv_turned[first, :] += mm(datt_turned[first, :], pa)
    ga = (pa.astype(F32) * ta).astype(BF16)
    dqa = mm(ga, ks[...])
    dk_turned[first, :] += mm(q_turned[first, :], ga)
    dv_turned[second, :] += mm(datt_turned[second, :], pb)
    gb = (pb.astype(F32) * tb).astype(BF16)
    dqb = mm(gb, ks[...])
    dk_turned[second, :] += mm(q_turned[second, :], gb)
    dq_ref[...] = (jnp.where(low, dqa, dqb) * SCALE).astype(BF16)

    @pl.when(index == pl.num_programs(1) - 1)
    def _():
        for part in range(parts):
            own = slice(part * rows, (part + 1) * rows)
            dkv_refs[part][0] = (dk_turned[:, own].T * LN2).astype(BF16)
            dkv_refs[part][1] = dv_turned[:, own].T.astype(BF16)


def attend_back(group, groups, q, inverse, att, datt, p, kv_parts, after):
    rows, width = q.shape
    parts = len(kv_parts)
    pairs = width // PAIR
    count = pairs // groups
    base = group * count
    tile = min(512, rows)
    keys = parts * rows
    some = pl.BlockSpec((tile, PAIR), lambda j, i: (i, base + j))
    first = pl.BlockSpec((rows, PAIR), lambda j, i: (0, base + j))
    second = pl.BlockSpec((rows, PAIR), lambda j, i: (0, pairs + base + j))
    both = pl.BlockSpec((2, rows, PAIR), lambda j, i: (0, 0, j))
    all_keys = pltpu.VMEM((keys, PAIR), BF16)
    turned_keys = pltpu.VMEM((PAIR, keys), F32)
    out = pl.pallas_call(
        without(functools.partial(attend_back_kernel, parts), 5 + 2 * parts, len(after)),
        grid=(count, rows // tile),
        in_specs=[some] * 4
        + [pl.BlockSpec((2, tile, keys), lambda j, i: (base + j, i, 0))]
        + [first] * parts
        + [second] * parts
        + ordered(after),
        out_specs=[pl.BlockSpec((tile, PAIR), lambda j, i: (i, j))] + [both] * parts,
        out_shape=[jax.ShapeDtypeStruct((rows, count * PAIR), BF16)]
        + [jax.ShapeDtypeStruct((2, rows, count * PAIR), BF16)] * parts,
        scratch_shapes=[all_keys] * 3 + [turned_keys] * 2,
        compiler_params=params(),
        cost_estimate=pl.CostEstimate(
            flops=32 * rows * keys * width // groups,
            bytes_accessed=4 * count * rows * keys,
            transcendentals=0,
        ),
        name="attend_back",
    )(q, inverse, att, datt, p, *kv_parts, *kv_parts, *after)
    return out[0], out[1:]


def gelu_parts(u):
    base = 1.0 + (0.3275911 * math.sqrt(0.5)) * jnp.abs(u)
    t = pl.reciprocal(base, approx=True)
    t = t * (2.0 - base * t)
    bell = jnp.exp2(u * u * (-0.5 * LOG2E))
    series = t * (
        0.5 * 0.254829592
        + t
        * (
            0.5 * -0.284496736
            + t * (0.5 * 1.421413741 + t * (0.5 * -1.453152027 + t * (0.5 * 1.061405429)))
        )
    )
    tail = series * bell
    share = jnp.where(u < 0.0, tail, 1.0 - tail)
    return u * share, share + u * bell * (1.0 / math.sqrt(2.0 * math.pi))


def pieces_of(rows, most):
    piece = min(most, rows)
    return [slice(at, at + piece) for at in range(0, rows, piece)]


def feed_kernel(x, tile, *refs):
    att_ref, wout_ref, gain_ref, bias_ref, wup_ref, wdown_ref = refs[x.count() : x.count() + 6]
    mid_ref, h_ref, att_turned_ref, act_ref, slope_ref, next_ref, h_kept = refs[x.count() + 6 :]

    @pl.when(pl.program_id(1) == 0)
    def _():
        middle = x.read(tile, refs[: x.count()]) + mm(att_ref[...], wout_ref[...])
        mid_ref[...] = middle
        next_ref[...] = middle
        att_turned_ref[...] = turned(att_ref[...].astype(F32))
        n, _ = normalise(middle)
        h = n * gain_ref[1:2, :] + bias_ref[1:2, :]
        h_ref[...] = turned(h)
        h_kept[...] = h.astype(BF16)

    pieces = pieces_of(tile, 512)
    ups = [mm(h_kept[pieces[0], :], wup_ref[...])]
    for i, piece in enumerate(pieces):
        if i + 1 < len(pieces):
            ups.append(mm(h_kept[pieces[i + 1], :], wup_ref[...]))
        active, slope = gelu_parts(ups[i])
        active = active.astype(BF16)
        act_ref[piece, :] = active
        slope_ref[piece, :] = slope.astype(BF16)
        next_ref[piece, :] += mm(active, wdown_ref[...])


def across(spec):
    return pl.BlockSpec(
        spec.block_shape, lambda i, c: spec.index_map(i), pipeline_mode=spec.pipeline_mode
    )


def feed_weights(layer, width, chunk):
    up = pl.BlockSpec((None, width, chunk), lambda i, c: (layer, 0, c))
    down = pl.BlockSpec((None, chunk, width), lambda i, c: (layer, c, 0))
    return up, down


def feed_forward(layer, att, x, wout, gain, bias, wup, wdown):
    rows, width = x.rows, x.width
    hidden = wup.shape[2]
    tile = min(512, rows // 2)
    chunk = 512
    wide = pl.BlockSpec((tile, chunk), lambda i, c: (i, c))
    return pl.pallas_call(
        functools.partial(feed_kernel, x, tile),
        grid=(rows // tile, hidden // chunk),
        in_specs=[
            across(spec)
            for spec in x.specs(tile)
            + [rows_of(tile, width)]
            + [layer_of(value, layer) for value in (wout, gain, bias)]
        ]
        + list(feed_weights(layer, width, chunk)),
        out_specs=[
            across(rows_of(tile, width)),
            across(columns_of(width, tile)),
            across(columns_of(width, tile)),
            wide,
            wide,
            across(rows_of(tile, width)),
        ],
        out_shape=[
            jax.ShapeDtypeStruct((rows, width), F32),
            jax.ShapeDtypeStruct((width, rows), BF16),
            jax.ShapeDtypeStruct((width, rows), BF16),
            jax.ShapeDtypeStruct((rows, hidden), BF16),
            jax.ShapeDtypeStruct((rows, hidden), BF16),
            jax.ShapeDtypeStruct((rows, width), F32),
        ],
        scratch_shapes=[pltpu.VMEM((tile, width), BF16)],
        compiler_params=params(),
        cost_estimate=pl.CostEstimate(
            flops=2 * rows * width * (width + 2 * hidden),
            bytes_accessed=16 * rows * width + 4 * rows * hidden + 4 * width * hidden,
            transcendentals=2 * rows * hidden,
        ),
        name="feed",
    )(*x.operands(), att, wout, gain, bias, wup, wdown)


def add_norm_sums(first_row, sum_ref, e, n):
    bias_row = first_row + 2 * LAYERS
    sum_ref[first_row : first_row + 1, :] += jnp.sum(e * n, axis=0, keepdims=True)
    sum_ref[bias_row : bias_row + 1, :] += jnp.sum(e, axis=0, keepdims=True)


def feed_back_kernel(layer, grad, dp_size, core_ref, *refs):
    count = grad.count()
    (
        slope_ref,
        act_ref,
        mid_ref,
        h_ref,
        att_ref,
        gain_ref,
        wup_ref,
        wdown_ref,
        wout_ref,
        start_ref,
        up_gone,
        up_kept,
        down_gone,
        down_kept,
        dmid_ref,
        datt_ref,
        sum_ref,
        gy_ref,
        gy_turned_ref,
        total_ref,
    ) = refs[count:]
    core = core_ref[0]
    step = pl.program_id(0)
    rows, width = gy_ref.shape
    chunk = slope_ref.shape[1]
    half = up_gone.shape[1]
    slabs = 2 * half
    deep = width // dp_size
    thin = width // slabs
    wide = up_gone.shape[3] - thin

    @pl.when(step == 0)
    def _():
        value = grad.read(rows, refs[:count])
        gy_ref[...] = value.astype(BF16)
        gy_turned = turned(value)
        for s in range(slabs):
            at = s // 2 * thin
            gy_turned_ref[s % 2, at : at + thin, :] = gy_turned[s * thin : (s + 1) * thin, :]
        total_ref[...] = jnp.zeros_like(total_ref)

    pieces = pieces_of(rows, 512)
    dups = []
    for piece in pieces:
        inner = mm_nt(gy_ref[piece, :], wdown_ref[...])
        dups.append((inner * slope_ref[piece, :].astype(F32)).astype(BF16))
    dup = dups[0] if len(dups) == 1 else jnp.concatenate(dups, axis=0)
    for piece, one in zip(pieces, dups):
        total_ref[piece, :] += mm_nt(one, wup_ref[...])
    for k in range(chunk // wide):
        slab = step * (chunk // wide) + k
        product = mm(h_ref[...], dup[:, k * wide : (k + 1) * wide]).astype(BF16)
        for goes, out_ref in ((slab % 2 != core, up_gone), (slab % 2 == core, up_kept)):

            @pl.when(goes)
            def _(product=product, out_ref=out_ref, slab=slab):
                for d in range(dp_size):
                    out_ref[d, slab // 2, :, :wide] = product[d * deep : (d + 1) * deep, :]

    active = act_ref[...]
    pair, _, _, across_wide = down_gone.shape
    for which, out_ref in ((1 - core, down_gone), (core, down_kept)):
        product = mm(gy_turned_ref[which], active).astype(BF16)
        for x in range(half):
            for d in range(pair):
                out_ref[d, x] = product[
                    x * thin : (x + 1) * thin, d * across_wide : (d + 1) * across_wide
                ]

    @pl.when(step == pl.num_programs(0) - 1)
    def _():
        total = total_ref[...]
        n, r = normalise(mid_ref[...])
        dmid = grad.read(rows, refs[:count]) + norm_backward(n, r, total, gain_ref[1:2, :])
        dmid_ref[...] = dmid
        gz = dmid.astype(BF16)
        datt_ref[...] = mm_nt(gz, wout_ref[...]).astype(BF16)
        sum_ref[...] = start_ref[...]
        add_norm_sums(2 * layer + 1, sum_ref, total, n)
        product = mm(att_ref[...], gz).astype(BF16)
        for own in range(2):

            @pl.when(core == own)
            def _(own=own):
                for s in range(slabs):
                    out_ref = up_kept if s % 2 == own else up_gone
                    for d in range(dp_size):
                        out_ref[d, s // 2, :, wide:] = product[
                            d * deep : (d + 1) * deep, s * thin : (s + 1) * thin
                        ]


def feed_backward(
    layer,
    grad,
    slope,
    active,
    mid,
    h,
    att_turned,
    gain,
    wdown,
    wup,
    wout,
    start,
    core,
    slabs,
    dp_size,
    after,
):
    rows, width = grad.rows, grad.width
    hidden = wup.shape[2]
    half = slabs // 2
    wide, thin = hidden // slabs, width // slabs
    chunk = max(wide, 768)
    down_wide = hidden // dp_size
    pair = chunk // down_wide

    def fixed(shape):
        return pl.BlockSpec(
            shape, lambda c, core: (0,) * len(shape), pipeline_mode=pl.Buffered(1)
        )

    def of_layer(stacked):
        rest = stacked.shape[1:]
        return pl.BlockSpec(
            (None,) + rest,
            lambda c, core: (layer,) + (0,) * len(rest),
            pipeline_mode=pl.Buffered(1),
        )

    by_chunk = pl.BlockSpec((rows, chunk), lambda c, core: (0, c))
    up_shape = (dp_size, half, width // dp_size, wide + thin)
    down_shape = (dp_size, half, thin, down_wide)
    down_spec = pl.BlockSpec((pair, half, thin, down_wide), lambda c, core: (c, 0, 0, 0))
    return pl.pallas_call(
        without(
            functools.partial(feed_back_kernel, layer, grad, dp_size),
            1 + grad.count() + 10,
            len(after),
        ),
        grid_spec=pltpu.PrefetchScalarGridSpec(
            num_scalar_prefetch=1,
            grid=(hidden // chunk,),
            in_specs=[fixed(operand.shape) for operand in grad.operands()]
            + [by_chunk, by_chunk]
            + [fixed(one.shape) for one in (mid, h, att_turned)]
            + [
                of_layer(gain),
                pl.BlockSpec((None, width, chunk), lambda c, core: (layer, 0, c)),
                pl.BlockSpec((None, chunk, width), lambda c, core: (layer, c, 0)),
                of_layer(wout),
                fixed(start.shape),
            ]
            + ordered(after),
            out_specs=[fixed(up_shape)] * 2
            + [down_spec] * 2
            + [fixed((rows, width))] * 2
            + [fixed(start.shape)],
            scratch_shapes=[
                pltpu.VMEM((rows, width), BF16),
                pltpu.VMEM((2, width // 2, rows), BF16),
                pltpu.VMEM((rows, width), F32),
            ],
        ),
        out_shape=[jax.ShapeDtypeStruct(up_shape, BF16)] * 2
        + [jax.ShapeDtypeStruct(down_shape, BF16)] * 2
        + [
            jax.ShapeDtypeStruct((rows, width), F32),
            jax.ShapeDtypeStruct((rows, width), BF16),
            jax.ShapeDtypeStruct(start.shape, F32),
        ],
        compiler_params=params(),
        cost_estimate=pl.CostEstimate(
            flops=4 * rows * width * (width + 2 * hidden),
            bytes_accessed=20 * rows * width + 4 * rows * hidden + 8 * width * hidden,
            transcendentals=0,
        ),
        name="feed_back",
    )(
        core,
        *grad.operands(),
        slope,
        active,
        mid,
        h,
        att_turned,
        gain,
        wup,
        wdown,
        wout,
        start,
        *after,
    )


def summed(refs):
    total = refs[0][...].astype(F32)
    for ref in refs[1:]:
        total += ref[...].astype(F32)
    return total.astype(BF16)


def joined(groups, parts, refs):
    dkv = [summed(refs[groups + g * parts : groups + (g + 1) * parts]) for g in range(groups)]
    pieces = [ref[...] for ref in refs[:groups]]
    pieces += [block[0] for block in dkv]
    pieces += [block[1] for block in dkv]
    return jnp.concatenate(pieces, axis=1)


def joined_specs(groups, parts, tile, width, offset=0):
    one = pl.BlockSpec((tile, width // groups), lambda i: (i + offset, 0))
    pair = pl.BlockSpec((2, tile, width // groups), lambda i: (0, i + offset, 0))
    return [one] * groups + [pair] * (groups * parts)


def qkv_grad_kernel(layer, groups, parts, x, tile, ends, core_ref, *refs):
    before = groups * (1 + parts)
    x_refs = refs[before : before + x.count()]
    gain_ref, w_ref, h_ref, dmid_ref, start_ref, species_ref = refs[before + x.count() :][:6]
    gone_ref, kept_ref, grad_ref, sum_ref, full_ref = refs[before + x.count() + 6 :]
    dp_size, half, deep, wide = gone_ref.shape
    step, steps = pl.program_id(0), pl.num_programs(0)
    full = joined(groups, parts, refs)
    full_ref[pl.ds(pl.multiple_of(step * tile, tile), tile), :] = full

    @pl.when(step == 0)
    def _():
        sum_ref[...] = start_ref[...]

    @pl.when(step < ends)
    def _():
        e = mm_nt(full, w_ref[...])
        n, r = normalise(x.read(tile, x_refs))
        grad = dmid_ref[...] + norm_backward(n, r, e, gain_ref[0:1, :])
        grad_ref[...] = grad.astype(grad_ref.dtype)
        add_norm_sums(2 * layer, sum_ref, e, n)
        if layer == 0:
            row = pl.ds(4 * LAYERS + species_ref[0], 1)
            sum_ref[row, :] += jnp.sum(grad, axis=0, keepdims=True)

    @pl.when(step == steps - 1)
    def _():
        first = h_ref.shape[1] // 2
        h = jnp.concatenate([h_ref[:, first:], h_ref[:, :first]], axis=1)
        for s in range(2 * half):
            product = mm(h, full_ref[:, s * wide : (s + 1) * wide]).astype(BF16)
            for own in range(2):

                @pl.when(core_ref[0] == own)
                def _(own=own, s=s, product=product):
                    out_ref = kept_ref if s % 2 == own else gone_ref
                    for d in range(dp_size):
                        out_ref[d, s // 2] = product[d * deep : (d + 1) * deep, :]


def qkv_gradients(
    layer, ends, kind, dq, dkv, x, gain, w, h, dmid, start, species, core, slabs, dp_size, after
):
    groups, parts = len(dq), len(dkv[0])
    rows, width = dmid.shape
    tile = min(256, rows // 2)
    tiles = rows // tile
    turn_to = tiles // 2
    half = slabs // 2
    shape = (dp_size, half, width // dp_size, 3 * width // slabs)

    def fixed(shape):
        return pl.BlockSpec(
            shape, lambda i, core: (0,) * len(shape), pipeline_mode=pl.Buffered(1)
        )

    def of_layer(stacked):
        rest = stacked.shape[1:]
        return pl.BlockSpec(
            (None,) + rest,
            lambda i, core: (layer,) + (0,) * len(rest),
            pipeline_mode=pl.Buffered(1),
        )

    def at(i):
        return lax.rem(i + turn_to, tiles)

    def used(i):
        return at(jnp.minimum(i, ends - 1))

    def out_at(i):
        return used(i) if ends == tiles else jnp.minimum(i, ends - 1)

    one = pl.BlockSpec((tile, width // groups), lambda i, core: (at(i), 0))
    both = pl.BlockSpec((2, tile, width // groups), lambda i, core: (0, at(i), 0))
    if ends == tiles:
        x_specs = [pl.BlockSpec((tile, width), lambda i, core: (used(i), 0))]
    else:
        x_specs = [pl.BlockSpec((tile, width), lambda i, core: (out_at(i), 0))]
    if x.shift is not None:
        x_specs.append(fixed((1, width)))
    return pl.pallas_call(
        without(
            functools.partial(qkv_grad_kernel, layer, groups, parts, x, tile, ends),
            1 + groups * (1 + parts) + x.count() + 6,
            len(after),
        ),
        grid_spec=pltpu.PrefetchScalarGridSpec(
            num_scalar_prefetch=1,
            grid=(tiles,),
            in_specs=[one] * groups
            + [both] * (groups * parts)
            + x_specs
            + [of_layer(gain), of_layer(w), fixed(h.shape)]
            + [pl.BlockSpec((tile, width), lambda i, core: (used(i), 0)), fixed(start.shape)]
            + [pl.BlockSpec(memory_space=pltpu.SMEM)]
            + ordered(after),
            out_specs=[fixed(shape)] * 2
            + [pl.BlockSpec((tile, width), lambda i, core: (out_at(i), 0)), fixed(start.shape)],
            scratch_shapes=[pltpu.VMEM((rows, 3 * width), BF16)],
        ),
        out_shape=[jax.ShapeDtypeStruct(shape, BF16)] * 2
        + [
            jax.ShapeDtypeStruct((ends * tile, width), kind),
            jax.ShapeDtypeStruct(start.shape, F32),
        ],
        compiler_params=params(),
        cost_estimate=pl.CostEstimate(
            flops=12 * rows * width * width, bytes_accessed=32 * rows * width, transcendentals=0
        ),
        name="qkv_grad",
    )(
        core,
        *dq,
        *[block for group in dkv for block in group],
        *x.operands(),
        gain,
        w,
        h,
        dmid,
        start,
        species,
        *after,
    )


def qkv_back_kernel(layer, groups, parts, x, tile, *refs):
    before = groups * (1 + parts)
    gain_ref, w_ref, dmid_ref, start_ref, species_ref = refs[before + x.count() :][:5]
    grad_ref, sum_ref = refs[before + x.count() + 5 :]
    full = joined(groups, parts, refs)
    e = mm_nt(full, w_ref[...])
    n, r = normalise(x.read(tile, refs[before : before + x.count()]))
    grad = dmid_ref[...] + norm_backward(n, r, e, gain_ref[0:1, :])
    grad_ref[...] = grad.astype(grad_ref.dtype)

    @pl.when(pl.program_id(0) == 0)
    def _():
        sum_ref[...] = start_ref[...]

    add_norm_sums(2 * layer, sum_ref, e, n)
    if layer == 0:
        row = pl.ds(4 * LAYERS + species_ref[0], 1)
        sum_ref[row, :] += jnp.sum(grad, axis=0, keepdims=True)


def qkv_backward(layer, first_row, kind, dq, dkv, x, gain, w, dmid, start, species, after):
    groups, parts = len(dq), len(dkv[0])
    rows, width = x.rows, x.width
    tile = min(256, dmid.shape[0] // 2)
    offset = first_row // tile
    sums = pl.BlockSpec(start.shape, lambda i: (0, 0))
    return pl.pallas_call(
        without(
            functools.partial(qkv_back_kernel, layer, groups, parts, x, tile),
            groups * (1 + parts) + x.count() + 5,
            len(after),
        ),
        grid=(rows // tile,),
        in_specs=joined_specs(groups, parts, tile, width, offset)
        + x.specs(tile)
        + [layer_of(gain, layer), layer_of(w, layer)]
        + [pl.BlockSpec((tile, width), lambda i: (i + offset, 0)), sums]
        + [pl.BlockSpec(memory_space=pltpu.SMEM)]
        + ordered(after),
        out_specs=[rows_of(tile, width), sums],
        out_shape=[
            jax.ShapeDtypeStruct((rows, width), kind),
            jax.ShapeDtypeStruct(start.shape, F32),
        ],
        compiler_params=params(),
        cost_estimate=pl.CostEstimate(
            flops=6 * rows * width * width, bytes_accessed=24 * rows * width, transcendentals=0
        ),
        name="qkv_back",
    )(
        *dq,
        *[block for group in dkv for block in group],
        *x.operands(),
        gain,
        w,
        dmid,
        start,
        species,
        *after,
    )


def token_of(ref):
    ref[...] = jnp.zeros_like(ref)


TOKEN = jax.ShapeDtypeStruct((8, 128), F32)


def place_kernel(mine_ref, own_ref, came_ref, out_ref, token_ref):
    token_of(token_ref)
    mine = pl.program_id(0) == mine_ref[0]
    out_ref[...] = jnp.where(mine, own_ref[...], came_ref[...].astype(F32))


def place_cells(mine, value, came):
    rows, width = came.shape
    tile = min(256, rows)
    spec = pl.BlockSpec((tile, width), lambda c, i, mine: (i, 0))
    return pl.pallas_call(
        place_kernel,
        grid_spec=pltpu.PrefetchScalarGridSpec(
            num_scalar_prefetch=1,
            grid=(2, rows // tile),
            in_specs=[spec, spec],
            out_specs=[
                pl.BlockSpec((None, tile, width), lambda c, i, mine: (c, i, 0)),
                pl.BlockSpec(TOKEN.shape, lambda c, i, mine: (0, 0)),
            ],
        ),
        out_shape=[jax.ShapeDtypeStruct((2, rows, width), F32), TOKEN],
        compiler_params=params(16),
        cost_estimate=pl.CostEstimate(
            flops=rows * width, bytes_accessed=20 * rows * width, transcendentals=0
        ),
        name="place_cells",
    )(mine, value, came)


class Sum:
    def __init__(self, came, kept, steps, sizes, places, layer, results, scatter, part=(0, 1)):
        self.part = part
        self.whole = True
        self.sizes = sizes
        self.places = places
        self.scatter = scatter
        self.left = {
            "blk": bits_of(sizes["blk"])[1:],
            "dp": bits_of(sizes["dp"]),
        }
        self.steps = [step for step in steps if not scatter or step[0] == "blk"]
        self.layer = layer
        self.results = results
        self.kept = kept
        self.came = came
        self.over_blk = False
        self.waiting = 0
        self.finished = False

    def ready(self):
        ends = not (self.scatter or self.over_blk or self.steps)
        return not ends or self.layer == LAYERS - 1 or bool(self.results.held)

    def spread(self, call, outer, inner, tail):
        by_outer, by_inner = math.gcd(call.count, outer), math.gcd(call.count, inner)
        if by_outer >= by_inner:
            by = by_outer
            return (outer // by, 1, inner) + tail, lambda j, side: (
                j // (call.count // by),
                side,
                0,
                0,
                0,
            )
        by = by_inner
        return (outer, 1, inner // by) + tail, lambda j, side: (
            0,
            side,
            j // (call.count // by),
            0,
            0,
        )

    def prepare_scatter(self, call):
        tail = self.kept.shape[-2:]
        shape = (math.prod(self.kept.shape[:-2]), 1, 1) + tail
        block, index = self.spread(call, shape[0], 1, tail)
        spec = pl.BlockSpec(block, lambda j, side: index(j, 0))
        reads = [call.read(one.reshape(shape), spec) for one in (self.kept, self.came)]
        write = call.write(shape, BF16, spec)

        def work(refs):
            refs[write][...] = refs[reads[0]][...] + refs[reads[1]][...]

        def finish(out):
            whole = out(write).reshape((self.sizes["dp"], -1) + tail)
            self.kept = lax.psum_scatter(whole, "dp", scatter_dimension=0, tiled=False)
            self.came = None
            self.left = {"blk": [], "dp": []}
            self.steps = []
            self.waiting = self.scatter
            self.scatter = 0
            self.over_blk = True

        return work, finish

    def prepare_over_blk(self, call):
        at = call.carry(self.kept)

        def finish(out):
            blk = self.sizes["blk"]
            cores = [list(range(core, blk, 2)) for core in range(2)]
            self.kept = lax.psum_scatter(
                out(at), "blk", scatter_dimension=0, axis_index_groups=cores, tiled=False
            )
            self.over_blk = False
            self.waiting = 2

        return (lambda refs: None), finish

    def prepare(self, call):
        if self.scatter:
            return self.prepare_scatter(call)
        if self.over_blk:
            return self.prepare_over_blk(call)
        if not self.steps:
            return self.prepare_last(call)
        axis, bit = self.steps[0]
        at = self.left[axis].index(bit)
        inner = 1 << at
        if axis == "dp":
            inner <<= len(self.left["blk"])
        total = 1 << (len(self.left["blk"]) + len(self.left["dp"]))
        outer = total // (2 * inner)
        tail = self.kept.shape[-2:]
        shape = (outer, 2, inner) + tail
        piece = 0
        if self.whole:
            piece = self.part[0]
            tail = (tail[0] // self.part[1], tail[1])
        block, index = self.spread(call, outer, inner, tail)
        side = (self.places[axis] // bit) % 2
        sources = [self.kept.reshape(shape)]
        if self.came is not None:
            sources.append(self.came.reshape(shape))
        reads = []
        for value in (1 - side, side):
            at = call.scalar(value)
            spec = pl.BlockSpec(
                block, lambda j, side, at=at: index(j, side[at])[:3] + (piece, 0)
            )
            reads.append([call.read(one, spec) for one in sources])
        spec = pl.BlockSpec(block, lambda j, side: index(j, 0))
        writes = [call.write((outer, 1, inner) + tail, BF16, spec) for _ in range(2)]

        def work(refs):
            for some, write in zip(reads, writes):
                values = [refs[i][...] for i in some]
                refs[write][...] = values[0] if len(values) == 1 else values[0] + values[1]

        def finish(out):
            self.steps.pop(0)
            self.left[axis].remove(bit)
            self.whole = False
            self.kept = out(writes[1])
            self.came = exchange(out(writes[0]), axis, self.sizes[axis], bit)

        return work, finish

    def prepare_last(self, call):
        rows, wide = self.kept.shape[-2:]
        spec = pl.BlockSpec((rows, wide), lambda j, side: (0, 0))
        sources = [one for one in (self.kept, self.came) if one is not None]
        reads = [call.read(one.reshape(rows, wide), spec) for one in sources]
        writes = []
        first, count = self.part
        for name, columns in self.results.names:
            block = (rows * count, columns)
            spec = pl.BlockSpec((None,) + block, lambda j, side: (self.layer, 0, 0))
            if name not in call.shared:
                held = self.results.held.get(name)
                call.shared[name] = call.write((LAYERS,) + block, F32, spec, held)
            writes.append(call.shared[name])

        def work(refs):
            total = refs[reads[0]][...].astype(F32)
            if len(reads) == 2:
                total += refs[reads[1]][...].astype(F32)
            at = 0
            for write, (_, columns) in zip(writes, self.results.names):
                refs[write][first * rows : (first + 1) * rows, :] = total[:, at : at + columns]
                at += columns

        def finish(out):
            self.finished = True
            for write, (name, _) in zip(writes, self.results.names):
                self.results.held[name] = out(write)

        return work, finish


class Results:
    def __init__(self, names):
        self.names = names
        self.held = {}


class SmallSum:
    def __init__(self, value, sizes):
        self.value = value
        self.sizes = sizes
        self.steps = []
        for axis in ("blk", "dp"):
            bits = bits_of(sizes[axis])
            apart = len(bits) - 2 if axis == "dp" and len(bits) > 2 else len(bits)
            self.steps += [(axis, (bit,)) for bit in bits[:apart]]
            if apart < len(bits):
                first, second = bits[apart:]
                self.steps.append((axis, (first, second, first + second)))
        self.came = None
        self.waiting = 0
        self.finished = False
        self.send()

    def ready(self):
        return True

    def send(self):
        axis, masks = self.steps.pop(0)
        self.came = [exchange(self.value, axis, self.sizes[axis], mask) for mask in masks]

    def prepare(self, call):
        shape = self.value.shape
        spec = pl.BlockSpec(shape, lambda j, side: (0, 0))
        reads = [call.read(one, spec) for one in [self.value] + self.came]
        if self.steps:
            writes = [call.write(shape, F32, spec)]
        else:
            norms = (LAYERS, 2, shape[1])
            spec = pl.BlockSpec(norms, lambda j, side: (0, 0, 0))
            writes = [call.write(norms, F32, spec) for _ in range(2)]
            spec = pl.BlockSpec((2, shape[1]), lambda j, side: (0, 0))
            writes.append(call.write((2, shape[1]), F32, spec))
        last = not self.steps

        def work(refs):
            values = [refs[i][...] for i in reads]
            while len(values) > 1:
                values = [a + b for a, b in zip(values[::2], values[1::2])]
            if not last:
                refs[writes[0]][...] = values[0]
                return
            for which in range(2):
                for row in range(2 * LAYERS):
                    at = which * 2 * LAYERS + row
                    refs[writes[which]][row // 2, row % 2 : row % 2 + 1, :] = values[0][
                        at : at + 1, :
                    ]
            refs[writes[2]][...] = values[0][4 * LAYERS : 4 * LAYERS + 2, :]

        def finish(out):
            if last:
                self.value = [out(write) for write in writes]
                self.finished = True
            else:
                self.value = out(writes[0])
                self.send()

        return work, finish


class Call:
    def __init__(self):
        self.count = 2
        self.scalars, self.operands, self.in_specs = [], [], []
        self.out_specs, self.shapes, self.held = [], [], []
        self.shared = {}

    def scalar(self, value):
        self.scalars.append(value)
        return len(self.scalars) - 1

    def read(self, operand, spec):
        self.operands.append(operand)
        self.in_specs.append(spec)
        return ("in", len(self.operands) - 1)

    def write(self, shape, kind, spec, held=None):
        self.shapes.append(jax.ShapeDtypeStruct(shape, kind))
        self.out_specs.append(spec)
        self.held.append(held)
        return ("out", len(self.shapes) - 1)

    def carry(self, operand):
        spec = pl.BlockSpec(memory_space=pl.ANY)
        return self.write(operand.shape, operand.dtype, spec, operand)


def fold(moving, after, passed=(), at_end=False):
    call = Call()
    call.scalar(jnp.int32(0))
    tasks = []
    for one in moving:
        if one.waiting:
            one.waiting -= 1
        elif one.ready():
            tasks.append(one.prepare(call))
    if not tasks:
        return after[0], passed
    token = call.write(
        TOKEN.shape, TOKEN.dtype, pl.BlockSpec(TOKEN.shape, lambda j, side: (0, 0))
    )
    tasks.append((lambda refs: token_of(refs[token]), lambda out: None))
    spare = pl.BlockSpec(memory_space=pl.ANY)
    kept_back = [(i, one) for i, one in enumerate(call.held) if one is not None]
    for array in passed:
        kept_back.append((len(call.shapes), array))
        call.shapes.append(jax.ShapeDtypeStruct(array.shape, array.dtype))
        call.out_specs.append(spare)
    inputs = len(call.operands)
    unused = len(kept_back) + len(after)

    def kernel(side_ref, *refs):
        where = {}
        for i in range(inputs):
            where[("in", i)] = refs[i]
        for i in range(len(call.shapes)):
            where[("out", i)] = refs[inputs + unused + i]
        for work, _ in tasks:
            work(where)

    size = sum(math.prod(shape.shape) for shape in call.shapes)
    out = pl.pallas_call(
        kernel,
        grid_spec=pltpu.PrefetchScalarGridSpec(
            num_scalar_prefetch=1,
            grid=(call.count,),
            in_specs=call.in_specs + [spare] * unused,
            out_specs=call.out_specs,
        ),
        out_shape=call.shapes,
        input_output_aliases={1 + inputs + i: at for i, (at, _) in enumerate(kept_back)},
        compiler_params=params(16 if at_end else 64),
        cost_estimate=pl.CostEstimate(flops=size, bytes_accessed=6 * size, transcendentals=0),
        name="fold",
    )(
        jnp.stack(call.scalars).astype(jnp.int32),
        *call.operands,
        *[array for _, array in kept_back],
        *after,
    )
    for _, finish in tasks:
        finish(lambda write: out[write[1]])
    moving[:] = [one for one in moving if not one.finished]
    return out[token[1]], tuple(out[len(out) - len(passed) :])


def exchange(value, axis, size, bit):
    return lax.ppermute(value, axis, [(i, i ^ bit) for i in range(size)])


def bits_of(size):
    return [1 << i for i in range(size.bit_length() - 1)]


def shards(
    dp_size,
    blk_size,
    embedded,
    species_flag,
    gene_ids,
    species_table,
    norm_gain,
    norm_bias,
    w_qkv,
    w_out,
    w_up,
    w_down,
    out_cotangent,
):
    _, block_len, width = embedded.shape
    half = blk_size // 2
    place = lax.axis_index("blk")
    mine = place // half

    def swap(value):
        return exchange(value, "blk", blk_size, half)

    def own_and_other(pair):
        first = mine == 0
        return jnp.where(first, pair[0], pair[1]), jnp.where(first, pair[1], pair[0])

    def collect(pair):
        own, other = own_and_other(pair)
        return own, swap(other)

    def turn(value, by):
        pairs = []
        for b in range(blk_size):
            base, j = b // half * half, b % half
            pairs.append((b, base + (j - by) % half))
        return lax.ppermute(value, "blk", pairs)

    def gather_parts(value):
        return [value] + [turn(value, by) for by in range(1, half)]

    ids = jnp.concatenate(collect(gene_ids))
    dead = jnp.where(ids != 0, 0.0, MASKED).astype(BF16)
    dead_parts = [
        jnp.broadcast_to(part[:, None], (part.shape[0], PAIR)) for part in gather_parts(dead)
    ]
    species, _ = own_and_other(species_flag)
    picked = jnp.where(species == 0, species_table[0], species_table[1])
    state = Tokens(collect(embedded), picked[None, :])
    cotangent = Tokens(collect(out_cotangent))

    kept = []
    for layer in range(LAYERS):
        first = tuple(dead_parts) if layer == 0 else ()
        h1, q, kv = qkv_forward(layer, state, norm_gain, norm_bias, w_qkv, first)
        kv_parts = gather_parts(kv)
        att, inverse, p = attend(q, kv_parts, dead_parts)
        mid, h2, att_turned, active, slope, after = feed_forward(
            layer, att, state, w_out, norm_gain, norm_bias, w_up, w_down
        )
        kept.append(
            (state, h1, q, kv_parts, att, inverse, p, mid, h2, att_turned, active, slope)
        )
        state = Tokens([after])
    came = swap(after[block_len:].astype(BF16))
    hidden_out, placed = place_cells(mine[None], after, came)

    sizes = {"blk": blk_size, "dp": dp_size}
    places = {"blk": place, "dp": lax.axis_index("dp")}
    core = place % 2
    over_blk = [("blk", bit) for bit in bits_of(blk_size)[1:]]
    over_dp = [("dp", bit) for bit in bits_of(dp_size)]
    core = core[None]

    def column_sums(pair, orders, layer, results, waits):
        gone, own = (value.reshape((half * dp_size,) + value.shape[-2:]) for value in pair)
        came = exchange(gone, "blk", blk_size, 1)
        scatter = waits if layer > 0 else 0
        if own.shape[1] % (16 * len(orders)):
            orders = orders[:1]
        return [
            Sum(came, own, order, sizes, places, layer, results, scatter, (i, len(orders)))
            for i, order in enumerate(orders)
        ]

    up_width = w_up.shape[2] // blk_size
    of_up_out = Results([("up", up_width), ("out", width // blk_size)])
    of_down = Results([("down", w_down.shape[1] // dp_size)])
    of_qkv = Results([("qkv", 3 * width // blk_size)])
    groups = 2
    grad = cotangent
    moving = []
    last = ()
    small = jnp.zeros((16, width), F32)
    species = species[None]
    for layer in reversed(range(LAYERS)):
        x, h1, q, kv_parts, att, inverse, p, mid, h2, att_turned, active, slope = kept[layer]
        up_gone, up_kept, down_gone, down_kept, dmid, datt, small = feed_backward(
            layer,
            grad,
            slope,
            active,
            mid,
            h2,
            att_turned,
            norm_gain,
            w_down,
            w_up,
            w_out,
            small,
            core,
            blk_size,
            dp_size,
            last,
        )
        last = (datt,)
        if moving:
            added, _ = fold(moving, last)
            last = (added,)
        moving += column_sums((up_gone, up_kept), [over_blk + over_dp], layer, of_up_out, 3)
        moving += column_sums((down_gone, down_kept), [over_dp + over_blk], layer, of_down, 3)
        arrived = (came,)
        dq, dkv = [], []
        for group in range(groups):
            one_dq, one_dkv = attend_back(
                group, groups, q, inverse, att, datt, p, kv_parts, last
            )
            others = tuple(one_dkv[1:])
            if group == groups - 1:
                added, others = fold(moving, (one_dq,) + arrived, others)
            else:
                added, _ = fold(moving, (one_dq,) + arrived)
            arrived = tuple(turn(value, half - 1 - by) for by, value in enumerate(others))
            last = (added,)
            dq.append(one_dq)
            dkv.append((one_dkv[0],) + arrived)
        if layer > 0:
            orders = [over_dp + over_blk]
        else:
            near, far = over_dp[:1], over_dp[1:]
            orders = [near + over_blk + far, far[:1] + near + over_blk + far[1:]]
        tiles = 2 * block_len // min(256, block_len)
        ends = tiles if layer > 0 else tiles // 2
        moved = x if layer > 0 else Tokens([x.arrays[1]], x.shift)
        gone, own, one_grad, small = qkv_gradients(
            layer,
            ends,
            F32 if layer > 0 else BF16,
            dq,
            dkv,
            moved,
            norm_gain,
            w_qkv,
            h1,
            dmid,
            small,
            species,
            core,
            blk_size,
            dp_size,
            last,
        )
        if layer == 0:
            added, (one_grad, gone) = fold(moving, (own,), (one_grad, gone))
            last = (added,)
        moving += column_sums((gone, own), orders, layer, of_qkv, 0)
        if layer > 0:
            last = (one_grad,)
            grad = Tokens([one_grad])
        else:
            came = swap(one_grad)
            own_x = Tokens([x.arrays[0]], x.shift)
            own_grad, small = qkv_backward(
                layer, 0, F32, dq, dkv, own_x, norm_gain, w_qkv, dmid, small, species, last
            )
            added, (small,) = fold(moving, (own_grad, came), (small,))
            last = (added,)
    small = SmallSum(small, sizes)
    moving.append(small)
    embed_grad, embed_placed = place_cells(mine[None], own_grad, came)
    last += (placed, embed_placed)
    while moving:
        added, _ = fold(moving, last, (), True)
        last = (added,)

    gain_grad, bias_grad, species_grad = small.value
    return (
        hidden_out,
        embed_grad,
        species_grad,
        gain_grad,
        bias_grad,
        of_qkv.held["qkv"],
        of_up_out.held["out"],
        of_up_out.held["up"],
        of_down.held["down"].transpose(0, 2, 1),
    )


def solution(mesh):
    placed = (
        P("dp", "blk", None),
        P("dp"),
        P("dp", "blk"),
        P(),
        P(),
        P(),
        P(),
        P(),
        P(),
        P(),
        P("dp", "blk", None),
    )
    return jax.shard_map(
        functools.partial(shards, mesh.shape["dp"], mesh.shape["blk"]),
        mesh=mesh,
        in_specs=placed,
        out_specs=(
            P("dp", "blk", None),
            P("dp", "blk", None),
            P(),
            P(),
            P(),
            P(None, "dp", "blk"),
            P(None, "dp", "blk"),
            P(None, "dp", "blk"),
            P(None, "dp", "blk"),
        ),
        check_vma=False,
    )
```

time: 1930 us -> 593 us (0.31)
  waiting for transfers between devices: 787 us -> 62.8 us
  matrix products: 694 us -> 0 us
  Pallas kernels: 0 us -> 449 us
  other arithmetic: 227 us -> 6.17 us
  local copies, waits for them, and re-layouts: 156 us -> 11.9 us
  blocking collectives: 49.2 us -> 0 us
  starting transfers between devices: 0.5 us -> 38.9 us
    dot_general x36 -> x0, matrix products: 615 us -> none  [the longest x2 130 us: shards(): jnp.einsum('cqhd,ckhd->chqk', d_att, values_all, preferred_element_type=j...]
    reduce_scatter x7 -> x4, waiting for transfers between devices: 583 us -> 0.04 us  [the longest x2 0.04 us: finish(): self.kept = lax.psum_scatter(whole, 'dp', scatter_dimension=0, tiled=False)]
    pallas_call x0 -> x27, Pallas kernels: none -> 449 us  [the longest x4 121 us: attend_back(): pl.pallas_call(without(functools.partial(attend_back_kernel, parts), 5 +...]
    convert_element_type x8 -> x1, other arithmetic: 165 us -> 0.01 us  [shards(): dead = jnp.where(ids != 0, 0.0, MASKED).astype(BF16)]
    all_gather x2 -> x0, waiting for transfers between devices: 151 us -> none  [share_keys(): return (lax.all_gather(pairs, 'blk', axis=1, tiled=True), fixed_valid)]
    sub x2 -> x0, matrix products: 78.8 us -> none  [attend(): shifted = jnp.exp(scores - jnp.max(scores, axis=-1, keepdims=True))]
    ppermute x0 -> x44, waiting for transfers between devices: none -> 62.7 us  [the longest x37 51.5 us: exchange(): return lax.ppermute(value, axis, [(i, i ^ bit) for i in range(size)])]
    slice x13 -> x2, local copies, waits for them, and re-layouts: 65.3 us -> 2.97 us  [the longest x1 2.39 us: shards(): came = swap(after[block_len:].astype(BF16))]
  transfers between devices with their start and end apart: 12 -> 48, of which waited for: 10 -> 16; matrix products, arithmetic and copies ran while one was open for 10% -> 2% of each run, Pallas kernels for 0% -> 52%
where the time goes in v1:
time: 593 us; the launch traced here: 585 us
  Pallas kernels  449 us (76%)
  waiting for transfers between devices  62.8 us (11%)
  starting transfers between devices  38.9 us (7%)
  between operations  16 us (3%)
  local copies, waits for them, and re-layouts  11.9 us (2%)
  other arithmetic  6.17 us (1%)
    pallas_call x4, Pallas kernels, attend_back(): pl.pallas_call(without(functools.partial(attend_back_kernel, parts), 5 +...  121 us
    pallas_call x2, Pallas kernels, feed_backward(): pl.pallas_call(without(functools.partial(feed_back_kernel, layer, grad, d...  81.8 us
    pallas_call x2, Pallas kernels, attend(): pl.pallas_call(functools.partial(attend_kernel, parts), grid=(pairs, rows...  74.7 us
    pallas_call x2, Pallas kernels, feed_forward(): pl.pallas_call(functools.partial(feed_kernel, x, tile), grid=(rows // til...  60.2 us
    ppermute x37, waiting for transfers between devices, exchange(): return lax.ppermute(value, axis, [(i, i ^ bit) for i in range(size)])  51.5 us
    pallas_call x2, Pallas kernels, qkv_gradients(): pl.pallas_call(without(functools.partial(qkv_grad_kernel, layer, groups,...  40 us
    pallas_call x10, Pallas kernels, fold(): pl.pallas_call(kernel, grid_spec=pltpu.PrefetchScalarGridSpec(num_scalar_...  38.8 us
    ppermute x37, starting transfers between devices, exchange(): return lax.ppermute(value, axis, [(i, i ^ bit) for i in range(size)])  37.7 us
  transfers between devices with their start and end apart: 48, of which 16 were waited for; matrix products, arithmetic and copies ran while one was open for 2% of the time, Pallas kernels for 52%

profile of v1, /device:TPU:0, one launch (start us, length us, event | category | flops | bytes accessed | tf_op | source)
XLA Modules:
  0.0 585.2 jit_solution(10957749582935019700)
XLA Ops:
  14.6 15.6 %collective-permute-done.1 = s32[512]{0:T(512)S(1)} collective-permute-done((s32[512]{0:T(512)S(1)}, s32[512]{0:T(512)S(1)}, u32[]{:S(2)}, u32[]{:S(2)}) %collective-permute-start.1) | collective-permute-done | bytes 2080 | tf_op jit(solution)/shard_map/ppermute | solution.py:1229
  33.3 8.8 %norm_qkv.2 = (bf16[768,1024]{1,0:T(8,128)(2,1)}, bf16[1024,768]{1,0:T(8,128)(2,1)}, bf16[1024,1536]{1,0:T(8,128)(2,1)}) custom-call(bf16[512,768]{1,0:T(8,128)(2,1)} %get-tuple-element.282.refs_0_.refs_6_, bf16[512,768]{1,0:T(8,128)(2,1)} %copy-done.13, f32[1,768]{1,0:T(1,128)} %broadcast_select_fusion.refs_2_.refs_8_.refs_7_, f32[2,2,768]{2,1,0:T(2,128)} %refs_8_.9, ...), custom_call_target="tpu_custom_call" | custom-call | flops 3623878656 | bytes 9437184 | tf_op jit(solution)/shard_map/norm_qkv/pallas_call | solution.py:157
  42.2 5.8 collective-permute-done.3.refs_2_.refs_4_.refs_6_.refs_8_
  48.1 37.3 %attend.2 = (bf16[1024,768]{1,0:T(8,128)(2,1)}, f32[1024,768]{1,0:T(8,128)}, bf16[12,1024,2048]{2,1,0:T(8,128)(2,1)}) custom-call(bf16[1024,768]{1,0:T(8,128)(2,1)} %get-tuple-element.144.refs_0_, bf16[1024,1536]{1,0:T(8,128)(2,1)} %get-tuple-element.145.refs_1_.refs_3_.refs_5_.refs_7_, ...), custom_call_target="tpu_custom_call" | custom-call | flops 25769803776 | bytes 50331648 | tf_op jit(solution)/shard_map/attend/pallas_call | solution.py:242
  85.3 30.3 %feed.2 = (f32[1024,768]{1,0:T(8,128)}, bf16[768,1024]{1,0:T(8,128)(2,1)}, bf16[768,1024]{1,0:T(8,128)(2,1)}, bf16[1024,3072]{1,0:T(8,128)(2,1)}, bf16[1024,3072]{1,0:T(8,128)(2,1)}, /*index=5*/f32[1024,768]{1,0:T(8,128)}) custom-call(bf16[512,768]{1,0:T(8,128)(2,1)} %get-tuple-element.282.refs_0_.refs_6_, bf16[512,768]{1,0:T(8,128)(2,1)} %copy-done.13, ...), custom_call_target="tpu_custom_call" | custom-call | flops 10871635968 | bytes 34603008 | tf_op jit(solution)/shard_map/feed/pallas_call | solution.py:422
  115.6 9.0 %norm_qkv.3 = (bf16[768,1024]{1,0:T(8,128)(2,1)}, bf16[1024,768]{1,0:T(8,128)(2,1)}, bf16[1024,1536]{1,0:T(8,128)(2,1)}) custom-call(f32[1024,768]{1,0:T(8,128)} %get-tuple-element.147.refs_0_.refs_7_, f32[2,2,768]{2,1,0:T(2,128)} %refs_8_.9, f32[2,2,768]{2,1,0:T(2,128)} %refs_4_.5, bf16[2,768,2304]{2,1,0:T(8,128)(2,1)} %refs_9_.9), custom_call_target="tpu_custom_call" | custom-call | flops 3623878656 | bytes 9437184 | tf_op jit(solution)/shard_map/norm_qkv/pallas_call | solution.py:157
  130.6 37.5 %attend.3 = (bf16[1024,768]{1,0:T(8,128)(2,1)}, f32[1024,768]{1,0:T(8,128)}, bf16[12,1024,2048]{2,1,0:T(8,128)(2,1)}) custom-call(bf16[1024,768]{1,0:T(8,128)(2,1)} %get-tuple-element.148.refs_0_, bf16[1024,1536]{1,0:T(8,128)(2,1)} %get-tuple-element.149.refs_1_.refs_3_.refs_5_.refs_7_, ...), custom_call_target="tpu_custom_call" | custom-call | flops 25769803776 | bytes 50331648 | tf_op jit(solution)/shard_map/attend/pallas_call | solution.py:242
  168.1 29.9 %feed.3 = (f32[1024,768]{1,0:T(8,128)}, bf16[768,1024]{1,0:T(8,128)(2,1)}, bf16[768,1024]{1,0:T(8,128)(2,1)}, bf16[1024,3072]{1,0:T(8,128)(2,1)}, bf16[1024,3072]{1,0:T(8,128)(2,1)}, /*index=5*/f32[1024,768]{1,0:T(8,128)}) custom-call(f32[1024,768]{1,0:T(8,128)} %get-tuple-element.147.refs_0_.refs_7_, bf16[1024,768]{1,0:T(8,128)(2,1)} %get-tuple-element.150.refs_1_.refs_2_, ...), custom_call_target="tpu_custom_call" | custom-call | flops 10871635968 | bytes 34603008 | tf_op jit(solution)/shard_map/feed/pallas_call | solution.py:422
  198.6 40.5 %feed_back.2 = (bf16[8,2,96,960]{3,2,1,0:T(8,128)(2,1)}, bf16[8,2,96,960]{3,2,1,0:T(8,128)(2,1)}, bf16[8,2,192,384]{3,2,1,0:T(8,128)(2,1)}, bf16[8,2,192,384]{3,...) custom-call(s32[1]{0:T(128)} %bitcast.7.refs_0_, ...), custom_call_target="tpu_custom_call" | custom-call | flops 21743271936 | bytes 47185920 | tf_op jit(solution)/shard_map/feed_back/pallas_call | solution.py:603
  243.9 30.2 %attend_back.4 = (bf16[1024,384]{1,0:T(8,128)(2,1)}, bf16[2,1024,384]{2,1,0:T(8,128)(2,1)}, bf16[2,1024,384]{2,1,0:T(8,128)(2,1)}) custom-call(bf16[1024,768]{1,0:T(8,128)(2,1)} %get-tuple-element.148.refs_0_, f32[1024,768]{1,0:T(8,128)} %get-tuple-element.154.refs_1_, bf16[1024,768]{1,0:T(8,128)(2,1)} %get-tuple-element.150.refs_1_.refs_2_, ...), custom_call_target="tpu_custom_call" | custom-call | flops 25769803776 | bytes 25165824 | tf_op jit(solution)/shard_map/attend_back/pallas_call | solution.py:331
  274.1 6.8 %fold.10 = (bf16[16,1,1,96,960]{4,3,2,1,0:T(8,128)(2,1)}, bf16[16,1,1,192,384]{4,3,2,1,0:T(8,128)(2,1)}, f32[8,128]{1,0:T(8,128)}) custom-call(s32[1]{0:T(128)} %constant.146.clone.1.side_ref, bf16[16,1,1,96,960]{4,3,2,1,0:T(8,128)(2,1)} %bitcast.153, bf16[16,1,1,96,960]{4,3,2,1,0:T(8,128)(2,1)} %bitcast.12.refs_1_, bf16[16,1,1,192,384]{4,3,2,1,0:T(8,128)(2,1)} %bitcast.157, ...), custom_call_target="tpu_custom_call" | custom-call | flops 2655232 | bytes 15931392 | tf_op jit(solution)/shard_map/fold/pallas_call | solution.py:1203
  281.1 30.1 %attend_back.5 = (bf16[1024,384]{1,0:T(8,128)(2,1)}, bf16[2,1024,384]{2,1,0:T(8,128)(2,1)}, bf16[2,1024,384]{2,1,0:T(8,128)(2,1)}) custom-call(bf16[1024,768]{1,0:T(8,128)(2,1)} %get-tuple-element.148.refs_0_, f32[1024,768]{1,0:T(8,128)} %get-tuple-element.154.refs_1_, bf16[1024,768]{1,0:T(8,128)(2,1)} %get-tuple-element.150.refs_1_.refs_2_, ...), custom_call_target="tpu_custom_call" | custom-call | flops 25769803776 | bytes 25165824 | tf_op jit(solution)/shard_map/attend_back/pallas_call | solution.py:331
  315.1 21.3 %qkv_grad.2 = (bf16[8,2,96,576]{3,2,1,0:T(8,128)(2,1)}, bf16[8,2,96,576]{3,2,1,0:T(8,128)(2,1)}, f32[1024,768]{1,0:T(8,128)}, f32[16,768]{1,0:T(8,128)}) custom-call(s32[1]{0:T(128)} %bitcast.7.refs_0_, bf16[1024,384]{1,0:T(8,128)(2,1)} %get-tuple-element.162.refs_4_.refs_1_, bf16[1024,384]{1,0:T(8,128)(2,1)} %get-tuple-element.168.refs_2_.refs_14_, ...), custom_call_target="tpu_custom_call" | custom-call | flops 7247757312 | bytes 25165824 | tf_op jit(solution)/shard_map/qkv_grad/pallas_call | solution.py:766
  336.9 41.2 %feed_back.3 = (bf16[8,2,96,960]{3,2,1,0:T(8,128)(2,1)}, bf16[8,2,96,960]{3,2,1,0:T(8,128)(2,1)}, bf16[8,2,192,384]{3,2,1,0:T(8,128)(2,1)}, bf16[8,2,192,384]{3,...) custom-call(s32[1]{0:T(128)} %bitcast.7.refs_0_, ...), custom_call_target="tpu_custom_call" | custom-call | flops 21743271936 | bytes 47185920 | tf_op jit(solution)/shard_map/feed_back/pallas_call | solution.py:603
  385.8 30.2 %attend_back.6 = (bf16[1024,384]{1,0:T(8,128)(2,1)}, bf16[2,1024,384]{2,1,0:T(8,128)(2,1)}, bf16[2,1024,384]{2,1,0:T(8,128)(2,1)}) custom-call(bf16[1024,768]{1,0:T(8,128)(2,1)} %get-tuple-element.144.refs_0_, f32[1024,768]{1,0:T(8,128)} %get-tuple-element.153.refs_1_, bf16[1024,768]{1,0:T(8,128)(2,1)} %get-tuple-element.146.refs_3_.refs_2_, ...), custom_call_target="tpu_custom_call" | custom-call | flops 25769803776 | bytes 25165824 | tf_op jit(solution)/shard_map/attend_back/pallas_call | solution.py:331
  416.9 9.2 %fold.12 = (bf16[2,1,2,96,576]{4,3,2,1,0:T(8,128)(2,1)}, bf16[2,1,2,96,576]{4,3,2,1,0:T(8,128)(2,1)}, bf16[8,1,1,96,960]{4,3,2,1,0:T(8,128)(2,1)}, bf16[8,1,1,96...) custom-call(s32[7]{0:T(128)} %stack.39.side_ref, ...), custom_call_target="tpu_custom_call" | custom-call | flops 3097600 | bytes 18585600 | tf_op jit(solution)/shard_map/fold/pallas_call | solution.py:1203
  429.5 30.1 %attend_back.7 = (bf16[1024,384]{1,0:T(8,128)(2,1)}, bf16[2,1024,384]{2,1,0:T(8,128)(2,1)}, bf16[2,1024,384]{2,1,0:T(8,128)(2,1)}) custom-call(bf16[1024,768]{1,0:T(8,128)(2,1)} %get-tuple-element.144.refs_0_, f32[1024,768]{1,0:T(8,128)} %get-tuple-element.153.refs_1_, bf16[1024,768]{1,0:T(8,128)(2,1)} %get-tuple-element.146.refs_3_.refs_2_, ...), custom_call_target="tpu_custom_call" | custom-call | flops 25769803776 | bytes 25165824 | tf_op jit(solution)/shard_map/attend_back/pallas_call | solution.py:331
  462.5 5.1 fold.13
  473.1 18.8 %qkv_grad.3 = (bf16[8,2,96,576]{3,2,1,0:T(8,128)(2,1)}, bf16[8,2,96,576]{3,2,1,0:T(8,128)(2,1)}, bf16[512,768]{1,0:T(8,128)(2,1)}, f32[16,768]{1,0:T(8,128)}) custom-call(s32[1]{0:T(128)} %bitcast.7.refs_0_, bf16[1024,384]{1,0:T(8,128)(2,1)} %get-tuple-element.188.refs_12_.refs_1_.refs_0_, bf16[1024,384]{1,0:T(8,128)(2,1)} %get-tuple-element.196.refs_15_.refs_2_.refs_1_, ...), custom_call_target="tpu_custom_call" | custom-call | flops 7247757312 | bytes 25165824 | tf_op jit(solution)/shard_map/qkv_grad/pallas_call | solution.py:766
  501.4 7.4 %qkv_back.1 = (f32[512,768]{1,0:T(8,128)}, f32[16,768]{1,0:T(8,128)}) custom-call(bf16[1024,384]{1,0:T(8,128)(2,1)} %get-tuple-element.188.refs_12_.refs_1_.refs_0_, bf16[1024,384]{1,0:T(8,128)(2,1)} %get-tuple-element.196.refs_15_.refs_2_.refs_1_, bf16[2,1024,384]{2,1,0:T(8,128)(2,1)} %get-tuple-element.197.refs_3_.refs_2_, ...), custom_call_target="tpu_custom_call" | custom-call | flops 1811939328 | bytes 9437184 | tf_op jit(solution)/shard_map/qkv_back/pallas_call | solution.py:837
  508.7 15.5 %collective-permute-done.24 = bf16[1,1,1,96,576]{4,3,2,1,0:T(8,128)(2,1)} collective-permute-done((bf16[1,1,1,96,576]{4,3,2,1,0:T(8,128)(2,1)}, bf16[1,1,1,96,576]{4,3,2,1,0:T(8,128)(2,1)}, u32[]{:S(2)}, u32[]{:S(2)}) %collective-permute-start.24) | collective-permute-done | bytes 110624 | tf_op jit(solution)/shard_map/ppermute | solution.py:1229
  524.3 5.1 fold.15
  533.2 4.0 place_cells.2
  549.8 7.2 %collective-permute-done.29 = bf16[1,1,1,192,384]{4,3,2,1,0:T(8,128)(2,1)S(1)} collective-permute-done((bf16[1,1,1,192,384]{4,3,2,1,0:T(8,128)(2,1)}, bf16[1,1,1,192,384]{4,3,2,1,0:T(8,128)(2,1)S(1)}, u32[]{:S(2)}, u32[]{:S(2)}) %collective-permute-start.29) | collective-permute-done | bytes 147488 | tf_op jit(solution)/shard_map/ppermute | solution.py:1229
  (149 shorter events, 92.3 us)
Async XLA Ops:
  7.2 452.4 %reduce-scatter.7.cloned.1.call-start = ((), (), s32[]{:S(2)}) async-start(), calls=%async_computation.5 | async-start | bytes 2654208 | tf_op jit(solution)/shard_map/reduce_scatter | solution.py:967
  127.4 70.6 %collective-permute-start.6 = (bf16[512,768]{1,0:T(8,128)(2,1)}, bf16[512,768]{1,0:T(8,128)(2,1)}, u32[]{:S(2)}, u32[]{:S(2)}) collective-permute-start(bf16[512,768]{1,0:T(8,128)(2,1)} %get-tuple-element.279), channel_id=1, source_target_pairs={{0,2},{1,3},{2,0},{3,1},{4,6},{5,7},{6,4},{7,5},{8,10},{9,11},{10,... | collective-permute-start | bytes 2359304 | tf_op jit(solution)/shard_map/ppermute | solution.py:1229
  239.2 35.0 %collective-permute-start.7 = (bf16[16,96,960]{2,1,0:T(8,128)(2,1)}, bf16[16,96,960]{2,1,0:T(8,128)(2,1)}, u32[]{:S(2)}, u32[]{:S(2)}) collective-permute-start(bf16[16,96,960]{2,1,0:T(8,128)(2,1)} %bitcast.174), channel_id=1, source_target_pairs={{0,1},{1,0},{2,3},{3,2},{4,5},{5,4},{6,7},{7,6},{8,9},{9,8},{10,11... | collective-permute-start | bytes 8847368 | tf_op jit(solution)/shard_map/ppermute | solution.py:1229
  239.4 34.7 %collective-permute-start.8 = (bf16[16,192,384]{2,1,0:T(8,128)(2,1)}, bf16[16,192,384]{2,1,0:T(8,128)(2,1)}, u32[]{:S(2)}, u32[]{:S(2)}) collective-permute-start(bf16[16,192,384]{2,1,0:T(8,128)(2,1)} %bitcast.176), channel_id=1, source_target_pairs={{0,1},{1,0},{2,3},{3,2},{4,5},{5,4},{6,7},{7,6},{8,9},{9,8},{10,11... | collective-permute-start | bytes 7077896 | tf_op jit(solution)/shard_map/ppermute | solution.py:1229
  242.1 32.0 %collective-permute-start.5 = (bf16[512,768]{1,0:T(8,128)(2,1)}, bf16[512,768]{1,0:T(8,128)(2,1)}, u32[]{:S(2)}, u32[]{:S(2)}) collective-permute-start(bf16[512,768]{1,0:T(8,128)(2,1)} %slice.67), channel_id=1, source_target_pairs={{0,2},{1,3},{2,0},{3,1},{4,6},{5,7},{6,4},{7,5},{8,10},{9,11},{10,... | collective-permute-start | bytes 2359304 | tf_op jit(solution)/shard_map/ppermute | solution.py:1229
  281.0 178.7 %reduce-scatter.5.cloned.1.call-start = ((), (), s32[]{:S(2)}) async-start(), calls=%async_computation.4 | async-start | bytes 3538944 | tf_op jit(solution)/shard_map/reduce_scatter | solution.py:967
  281.0 30.7 %collective-permute-start.9 = (bf16[2,1024,384]{2,1,0:T(8,128)(2,1)}, bf16[2,1024,384]{2,1,0:T(8,128)(2,1)}, u32[]{:S(2)}, u32[]{:S(2)}) collective-permute-start(bf16[2,1024,384]{2,1,0:T(8,128)(2,1)} %get-tuple-element.170), channel_id=1, source_target_pairs={{0,1},{1,0},{2,3},{3,2},{4,5},{5,4},{6,7},{7,6},{8,9},{9,8},{10,11... | collective-permute-start | bytes 4718600 | tf_op jit(solution)/shard_map/ppermute | solution.py:1272
  311.7 229.5 %reduce-scatter.11.cloned.1.call-start = ((), (), s32[]{:S(2)}) async-start(), calls=%async_computation.7 | async-start | bytes 442368 | tf_op jit(solution)/shard_map/reduce_scatter | solution.py:983
  336.3 44.1 %collective-permute-start.11 = (bf16[16,96,576]{2,1,0:T(8,128)(2,1)}, bf16[16,96,576]{2,1,0:T(8,128)(2,1)}, u32[]{:S(2)}, u32[]{:S(2)}) collective-permute-start(bf16[16,96,576]{2,1,0:T(8,128)(2,1)} %bitcast.177), channel_id=1, source_target_pairs={{0,1},{1,0},{2,3},{3,2},{4,5},{5,4},{6,7},{7,6},{8,9},{9,8},{10,11... | collective-permute-start | bytes 5308424 | tf_op jit(solution)/shard_map/ppermute | solution.py:1229
  378.1 38.8 %collective-permute-start.13 = (bf16[16,96,960]{2,1,0:T(8,128)(2,1)}, bf16[16,96,960]{2,1,0:T(8,128)(2,1)}, u32[]{:S(2)}, u32[]{:S(2)}) collective-permute-start(bf16[16,96,960]{2,1,0:T(8,128)(2,1)} %bitcast.173), channel_id=1, source_target_pairs={{0,1},{1,0},{2,3},{3,2},{4,5},{5,4},{6,7},{7,6},{8,9},{9,8},{10,11... | collective-permute-start | bytes 8847368 | tf_op jit(solution)/shard_map/ppermute | solution.py:1229
  380.0 36.1 %collective-permute-start.14 = (bf16[16,192,384]{2,1,0:T(8,128)(2,1)}, bf16[16,192,384]{2,1,0:T(8,128)(2,1)}, u32[]{:S(2)}, u32[]{:S(2)}) collective-permute-start(bf16[16,192,384]{2,1,0:T(8,128)(2,1)} %bitcast.175), channel_id=1, source_target_pairs={{0,1},{1,0},{2,3},{3,2},{4,5},{5,4},{6,7},{7,6},{8,9},{9,8},{10,11... | collective-permute-start | bytes 7077896 | tf_op jit(solution)/shard_map/ppermute | solution.py:1229
  384.3 32.5 %collective-permute-start.12 = (bf16[4,1,2,96,576]{4,3,2,1,0:T(8,128)(2,1)}, bf16[4,1,2,96,576]{4,3,2,1,0:T(8,128)(2,1)}, u32[]{:S(2)}, u32[]{:S(2)}) collective-permute-start(bf16[4,1,2,96,576]{4,3,2,1,0:T(8,128)(2,1)} %get-tuple-element.190), channel_id=1, source_target_pairs={{0,4},{4,0},{8,12},{12,8},{16,20},{20,16},{24,28},{28,24},{1,5},{5... | collective-permute-start | bytes 2654216 | tf_op jit(solution)/shard_map/ppermute | solution.py:1229
  416.1 43.5 %collective-permute-start.15 = (bf16[2,1024,384]{2,1,0:T(8,128)(2,1)}, bf16[2,1024,384]{2,1,0:T(8,128)(2,1)}, u32[]{:S(2)}, u32[]{:S(2)}) collective-permute-start(bf16[2,1024,384]{2,1,0:T(8,128)(2,1)} %get-tuple-element.198), channel_id=1, source_target_pairs={{0,1},{1,0},{2,3},{3,2},{4,5},{5,4},{6,7},{7,6},{8,9},{9,8},{10,11... | collective-permute-start | bytes 4718600 | tf_op jit(solution)/shard_map/ppermute | solution.py:1272
  426.1 36.4 %collective-permute-start.17 = (bf16[8,1,1,96,960]{4,3,2,1,0:T(8,128)(2,1)}, bf16[8,1,1,96,960]{4,3,2,1,0:T(8,128)(2,1)}, u32[]{:S(2)}, u32[]{:S(2)}) collective-permute-start(bf16[8,1,1,96,960]{4,3,2,1,0:T(8,128)(2,1)} %get-tuple-element.203), channel_id=1, source_target_pairs={{0,2},{1,3},{2,0},{3,1},{4,6},{5,7},{6,4},{7,5},{8,10},{9,11},{10,... | collective-permute-start | bytes 4423688 | tf_op jit(solution)/shard_map/ppermute | solution.py:1229
  426.5 33.2 %collective-permute-start.18 = (bf16[4,1,2,192,384]{4,3,2,1,0:T(8,128)(2,1)}, bf16[4,1,2,192,384]{4,3,2,1,0:T(8,128)(2,1)}, u32[]{:S(2)}, u32[]{:S(2)}) collective-permute-start(bf16[4,1,2,192,384]{4,3,2,1,0:T(8,128)(2,1)} %get-tuple-element.205), channel_id=1, source_target_pairs={{0,4},{4,0},{8,12},{12,8},{16,20},{20,16},{24,28},{28,24},{1,5},{5... | collective-permute-start | bytes 3538952 | tf_op jit(solution)/shard_map/ppermute | solution.py:1229
  428.2 31.4 %collective-permute-start.16 = (bf16[2,1,2,96,576]{4,3,2,0,1:T(8,128)(2,1)}, bf16[2,1,2,96,576]{4,3,2,0,1:T(8,128)(2,1)}, u32[]{:S(2)}, u32[]{:S(2)}) collective-permute-start(bf16[2,1,2,96,576]{4,3,2,0,1:T(8,128)(2,1)} %bitcast.180), channel_id=1, source_target_pairs={{0,8},{4,12},{8,0},{12,4},{16,24},{20,28},{24,16},{28,20},{1,9},{5... | collective-permute-start | bytes 1327112 | tf_op jit(solution)/shard_map/ppermute | solution.py:1229
  467.7 24.2 %collective-permute-start.21 = (bf16[4,1,1,96,960]{4,3,2,1,0:T(8,128)(2,1)}, bf16[4,1,1,96,960]{4,3,2,1,0:T(8,128)(2,1)}, u32[]{:S(2)}, u32[]{:S(2)}) collective-permute-start(bf16[4,1,1,96,960]{4,3,2,1,0:T(8,128)(2,1)} %get-tuple-element.218), channel_id=1, source_target_pairs={{0,4},{4,0},{8,12},{12,8},{16,20},{20,16},{24,28},{28,24},{1,5},{5... | collective-permute-start | bytes 2211848 | tf_op jit(solution)/shard_map/ppermute | solution.py:1229
  469.4 22.5 %collective-permute-start.22 = (bf16[2,1,2,192,384]{4,3,2,0,1:T(8,128)(2,1)}, bf16[2,1,2,192,384]{4,3,2,0,1:T(8,128)(2,1)}, u32[]{:S(2)}, u32[]{:S(2)}) collective-permute-start(bf16[2,1,2,192,384]{4,3,2,0,1:T(8,128)(2,1)} %bitcast.178), channel_id=1, source_target_pairs={{0,8},{4,12},{8,0},{12,4},{16,24},{20,28},{24,16},{28,20},{1,9},{5... | collective-permute-start | bytes 1769480 | tf_op jit(solution)/shard_map/ppermute | solution.py:1229
  495.7 28.5 %collective-permute-start.27 = (bf16[16,96,576]{2,1,0:T(8,128)(2,1)}, bf16[16,96,576]{2,1,0:T(8,128)(2,1)}, u32[]{:S(2)}, u32[]{:S(2)}) collective-permute-start(bf16[16,96,576]{2,1,0:T(8,128)(2,1)} %bitcast.158), channel_id=1, source_target_pairs={{0,1},{1,0},{2,3},{3,2},{4,5},{5,4},{6,7},{7,6},{8,9},{9,8},{10,11... | collective-permute-start | bytes 5308424 | tf_op jit(solution)/shard_map/ppermute | solution.py:1229
  495.9 45.4 %reduce-scatter.9.cloned.1.call-start = ((), (), s32[]{:S(2)}) async-start(), calls=%async_computation.6 | async-start | bytes 589824 | tf_op jit(solution)/shard_map/reduce_scatter | solution.py:983
  495.9 28.4 %collective-permute-start.23 = (bf16[512,768]{1,0:T(8,128)(2,1)}, bf16[512,768]{1,0:T(8,128)(2,1)}, u32[]{:S(2)}, u32[]{:S(2)}) collective-permute-start(bf16[512,768]{1,0:T(8,128)(2,1)} %get-tuple-element.226), channel_id=1, source_target_pairs={{0,2},{1,3},{2,0},{3,1},{4,6},{5,7},{6,4},{7,5},{8,10},{9,11},{10,... | collective-permute-start | bytes 2359304 | tf_op jit(solution)/shard_map/ppermute | solution.py:1229
  496.3 28.0 %collective-permute-start.25 = (bf16[2,1,1,96,960]{4,3,0,2,1:T(8,128)(2,1)}, bf16[2,1,1,96,960]{4,3,0,2,1:T(8,128)(2,1)}, u32[]{:S(2)}, u32[]{:S(2)}) collective-permute-start(bf16[2,1,1,96,960]{4,3,0,2,1:T(8,128)(2,1)} %bitcast.181), channel_id=1, source_target_pairs={{0,8},{4,12},{8,0},{12,4},{16,24},{20,28},{24,16},{28,20},{1,9},{5... | collective-permute-start | bytes 1105928 | tf_op jit(solution)/shard_map/ppermute | solution.py:1229
  497.4 26.9 %collective-permute-start.26 = (bf16[1,1,2,192,384]{4,3,2,1,0:T(8,128)(2,1)}, bf16[1,1,2,192,384]{4,3,2,1,0:T(8,128)(2,1)}, u32[]{:S(2)}, u32[]{:S(2)}) collective-permute-start(bf16[1,1,2,192,384]{4,3,2,1,0:T(8,128)(2,1)} %get-tuple-element.233), channel_id=1, source_target_pairs={{0,16},{4,20},{8,24},{12,28},{16,0},{20,4},{24,8},{28,12},{1,17},{... | collective-permute-start | bytes 884744 | tf_op jit(solution)/shard_map/ppermute | solution.py:1229
  499.9 24.4 %collective-permute-start.24 = (bf16[1,1,1,96,576]{4,3,2,1,0:T(8,128)(2,1)}, bf16[1,1,1,96,576]{4,3,2,1,0:T(8,128)(2,1)}, u32[]{:S(2)}, u32[]{:S(2)}) collective-permute-start(bf16[1,1,1,96,576]{4,3,2,1,0:T(8,128)(2,1)} %get-tuple-element.229), channel_id=1, source_target_pairs={{0,2},{1,3},{2,0},{3,1},{4,6},{5,7},{6,4},{7,5},{8,10},{9,11},{10,... | collective-permute-start | bytes 331784 | tf_op jit(solution)/shard_map/ppermute | solution.py:1229
  (38 other events, 314.5 us)
Sparse Core Ops, SparseCore 0:
  281.1 69.2 reduce-scatter.6
  354.0 83.9 reduce-scatter.4
  496.0 13.8 reduce-scatter.10
  511.9 15.0 reduce-scatter.8

commit v2 on v1

--- a/solution.py
+++ b/solution.py
@@ -209,8 +209,8 @@
             extra = jnp.where(sub == 3, dead_refs[part][...].astype(F32), 0.0)
             ka[own, :] = jnp.where(low, k, extra).astype(BF16)
             kb[own, :] = jnp.where(low, extra, k).astype(BF16)
-            va[own, :] = jnp.where(low, v, 1.0).astype(BF16)
-            vb[own, :] = jnp.where(low, 1.0, v).astype(BF16)
+            va[:, own] = turned(jnp.where(low, v, 1.0))
+            vb[:, own] = turned(jnp.where(low, 1.0, v))
 
     low, sub = lanes_like(q_ref.shape)
     fourth = jnp.where(sub == 3, 1.0, 0.0)
@@ -219,13 +219,15 @@
     sb = mm_nt(jnp.where(low, fourth, q).astype(BF16), kb[...])
     pa = jnp.exp2(sa - jnp.max(sa, axis=-1, keepdims=True)).astype(BF16)
     p_ref[0] = pa
-    oa = mm(pa, va[...])
+    oa = mm_nt(va[...], pa)
     pb = jnp.exp2(sb - jnp.max(sb, axis=-1, keepdims=True)).astype(BF16)
     p_ref[1] = pb
-    ob = mm(pb, vb[...])
-    inverse = 1.0 / pltpu.roll(jnp.where(low, ob, oa), HEAD_DIM, 1)
-    inverse_ref[...] = inverse
-    o_ref[...] = (jnp.where(low, oa, ob) * inverse).astype(BF16)
+    ob = mm_nt(vb[...], pb)
+    inverse_a = 1.0 / oa[HEAD_DIM:, :]
+    inverse_b = 1.0 / ob[:HEAD_DIM, :]
+    value = jnp.concatenate([oa[:HEAD_DIM, :] * inverse_a, ob[HEAD_DIM:, :] * inverse_b], axis=0)
+    inverse_ref[...] = jnp.concatenate([inverse_a, inverse_b], axis=0).T
+    o_ref[...] = turned(value)
 
 
 def attend(q, kv_parts, dead_parts):
@@ -239,6 +241,7 @@
     second = pl.BlockSpec((rows, PAIR), lambda j, i: (0, pairs + j))
     fixed = pl.BlockSpec((rows, PAIR), lambda j, i: (0, 0))
     scratch = pltpu.VMEM((keys, PAIR), BF16)
+    turned_scratch = pltpu.VMEM((PAIR, keys), BF16)
     return pl.pallas_call(
         functools.partial(attend_kernel, parts),
         grid=(pairs, rows // tile),
@@ -249,7 +252,7 @@
             jax.ShapeDtypeStruct((rows, width), F32),
             jax.ShapeDtypeStruct((2 * pairs, rows, keys), BF16),
         ],
-        scratch_shapes=[scratch] * 4,
+        scratch_shapes=[scratch] * 2 + [turned_scratch] * 2,
         compiler_params=params(),
         cost_estimate=pl.CostEstimate(
             flops=16 * rows * keys * width,
@@ -277,7 +280,7 @@
         ones = jnp.where(sub < 3, 1.0, 0.0)
         for part in range(parts):
             own = slice(part * rows, (part + 1) * rows)
-            ks[own, :] = k_refs[part][...]
+            ks[:, own] = turned(k_refs[part][...].astype(F32))
             v = v_refs[part][...].astype(F32)
             va[own, :] = jnp.where(low, v, ones).astype(BF16)
             vb[own, :] = jnp.where(low, ones, v).astype(BF16)
@@ -298,13 +301,13 @@
     pa, pb = p_ref[0], p_ref[1]
     dv_turned[first, :] += mm(datt_turned[first, :], pa)
     ga = (pa.astype(F32) * ta).astype(BF16)
-    dqa = mm(ga, ks[...])
+    dqa = mm_nt(ks[first, :], ga)
     dk_turned[first, :] += mm(q_turned[first, :], ga)
     dv_turned[second, :] += mm(datt_turned[second, :], pb)
     gb = (pb.astype(F32) * tb).astype(BF16)
-    dqb = mm(gb, ks[...])
+    dqb = mm_nt(ks[second, :], gb)
     dk_turned[second, :] += mm(q_turned[second, :], gb)
-    dq_ref[...] = (jnp.where(low, dqa, dqb) * SCALE).astype(BF16)
+    dq_ref[...] = turned(jnp.concatenate([dqa, dqb], axis=0) * SCALE)
 
     @pl.when(index == pl.num_programs(1) - 1)
     def _():
@@ -339,7 +342,7 @@
         out_specs=[pl.BlockSpec((tile, PAIR), lambda j, i: (i, j))] + [both] * parts,
         out_shape=[jax.ShapeDtypeStruct((rows, count * PAIR), BF16)]
         + [jax.ShapeDtypeStruct((2, rows, count * PAIR), BF16)] * parts,
-        scratch_shapes=[all_keys] * 3 + [turned_keys] * 2,
+        scratch_shapes=[pltpu.VMEM((PAIR, keys), BF16)] + [all_keys] * 2 + [turned_keys] * 2,
         compiler_params=params(),
         cost_estimate=pl.CostEstimate(
             flops=32 * rows * keys * width // groups,
@@ -354,7 +357,6 @@
 def gelu_parts(u):
     base = 1.0 + (0.3275911 * math.sqrt(0.5)) * jnp.abs(u)
     t = pl.reciprocal(base, approx=True)
-    t = t * (2.0 - base * t)
     bell = jnp.exp2(u * u * (-0.5 * LOG2E))
     series = t * (
         0.5 * 0.254829592
@@ -374,9 +376,13 @@
     return [slice(at, at + piece) for at in range(0, rows, piece)]
 
 
-def feed_kernel(x, tile, *refs):
+def feed_kernel(x, tile, last, *refs):
     att_ref, wout_ref, gain_ref, bias_ref, wup_ref, wdown_ref = refs[x.count() : x.count() + 6]
-    mid_ref, h_ref, att_turned_ref, act_ref, slope_ref, next_ref, h_kept = refs[x.count() + 6 :]
+    mid_ref, h_ref, att_turned_ref, act_ref, slope_ref = refs[x.count() + 6 : x.count() + 11]
+    if last:
+        own_ref, away_ref, h_kept, next_ref = refs[x.count() + 11 :]
+    else:
+        next_ref, h_kept = refs[x.count() + 11 :]
 
     @pl.when(pl.program_id(1) == 0)
     def _():
@@ -389,7 +395,7 @@
         h_ref[...] = turned(h)
         h_kept[...] = h.astype(BF16)
 
-    pieces = pieces_of(tile, 512)
+    pieces = pieces_of(tile, 256)
     ups = [mm(h_kept[pieces[0], :], wup_ref[...])]
     for i, piece in enumerate(pieces):
         if i + 1 < len(pieces):
@@ -399,6 +405,17 @@
         act_ref[piece, :] = active
         slope_ref[piece, :] = slope.astype(BF16)
         next_ref[piece, :] += mm(active, wdown_ref[...])
+    if last:
+        ends = pl.program_id(1) == pl.num_programs(1) - 1
+        own = pl.program_id(0) < pl.num_programs(0) // 2
+
+        @pl.when(ends & own)
+        def _():
+            own_ref[...] = next_ref[...]
+
+        @pl.when(ends & jnp.logical_not(own))
+        def _():
+            away_ref[...] = next_ref[...].astype(BF16)
 
 
 def across(spec):
@@ -413,14 +430,19 @@
     return up, down
 
 
-def feed_forward(layer, att, x, wout, gain, bias, wup, wdown):
+def feed_forward(layer, last, att, x, wout, gain, bias, wup, wdown):
     rows, width = x.rows, x.width
     hidden = wup.shape[2]
     tile = min(512, rows // 2)
     chunk = 512
     wide = pl.BlockSpec((tile, chunk), lambda i, c: (i, c))
+    tiles = rows // 2 // tile
+    halves = [
+        pl.BlockSpec((tile, width), lambda i, c: (jnp.minimum(i, tiles - 1), 0)),
+        pl.BlockSpec((tile, width), lambda i, c: (jnp.maximum(i - tiles, 0), 0)),
+    ]
     return pl.pallas_call(
-        functools.partial(feed_kernel, x, tile),
+        functools.partial(feed_kernel, x, tile, last),
         grid=(rows // tile, hidden // chunk),
         in_specs=[
             across(spec)
@@ -435,17 +457,25 @@
             across(columns_of(width, tile)),
             wide,
             wide,
-            across(rows_of(tile, width)),
-        ],
+        ]
+        + (halves if last else [across(rows_of(tile, width))]),
         out_shape=[
             jax.ShapeDtypeStruct((rows, width), F32),
             jax.ShapeDtypeStruct((width, rows), BF16),
             jax.ShapeDtypeStruct((width, rows), BF16),
             jax.ShapeDtypeStruct((rows, hidden), BF16),
             jax.ShapeDtypeStruct((rows, hidden), BF16),
-            jax.ShapeDtypeStruct((rows, width), F32),
-        ],
-        scratch_shapes=[pltpu.VMEM((tile, width), BF16)],
+        ]
+        + (
+            [
+                jax.ShapeDtypeStruct((rows // 2, width), F32),
+                jax.ShapeDtypeStruct((rows // 2, width), BF16),
+            ]
+            if last
+            else [jax.ShapeDtypeStruct((rows, width), F32)]
+        ),
+        scratch_shapes=[pltpu.VMEM((tile, width), BF16)]
+        + ([pltpu.VMEM((tile, width), F32)] if last else []),
         compiler_params=params(),
         cost_estimate=pl.CostEstimate(
             flops=2 * rows * width * (width + 2 * hidden),
@@ -1257,8 +1287,10 @@
         return exchange(value, "blk", blk_size, half)
 
     def own_and_other(pair):
-        first = mine == 0
-        return jnp.where(first, pair[0], pair[1]), jnp.where(first, pair[1], pair[0])
+        return tuple(
+            lax.dynamic_index_in_dim(pair, which, 0, keepdims=False)
+            for which in (mine, 1 - mine)
+        )
 
     def collect(pair):
         own, other = own_and_other(pair)
@@ -1290,15 +1322,16 @@
         h1, q, kv = qkv_forward(layer, state, norm_gain, norm_bias, w_qkv, first)
         kv_parts = gather_parts(kv)
         att, inverse, p = attend(q, kv_parts, dead_parts)
-        mid, h2, att_turned, active, slope, after = feed_forward(
-            layer, att, state, w_out, norm_gain, norm_bias, w_up, w_down
+        last_one = layer == LAYERS - 1
+        mid, h2, att_turned, active, slope, *after = feed_forward(
+            layer, last_one, att, state, w_out, norm_gain, norm_bias, w_up, w_down
         )
         kept.append(
             (state, h1, q, kv_parts, att, inverse, p, mid, h2, att_turned, active, slope)
         )
-        state = Tokens([after])
-    came = swap(after[block_len:].astype(BF16))
-    hidden_out, placed = place_cells(mine[None], after, came)
+        state = Tokens(after)
+    came = swap(after[1])
+    hidden_out, placed = place_cells(mine[None], after[0], came)
 
     sizes = {"blk": blk_size, "dp": dp_size}
     places = {"blk": place, "dp": lax.axis_index("dp")}
@@ -1408,7 +1441,7 @@
             own_grad, small = qkv_backward(
                 layer, 0, F32, dq, dkv, own_x, norm_gain, w_qkv, dmid, small, species, last
             )
-            added, (small,) = fold(moving, (own_grad, came), (small,))
+            added, (small,) = fold(moving, (own_grad,), (small,))
             last = (added,)
     small = SmallSum(small, sizes)
     moving.append(small)

time: 593 us -> 618 us (1.042)
  Pallas kernels: 449 us -> 472 us
  local copies, waits for them, and re-layouts: 11.9 us -> 18.5 us
    pallas_call x2, Pallas kernels: 74.7 us -> 91.5 us  [attend(): pl.pallas_call(functools.partial(attend_kernel, parts), grid=(pairs, rows...]
    pallas_call x4, Pallas kernels: 121 us -> 127 us  [attend_back(): pl.pallas_call(without(functools.partial(attend_back_kernel, parts), 5 +...]
  transfers between devices with their start and end apart: 48 -> 48, of which waited for: 16 -> 11; matrix products, arithmetic and copies ran while one was open for 2% -> 1% of each run, Pallas kernels for 52% -> 52%
where the time goes in v2:
time: 618 us; the launch traced here: 609 us
  Pallas kernels  472 us (76%)
  waiting for transfers between devices  62.4 us (10%)
  starting transfers between devices  39.9 us (6%)
  local copies, waits for them, and re-layouts  18.5 us (3%)
  between operations  15.3 us (2%)
    pallas_call x4, Pallas kernels, attend_back(): pl.pallas_call(without(functools.partial(attend_back_kernel, parts), 5 +...  127 us
    pallas_call x2, Pallas kernels, attend(): pl.pallas_call(functools.partial(attend_kernel, parts), grid=(pairs, rows...  91.5 us
    pallas_call x2, Pallas kernels, feed_backward(): pl.pallas_call(without(functools.partial(feed_back_kernel, layer, grad, d...  82.2 us
    pallas_call x2, Pallas kernels, feed_forward(): pl.pallas_call(functools.partial(feed_kernel, x, tile, last), grid=(rows...  56.6 us
    ppermute x37, waiting for transfers between devices, exchange(): return lax.ppermute(value, axis, [(i, i ^ bit) for i in range(size)])  51.1 us
    pallas_call x2, Pallas kernels, qkv_gradients(): pl.pallas_call(without(functools.partial(qkv_grad_kernel, layer, groups,...  41.3 us
    pallas_call x10, Pallas kernels, fold(): pl.pallas_call(kernel, grid_spec=pltpu.PrefetchScalarGridSpec(num_scalar_...  39.4 us
    ppermute x37, starting transfers between devices, exchange(): return lax.ppermute(value, axis, [(i, i ^ bit) for i in range(size)])  38.7 us
  transfers between devices with their start and end apart: 48, of which 11 were waited for; matrix products, arithmetic and copies ran while one was open for 1% of the time, Pallas kernels for 52%

profile of v2, /device:TPU:0, one launch (start us, length us, event | category | flops | bytes accessed | tf_op | source)
XLA Modules:
  0.0 609.3 jit_solution(17457791863953641850)
XLA Ops:
  13.9 16.3 %collective-permute-done.1 = s32[512]{0:T(512)S(1)} collective-permute-done((s32[512]{0:T(512)S(1)}, s32[512]{0:T(512)S(1)}, u32[]{:S(2)}, u32[]{:S(2)}) %collective-permute-start.1) | collective-permute-done | bytes 2080 | tf_op jit(solution)/shard_map/ppermute | solution.py:1259
  33.3 8.8 %norm_qkv.2 = (bf16[768,1024]{1,0:T(8,128)(2,1)}, bf16[1024,768]{1,0:T(8,128)(2,1)}, bf16[1024,1536]{1,0:T(8,128)(2,1)}) custom-call(bf16[512,768]{1,0:T(8,128)(2,1)} %get-tuple-element.284.refs_0_.refs_6_, bf16[512,768]{1,0:T(8,128)(2,1)} %copy-done.15, f32[1,768]{1,0:T(1,128)} %broadcast_select_fusion.refs_2_.refs_8_.refs_7_, f32[2,2,768]{2,1,0:T(2,128)} %refs_8_.9, ...), custom_call_target="tpu_custom_call" | custom-call | flops 3623878656 | bytes 9437184 | tf_op jit(solution)/shard_map/norm_qkv/pallas_call | solution.py:157
  42.2 5.8 collective-permute-done.3.refs_2_.refs_4_.refs_6_.refs_8_
  48.0 45.7 %attend.2 = (bf16[1024,768]{1,0:T(8,128)(2,1)}, f32[1024,768]{1,0:T(8,128)}, bf16[12,1024,2048]{2,1,0:T(8,128)(2,1)}) custom-call(bf16[1024,768]{1,0:T(8,128)(2,1)} %get-tuple-element.145.refs_0_, bf16[1024,1536]{1,0:T(8,128)(2,1)} %get-tuple-element.146.refs_1_.refs_3_.refs_5_.refs_7_, ...), custom_call_target="tpu_custom_call" | custom-call | flops 25769803776 | bytes 50331648 | tf_op jit(solution)/shard_map/attend/pallas_call | solution.py:245
  93.7 27.5 %feed.2 = (f32[1024,768]{1,0:T(8,128)}, bf16[768,1024]{1,0:T(8,128)(2,1)}, bf16[768,1024]{1,0:T(8,128)(2,1)}, bf16[1024,3072]{1,0:T(8,128)(2,1)}, bf16[1024,3072]{1,0:T(8,128)(2,1)}, /*index=5*/f32[1024,768]{1,0:T(8,128)}) custom-call(bf16[512,768]{1,0:T(8,128)(2,1)} %get-tuple-element.284.refs_0_.refs_6_, bf16[512,768]{1,0:T(8,128)(2,1)} %copy-done.15, ...), custom_call_target="tpu_custom_call" | custom-call | flops 10871635968 | bytes 34603008 | tf_op jit(solution)/shard_map/feed/pallas_call | solution.py:444
  121.2 9.0 %norm_qkv.3 = (bf16[768,1024]{1,0:T(8,128)(2,1)}, bf16[1024,768]{1,0:T(8,128)(2,1)}, bf16[1024,1536]{1,0:T(8,128)(2,1)}) custom-call(f32[1024,768]{1,0:T(8,128)} %get-tuple-element.148.refs_0_.refs_7_, f32[2,2,768]{2,1,0:T(2,128)} %refs_8_.9, f32[2,2,768]{2,1,0:T(2,128)} %refs_4_.5, bf16[2,768,2304]{2,1,0:T(8,128)(2,1)} %refs_9_.9), custom_call_target="tpu_custom_call" | custom-call | flops 3623878656 | bytes 9437184 | tf_op jit(solution)/shard_map/norm_qkv/pallas_call | solution.py:157
  136.2 45.8 %attend.3 = (bf16[1024,768]{1,0:T(8,128)(2,1)}, f32[1024,768]{1,0:T(8,128)}, bf16[12,1024,2048]{2,1,0:T(8,128)(2,1)}) custom-call(bf16[1024,768]{1,0:T(8,128)(2,1)} %get-tuple-element.149.refs_0_, bf16[1024,1536]{1,0:T(8,128)(2,1)} %get-tuple-element.150.refs_1_.refs_3_.refs_5_.refs_7_, ...), custom_call_target="tpu_custom_call" | custom-call | flops 25769803776 | bytes 50331648 | tf_op jit(solution)/shard_map/attend/pallas_call | solution.py:245
  182.0 29.1 %feed.3 = (f32[1024,768]{1,0:T(8,128)}, bf16[768,1024]{1,0:T(8,128)(2,1)}, bf16[768,1024]{1,0:T(8,128)(2,1)}, bf16[1024,3072]{1,0:T(8,128)(2,1)}, bf16[1024,3072...) custom-call(f32[1024,768]{1,0:T(8,128)} %get-tuple-element.148.refs_0_.refs_7_, ...), custom_call_target="tpu_custom_call" | custom-call | flops 10871635968 | bytes 34603008 | tf_op jit(solution)/shard_map/feed/pallas_call | solution.py:444
  211.7 41.0 %feed_back.2 = (bf16[8,2,96,960]{3,2,1,0:T(8,128)(2,1)}, bf16[8,2,96,960]{3,2,1,0:T(8,128)(2,1)}, bf16[8,2,192,384]{3,2,1,0:T(8,128)(2,1)}, bf16[8,2,192,384]{3,...) custom-call(s32[1]{0:T(128)} %bitcast.6.refs_0_, ...), custom_call_target="tpu_custom_call" | custom-call | flops 21743271936 | bytes 47185920 | tf_op jit(solution)/shard_map/feed_back/pallas_call | solution.py:633
  255.0 31.9 %attend_back.4 = (bf16[1024,384]{1,0:T(8,128)(2,1)}, bf16[2,1024,384]{2,1,0:T(8,128)(2,1)}, bf16[2,1024,384]{2,1,0:T(8,128)(2,1)}) custom-call(bf16[1024,768]{1,0:T(8,128)(2,1)} %get-tuple-element.149.refs_0_, f32[1024,768]{1,0:T(8,128)} %get-tuple-element.156.refs_1_, bf16[1024,768]{1,0:T(8,128)(2,1)} %get-tuple-element.151.refs_1_.refs_2_, ...), custom_call_target="tpu_custom_call" | custom-call | flops 25769803776 | bytes 25165824 | tf_op jit(solution)/shard_map/attend_back/pallas_call | solution.py:334
  286.9 6.8 %fold.10 = (bf16[16,1,1,96,960]{4,3,2,1,0:T(8,128)(2,1)}, bf16[16,1,1,192,384]{4,3,2,1,0:T(8,128)(2,1)}, f32[8,128]{1,0:T(8,128)}) custom-call(s32[1]{0:T(128)} %constant.167.clone.1.side_ref, bf16[16,1,1,96,960]{4,3,2,1,0:T(8,128)(2,1)} %bitcast.150, bf16[16,1,1,96,960]{4,3,2,1,0:T(8,128)(2,1)} %bitcast.11.refs_1_, bf16[16,1,1,192,384]{4,3,2,1,0:T(8,128)(2,1)} %bitcast.154, ...), custom_call_target="tpu_custom_call" | custom-call | flops 2655232 | bytes 15931392 | tf_op jit(solution)/shard_map/fold/pallas_call | solution.py:1233
  293.9 31.7 %attend_back.5 = (bf16[1024,384]{1,0:T(8,128)(2,1)}, bf16[2,1024,384]{2,1,0:T(8,128)(2,1)}, bf16[2,1024,384]{2,1,0:T(8,128)(2,1)}) custom-call(bf16[1024,768]{1,0:T(8,128)(2,1)} %get-tuple-element.149.refs_0_, f32[1024,768]{1,0:T(8,128)} %get-tuple-element.156.refs_1_, bf16[1024,768]{1,0:T(8,128)(2,1)} %get-tuple-element.151.refs_1_.refs_2_, ...), custom_call_target="tpu_custom_call" | custom-call | flops 25769803776 | bytes 25165824 | tf_op jit(solution)/shard_map/attend_back/pallas_call | solution.py:334
  329.5 21.9 %qkv_grad.2 = (bf16[8,2,96,576]{3,2,1,0:T(8,128)(2,1)}, bf16[8,2,96,576]{3,2,1,0:T(8,128)(2,1)}, f32[1024,768]{1,0:T(8,128)}, f32[16,768]{1,0:T(8,128)}) custom-call(s32[1]{0:T(128)} %bitcast.6.refs_0_, bf16[1024,384]{1,0:T(8,128)(2,1)} %get-tuple-element.164.refs_4_.refs_1_, bf16[1024,384]{1,0:T(8,128)(2,1)} %get-tuple-element.170.refs_2_.refs_14_, ...), custom_call_target="tpu_custom_call" | custom-call | flops 7247757312 | bytes 25165824 | tf_op jit(solution)/shard_map/qkv_grad/pallas_call | solution.py:796
  351.9 41.2 %feed_back.3 = (bf16[8,2,96,960]{3,2,1,0:T(8,128)(2,1)}, bf16[8,2,96,960]{3,2,1,0:T(8,128)(2,1)}, bf16[8,2,192,384]{3,2,1,0:T(8,128)(2,1)}, bf16[8,2,192,384]{3,...) custom-call(s32[1]{0:T(128)} %bitcast.6.refs_0_, ...), custom_call_target="tpu_custom_call" | custom-call | flops 21743271936 | bytes 47185920 | tf_op jit(solution)/shard_map/feed_back/pallas_call | solution.py:633
  400.9 32.1 %attend_back.6 = (bf16[1024,384]{1,0:T(8,128)(2,1)}, bf16[2,1024,384]{2,1,0:T(8,128)(2,1)}, bf16[2,1024,384]{2,1,0:T(8,128)(2,1)}) custom-call(bf16[1024,768]{1,0:T(8,128)(2,1)} %get-tuple-element.145.refs_0_, f32[1024,768]{1,0:T(8,128)} %get-tuple-element.155.refs_1_, bf16[1024,768]{1,0:T(8,128)(2,1)} %get-tuple-element.147.refs_3_.refs_2_, ...), custom_call_target="tpu_custom_call" | custom-call | flops 25769803776 | bytes 25165824 | tf_op jit(solution)/shard_map/attend_back/pallas_call | solution.py:334
  433.0 9.0 %fold.12 = (bf16[2,1,2,96,576]{4,3,2,1,0:T(8,128)(2,1)}, bf16[2,1,2,96,576]{4,3,2,1,0:T(8,128)(2,1)}, bf16[8,1,1,96,960]{4,3,2,1,0:T(8,128)(2,1)}, bf16[8,1,1,96...) custom-call(s32[7]{0:T(128)} %stack.39.side_ref, ...), custom_call_target="tpu_custom_call" | custom-call | flops 3097600 | bytes 18585600 | tf_op jit(solution)/shard_map/fold/pallas_call | solution.py:1233
  444.7 31.7 %attend_back.7 = (bf16[1024,384]{1,0:T(8,128)(2,1)}, bf16[2,1024,384]{2,1,0:T(8,128)(2,1)}, bf16[2,1024,384]{2,1,0:T(8,128)(2,1)}) custom-call(bf16[1024,768]{1,0:T(8,128)(2,1)} %get-tuple-element.145.refs_0_, f32[1024,768]{1,0:T(8,128)} %get-tuple-element.155.refs_1_, bf16[1024,768]{1,0:T(8,128)(2,1)} %get-tuple-element.147.refs_3_.refs_2_, ...), custom_call_target="tpu_custom_call" | custom-call | flops 25769803776 | bytes 25165824 | tf_op jit(solution)/shard_map/attend_back/pallas_call | solution.py:334
  479.2 5.1 fold.13
  489.7 19.4 %qkv_grad.3 = (bf16[8,2,96,576]{3,2,1,0:T(8,128)(2,1)}, bf16[8,2,96,576]{3,2,1,0:T(8,128)(2,1)}, bf16[512,768]{1,0:T(8,128)(2,1)}, f32[16,768]{1,0:T(8,128)}) custom-call(s32[1]{0:T(128)} %bitcast.6.refs_0_, bf16[1024,384]{1,0:T(8,128)(2,1)} %get-tuple-element.190.refs_12_.refs_1_.refs_0_, bf16[1024,384]{1,0:T(8,128)(2,1)} %get-tuple-element.198.refs_15_.refs_2_.refs_1_, ...), custom_call_target="tpu_custom_call" | custom-call | flops 7247757312 | bytes 25165824 | tf_op jit(solution)/shard_map/qkv_grad/pallas_call | solution.py:796
  518.6 8.0 %qkv_back.1 = (f32[512,768]{1,0:T(8,128)}, f32[16,768]{1,0:T(8,128)}) custom-call(bf16[1024,384]{1,0:T(8,128)(2,1)} %get-tuple-element.190.refs_12_.refs_1_.refs_0_, bf16[1024,384]{1,0:T(8,128)(2,1)} %get-tuple-element.198.refs_15_.refs_2_.refs_1_, bf16[2,1024,384]{2,1,0:T(8,128)(2,1)} %get-tuple-element.199.refs_3_.refs_2_, ...), custom_call_target="tpu_custom_call" | custom-call | flops 1811939328 | bytes 9437184 | tf_op jit(solution)/shard_map/qkv_back/pallas_call | solution.py:867
  526.6 16.3 %collective-permute-done.24 = bf16[1,1,1,96,576]{4,3,2,1,0:T(8,128)(2,1)} collective-permute-done((bf16[1,1,1,96,576]{4,3,2,1,0:T(8,128)(2,1)}, bf16[1,1,1,96,576]{4,3,2,1,0:T(8,128)(2,1)}, u32[]{:S(2)}, u32[]{:S(2)}) %collective-permute-start.24) | collective-permute-done | bytes 110624 | tf_op jit(solution)/shard_map/ppermute | solution.py:1259
  542.9 5.1 fold.15
  571.5 7.7 %collective-permute-done.29 = bf16[1,1,1,192,384]{4,3,2,1,0:T(8,128)(2,1)S(1)} collective-permute-done((bf16[1,1,1,192,384]{4,3,2,1,0:T(8,128)(2,1)}, bf16[1,1,1,192,384]{4,3,2,1,0:T(8,128)(2,1)S(1)}, u32[]{:S(2)}, u32[]{:S(2)}) %collective-permute-start.29) | collective-permute-done | bytes 147488 | tf_op jit(solution)/shard_map/ppermute | solution.py:1259
  596.9 4.5 collective-permute-done.42.refs_6_
  (156 shorter events, 92.6 us)
Async XLA Ops:
  7.2 469.2 %reduce-scatter.7.cloned.1.call-start = ((), (), s32[]{:S(2)}) async-start(), calls=%async_computation.5 | async-start | bytes 2654208 | tf_op jit(solution)/shard_map/reduce_scatter | solution.py:997
  133.0 78.1 %collective-permute-start.6 = (bf16[512,768]{1,0:T(8,128)(2,1)}, bf16[512,768]{1,0:T(8,128)(2,1)}, u32[]{:S(2)}, u32[]{:S(2)}) collective-permute-start(bf16[512,768]{1,0:T(8,128)(2,1)} %get-tuple-element.281), channel_id=1, source_target_pairs={{0,2},{1,3},{2,0},{3,1},{4,6},{5,7},{6,4},{7,5},{8,10},{9,11},{10,... | collective-permute-start | bytes 2359304 | tf_op jit(solution)/shard_map/ppermute | solution.py:1259
  252.7 34.2 %collective-permute-start.7 = (bf16[16,96,960]{2,1,0:T(8,128)(2,1)}, bf16[16,96,960]{2,1,0:T(8,128)(2,1)}, u32[]{:S(2)}, u32[]{:S(2)}) collective-permute-start(bf16[16,96,960]{2,1,0:T(8,128)(2,1)} %bitcast.171), channel_id=1, source_target_pairs={{0,1},{1,0},{2,3},{3,2},{4,5},{5,4},{6,7},{7,6},{8,9},{9,8},{10,11... | collective-permute-start | bytes 8847368 | tf_op jit(solution)/shard_map/ppermute | solution.py:1259
  252.9 34.0 %collective-permute-start.8 = (bf16[16,192,384]{2,1,0:T(8,128)(2,1)}, bf16[16,192,384]{2,1,0:T(8,128)(2,1)}, u32[]{:S(2)}, u32[]{:S(2)}) collective-permute-start(bf16[16,192,384]{2,1,0:T(8,128)(2,1)} %bitcast.173), channel_id=1, source_target_pairs={{0,1},{1,0},{2,3},{3,2},{4,5},{5,4},{6,7},{7,6},{8,9},{9,8},{10,11... | collective-permute-start | bytes 7077896 | tf_op jit(solution)/shard_map/ppermute | solution.py:1259
  253.3 33.7 %collective-permute-start.5 = (bf16[512,768]{1,0:T(8,128)(2,1)}, bf16[512,768]{1,0:T(8,128)(2,1)}, u32[]{:S(2)}, u32[]{:S(2)}) collective-permute-start(bf16[512,768]{1,0:T(8,128)(2,1)} %get-tuple-element.153), channel_id=1, source_target_pairs={{0,2},{1,3},{2,0},{3,1},{4,6},{5,7},{6,4},{7,5},{8,10},{9,11},{10,... | collective-permute-start | bytes 2359304 | tf_op jit(solution)/shard_map/ppermute | solution.py:1259
  293.8 182.6 %reduce-scatter.5.cloned.1.call-start = ((), (), s32[]{:S(2)}) async-start(), calls=%async_computation.4 | async-start | bytes 3538944 | tf_op jit(solution)/shard_map/reduce_scatter | solution.py:997
  293.9 32.4 %collective-permute-start.9 = (bf16[2,1024,384]{2,1,0:T(8,128)(2,1)}, bf16[2,1024,384]{2,1,0:T(8,128)(2,1)}, u32[]{:S(2)}, u32[]{:S(2)}) collective-permute-start(bf16[2,1024,384]{2,1,0:T(8,128)(2,1)} %get-tuple-element.172), channel_id=1, source_target_pairs={{0,1},{1,0},{2,3},{3,2},{4,5},{5,4},{6,7},{7,6},{8,9},{9,8},{10,11... | collective-permute-start | bytes 4718600 | tf_op jit(solution)/shard_map/ppermute | solution.py:1304
  326.2 235.0 %reduce-scatter.11.cloned.1.call-start = ((), (), s32[]{:S(2)}) async-start(), calls=%async_computation.7 | async-start | bytes 442368 | tf_op jit(solution)/shard_map/reduce_scatter | solution.py:1013
  351.5 44.0 %collective-permute-start.11 = (bf16[16,96,576]{2,1,0:T(8,128)(2,1)}, bf16[16,96,576]{2,1,0:T(8,128)(2,1)}, u32[]{:S(2)}, u32[]{:S(2)}) collective-permute-start(bf16[16,96,576]{2,1,0:T(8,128)(2,1)} %bitcast.174), channel_id=1, source_target_pairs={{0,1},{1,0},{2,3},{3,2},{4,5},{5,4},{6,7},{7,6},{8,9},{9,8},{10,11... | collective-permute-start | bytes 5308424 | tf_op jit(solution)/shard_map/ppermute | solution.py:1259
  393.1 39.9 %collective-permute-start.13 = (bf16[16,96,960]{2,1,0:T(8,128)(2,1)}, bf16[16,96,960]{2,1,0:T(8,128)(2,1)}, u32[]{:S(2)}, u32[]{:S(2)}) collective-permute-start(bf16[16,96,960]{2,1,0:T(8,128)(2,1)} %bitcast.170), channel_id=1, source_target_pairs={{0,1},{1,0},{2,3},{3,2},{4,5},{5,4},{6,7},{7,6},{8,9},{9,8},{10,11... | collective-permute-start | bytes 8847368 | tf_op jit(solution)/shard_map/ppermute | solution.py:1259
  395.1 37.9 %collective-permute-start.14 = (bf16[16,192,384]{2,1,0:T(8,128)(2,1)}, bf16[16,192,384]{2,1,0:T(8,128)(2,1)}, u32[]{:S(2)}, u32[]{:S(2)}) collective-permute-start(bf16[16,192,384]{2,1,0:T(8,128)(2,1)} %bitcast.172), channel_id=1, source_target_pairs={{0,1},{1,0},{2,3},{3,2},{4,5},{5,4},{6,7},{7,6},{8,9},{9,8},{10,11... | collective-permute-start | bytes 7077896 | tf_op jit(solution)/shard_map/ppermute | solution.py:1259
  399.4 33.6 %collective-permute-start.12 = (bf16[4,1,2,96,576]{4,3,2,1,0:T(8,128)(2,1)}, bf16[4,1,2,96,576]{4,3,2,1,0:T(8,128)(2,1)}, u32[]{:S(2)}, u32[]{:S(2)}) collective-permute-start(bf16[4,1,2,96,576]{4,3,2,1,0:T(8,128)(2,1)} %get-tuple-element.192), channel_id=1, source_target_pairs={{0,4},{4,0},{8,12},{12,8},{16,20},{20,16},{24,28},{28,24},{1,5},{5... | collective-permute-start | bytes 2654216 | tf_op jit(solution)/shard_map/ppermute | solution.py:1259
  433.0 43.4 %collective-permute-start.15 = (bf16[2,1024,384]{2,1,0:T(8,128)(2,1)}, bf16[2,1024,384]{2,1,0:T(8,128)(2,1)}, u32[]{:S(2)}, u32[]{:S(2)}) collective-permute-start(bf16[2,1024,384]{2,1,0:T(8,128)(2,1)} %get-tuple-element.200), channel_id=1, source_target_pairs={{0,1},{1,0},{2,3},{3,2},{4,5},{5,4},{6,7},{7,6},{8,9},{9,8},{10,11... | collective-permute-start | bytes 4718600 | tf_op jit(solution)/shard_map/ppermute | solution.py:1304
  442.0 37.2 %collective-permute-start.17 = (bf16[8,1,1,96,960]{4,3,2,1,0:T(8,128)(2,1)}, bf16[8,1,1,96,960]{4,3,2,1,0:T(8,128)(2,1)}, u32[]{:S(2)}, u32[]{:S(2)}) collective-permute-start(bf16[8,1,1,96,960]{4,3,2,1,0:T(8,128)(2,1)} %get-tuple-element.205), channel_id=1, source_target_pairs={{0,2},{1,3},{2,0},{3,1},{4,6},{5,7},{6,4},{7,5},{8,10},{9,11},{10,... | collective-permute-start | bytes 4423688 | tf_op jit(solution)/shard_map/ppermute | solution.py:1259
  442.7 33.7 %collective-permute-start.18 = (bf16[4,1,2,192,384]{4,3,2,1,0:T(8,128)(2,1)}, bf16[4,1,2,192,384]{4,3,2,1,0:T(8,128)(2,1)}, u32[]{:S(2)}, u32[]{:S(2)}) collective-permute-start(bf16[4,1,2,192,384]{4,3,2,1,0:T(8,128)(2,1)} %get-tuple-element.207), channel_id=1, source_target_pairs={{0,4},{4,0},{8,12},{12,8},{16,20},{20,16},{24,28},{28,24},{1,5},{5... | collective-permute-start | bytes 3538952 | tf_op jit(solution)/shard_map/ppermute | solution.py:1259
  442.9 33.5 %collective-permute-start.16 = (bf16[2,1,2,96,576]{4,3,2,0,1:T(8,128)(2,1)}, bf16[2,1,2,96,576]{4,3,2,0,1:T(8,128)(2,1)}, u32[]{:S(2)}, u32[]{:S(2)}) collective-permute-start(bf16[2,1,2,96,576]{4,3,2,0,1:T(8,128)(2,1)} %bitcast.177), channel_id=1, source_target_pairs={{0,8},{4,12},{8,0},{12,4},{16,24},{20,28},{24,16},{28,20},{1,9},{5... | collective-permute-start | bytes 1327112 | tf_op jit(solution)/shard_map/ppermute | solution.py:1259
  484.4 24.8 %collective-permute-start.21 = (bf16[4,1,1,96,960]{4,3,2,1,0:T(8,128)(2,1)}, bf16[4,1,1,96,960]{4,3,2,1,0:T(8,128)(2,1)}, u32[]{:S(2)}, u32[]{:S(2)}) collective-permute-start(bf16[4,1,1,96,960]{4,3,2,1,0:T(8,128)(2,1)} %get-tuple-element.220), channel_id=1, source_target_pairs={{0,4},{4,0},{8,12},{12,8},{16,20},{20,16},{24,28},{28,24},{1,5},{5... | collective-permute-start | bytes 2211848 | tf_op jit(solution)/shard_map/ppermute | solution.py:1259
  485.6 23.6 %collective-permute-start.22 = (bf16[2,1,2,192,384]{4,3,2,0,1:T(8,128)(2,1)}, bf16[2,1,2,192,384]{4,3,2,0,1:T(8,128)(2,1)}, u32[]{:S(2)}, u32[]{:S(2)}) collective-permute-start(bf16[2,1,2,192,384]{4,3,2,0,1:T(8,128)(2,1)} %bitcast.175), channel_id=1, source_target_pairs={{0,8},{4,12},{8,0},{12,4},{16,24},{20,28},{24,16},{28,20},{1,9},{5... | collective-permute-start | bytes 1769480 | tf_op jit(solution)/shard_map/ppermute | solution.py:1259
  513.0 29.9 %collective-permute-start.27 = (bf16[16,96,576]{2,1,0:T(8,128)(2,1)}, bf16[16,96,576]{2,1,0:T(8,128)(2,1)}, u32[]{:S(2)}, u32[]{:S(2)}) collective-permute-start(bf16[16,96,576]{2,1,0:T(8,128)(2,1)} %bitcast.155), channel_id=1, source_target_pairs={{0,1},{1,0},{2,3},{3,2},{4,5},{5,4},{6,7},{7,6},{8,9},{9,8},{10,11... | collective-permute-start | bytes 5308424 | tf_op jit(solution)/shard_map/ppermute | solution.py:1259
  513.1 48.0 %reduce-scatter.9.cloned.1.call-start = ((), (), s32[]{:S(2)}) async-start(), calls=%async_computation.6 | async-start | bytes 589824 | tf_op jit(solution)/shard_map/reduce_scatter | solution.py:1013
  513.2 29.7 %collective-permute-start.25 = (bf16[2,1,1,96,960]{4,3,0,2,1:T(8,128)(2,1)}, bf16[2,1,1,96,960]{4,3,0,2,1:T(8,128)(2,1)}, u32[]{:S(2)}, u32[]{:S(2)}) collective-permute-start(bf16[2,1,1,96,960]{4,3,0,2,1:T(8,128)(2,1)} %bitcast.178), channel_id=1, source_target_pairs={{0,8},{4,12},{8,0},{12,4},{16,24},{20,28},{24,16},{28,20},{1,9},{5... | collective-permute-start | bytes 1105928 | tf_op jit(solution)/shard_map/ppermute | solution.py:1259
  513.7 43.5 %collective-permute-start.23 = (bf16[512,768]{1,0:T(8,128)(2,1)}, bf16[512,768]{1,0:T(8,128)(2,1)}, u32[]{:S(2)}, u32[]{:S(2)}) collective-permute-start(bf16[512,768]{1,0:T(8,128)(2,1)} %get-tuple-element.228), channel_id=1, source_target_pairs={{0,2},{1,3},{2,0},{3,1},{4,6},{5,7},{6,4},{7,5},{8,10},{9,11},{10,... | collective-permute-start | bytes 2359304 | tf_op jit(solution)/shard_map/ppermute | solution.py:1259
  514.3 28.6 %collective-permute-start.26 = (bf16[1,1,2,192,384]{4,3,2,1,0:T(8,128)(2,1)}, bf16[1,1,2,192,384]{4,3,2,1,0:T(8,128)(2,1)}, u32[]{:S(2)}, u32[]{:S(2)}) collective-permute-start(bf16[1,1,2,192,384]{4,3,2,1,0:T(8,128)(2,1)} %get-tuple-element.235), channel_id=1, source_target_pairs={{0,16},{4,20},{8,24},{12,28},{16,0},{20,4},{24,8},{28,12},{1,17},{... | collective-permute-start | bytes 884744 | tf_op jit(solution)/shard_map/ppermute | solution.py:1259
  517.1 25.8 %collective-permute-start.24 = (bf16[1,1,1,96,576]{4,3,2,1,0:T(8,128)(2,1)}, bf16[1,1,1,96,576]{4,3,2,1,0:T(8,128)(2,1)}, u32[]{:S(2)}, u32[]{:S(2)}) collective-permute-start(bf16[1,1,1,96,576]{4,3,2,1,0:T(8,128)(2,1)} %get-tuple-element.231), channel_id=1, source_target_pairs={{0,2},{1,3},{2,0},{3,1},{4,6},{5,7},{6,4},{7,5},{8,10},{9,11},{10,... | collective-permute-start | bytes 331784 | tf_op jit(solution)/shard_map/ppermute | solution.py:1259
  (42 other events, 325.4 us)
Sparse Core Ops, SparseCore 0:
  293.9 69.2 reduce-scatter.6
  366.9 81.3 reduce-scatter.4
  513.3 13.1 reduce-scatter.10
  528.5 15.9 reduce-scatter.8

commit v3 on v2

--- a/solution.py
+++ b/solution.py
@@ -106,6 +106,13 @@
     return value.T.astype(BF16)
 
 
+def token_of(ref):
+    ref[...] = jnp.zeros_like(ref)
+
+
+TOKEN = jax.ShapeDtypeStruct((8, 128), F32)
+
+
 class Tokens:
     def __init__(self, arrays, shift=None):
         self.arrays = arrays
@@ -141,7 +148,8 @@
 
 
 def qkv_kernel(x, tile, *refs):
-    gain_ref, bias_ref, w_ref, h_ref, q_ref, kv_ref = refs[x.count() :]
+    gain_ref, bias_ref, w_ref, h_ref, q_ref, kv_ref, token_ref = refs[x.count() :]
+    token_of(token_ref)
     width = x.width
     n, _ = normalise(x.read(tile, refs[: x.count()]))
     h = n * gain_ref[0:1, :] + bias_ref[0:1, :]
@@ -151,27 +159,42 @@
     q_ref[...] = (mm(h, w_ref[:, :width]) * (SCALE * LOG2E)).astype(BF16)
 
 
-def qkv_forward(layer, x, gain, bias, w, after):
-    rows, width = x.rows, x.width
+def qkv_forward(layer, x, gain, bias, w, after, rows=None, held=None):
+    width = x.width
+    rows = rows or x.rows
     tile = min(256, rows // 2)
+    held = held or []
+    offset = (rows - x.rows) // tile if held else 0
     return pl.pallas_call(
-        without(functools.partial(qkv_kernel, x, tile), x.count() + 3, len(after)),
-        grid=(rows // tile,),
+        without(
+            functools.partial(qkv_kernel, x, tile), x.count() + 3, len(held) + len(after)
+        ),
+        grid=(x.rows // tile,),
         in_specs=x.specs(tile)
         + [layer_of(value, layer) for value in (gain, bias, w)]
+        + ordered(held)
         + ordered(after),
-        out_specs=[columns_of(width, tile), rows_of(tile, width), rows_of(tile, 2 * width)],
+        out_specs=[
+            pl.BlockSpec((width, tile), lambda i: (0, i + offset)),
+            pl.BlockSpec((tile, width), lambda i: (i + offset, 0)),
+            pl.BlockSpec((tile, 2 * width), lambda i: (i + offset, 0)),
+            pl.BlockSpec(TOKEN.shape, lambda i: (0, 0)),
+        ],
         out_shape=[
             jax.ShapeDtypeStruct((width, rows), BF16),
             jax.ShapeDtypeStruct((rows, width), BF16),
             jax.ShapeDtypeStruct((rows, 2 * width), BF16),
+            TOKEN,
         ],
+        input_output_aliases={x.count() + 3 + i: i for i in range(len(held))},
         compiler_params=params(),
         cost_estimate=pl.CostEstimate(
-            flops=6 * rows * width * width, bytes_accessed=12 * rows * width, transcendentals=0
+            flops=6 * x.rows * width * width,
+            bytes_accessed=12 * x.rows * width,
+            transcendentals=0,
         ),
         name="norm_qkv",
-    )(*x.operands(), gain, bias, w, *after)
+    )(*x.operands(), gain, bias, w, *held, *after)
 
 
 def lanes_like(shape):
@@ -209,8 +232,8 @@
             extra = jnp.where(sub == 3, dead_refs[part][...].astype(F32), 0.0)
             ka[own, :] = jnp.where(low, k, extra).astype(BF16)
             kb[own, :] = jnp.where(low, extra, k).astype(BF16)
-            va[:, own] = turned(jnp.where(low, v, 1.0))
-            vb[:, own] = turned(jnp.where(low, 1.0, v))
+            va[own, :] = jnp.where(low, v, 1.0).astype(BF16)
+            vb[own, :] = jnp.where(low, 1.0, v).astype(BF16)
 
     low, sub = lanes_like(q_ref.shape)
     fourth = jnp.where(sub == 3, 1.0, 0.0)
@@ -219,15 +242,13 @@
     sb = mm_nt(jnp.where(low, fourth, q).astype(BF16), kb[...])
     pa = jnp.exp2(sa - jnp.max(sa, axis=-1, keepdims=True)).astype(BF16)
     p_ref[0] = pa
-    oa = mm_nt(va[...], pa)
+    oa = mm(pa, va[...])
     pb = jnp.exp2(sb - jnp.max(sb, axis=-1, keepdims=True)).astype(BF16)
     p_ref[1] = pb
-    ob = mm_nt(vb[...], pb)
-    inverse_a = 1.0 / oa[HEAD_DIM:, :]
-    inverse_b = 1.0 / ob[:HEAD_DIM, :]
-    value = jnp.concatenate([oa[:HEAD_DIM, :] * inverse_a, ob[HEAD_DIM:, :] * inverse_b], axis=0)
-    inverse_ref[...] = jnp.concatenate([inverse_a, inverse_b], axis=0).T
-    o_ref[...] = turned(value)
+    ob = mm(pb, vb[...])
+    inverse = 1.0 / pltpu.roll(jnp.where(low, ob, oa), HEAD_DIM, 1)
+    inverse_ref[...] = inverse
+    o_ref[...] = (jnp.where(low, oa, ob) * inverse).astype(BF16)
 
 
 def attend(q, kv_parts, dead_parts):
@@ -241,7 +262,6 @@
     second = pl.BlockSpec((rows, PAIR), lambda j, i: (0, pairs + j))
     fixed = pl.BlockSpec((rows, PAIR), lambda j, i: (0, 0))
     scratch = pltpu.VMEM((keys, PAIR), BF16)
-    turned_scratch = pltpu.VMEM((PAIR, keys), BF16)
     return pl.pallas_call(
         functools.partial(attend_kernel, parts),
         grid=(pairs, rows // tile),
@@ -252,7 +272,7 @@
             jax.ShapeDtypeStruct((rows, width), F32),
             jax.ShapeDtypeStruct((2 * pairs, rows, keys), BF16),
         ],
-        scratch_shapes=[scratch] * 2 + [turned_scratch] * 2,
+        scratch_shapes=[scratch] * 4,
         compiler_params=params(),
         cost_estimate=pl.CostEstimate(
             flops=16 * rows * keys * width,
@@ -280,7 +300,7 @@
         ones = jnp.where(sub < 3, 1.0, 0.0)
         for part in range(parts):
             own = slice(part * rows, (part + 1) * rows)
-            ks[:, own] = turned(k_refs[part][...].astype(F32))
+            ks[own, :] = k_refs[part][...]
             v = v_refs[part][...].astype(F32)
             va[own, :] = jnp.where(low, v, ones).astype(BF16)
             vb[own, :] = jnp.where(low, ones, v).astype(BF16)
@@ -301,13 +321,13 @@
     pa, pb = p_ref[0], p_ref[1]
     dv_turned[first, :] += mm(datt_turned[first, :], pa)
     ga = (pa.astype(F32) * ta).astype(BF16)
-    dqa = mm_nt(ks[first, :], ga)
+    dqa = mm(ga, ks[...])
     dk_turned[first, :] += mm(q_turned[first, :], ga)
     dv_turned[second, :] += mm(datt_turned[second, :], pb)
     gb = (pb.astype(F32) * tb).astype(BF16)
-    dqb = mm_nt(ks[second, :], gb)
+    dqb = mm(gb, ks[...])
     dk_turned[second, :] += mm(q_turned[second, :], gb)
-    dq_ref[...] = turned(jnp.concatenate([dqa, dqb], axis=0) * SCALE)
+    dq_ref[...] = (jnp.where(low, dqa, dqb) * SCALE).astype(BF16)
 
     @pl.when(index == pl.num_programs(1) - 1)
     def _():
@@ -342,7 +362,7 @@
         out_specs=[pl.BlockSpec((tile, PAIR), lambda j, i: (i, j))] + [both] * parts,
         out_shape=[jax.ShapeDtypeStruct((rows, count * PAIR), BF16)]
         + [jax.ShapeDtypeStruct((2, rows, count * PAIR), BF16)] * parts,
-        scratch_shapes=[pltpu.VMEM((PAIR, keys), BF16)] + [all_keys] * 2 + [turned_keys] * 2,
+        scratch_shapes=[all_keys] * 3 + [turned_keys] * 2,
         compiler_params=params(),
         cost_estimate=pl.CostEstimate(
             flops=32 * rows * keys * width // groups,
@@ -900,13 +920,6 @@
     )
 
 
-def token_of(ref):
-    ref[...] = jnp.zeros_like(ref)
-
-
-TOKEN = jax.ShapeDtypeStruct((8, 128), F32)
-
-
 def place_kernel(mine_ref, own_ref, came_ref, out_ref, token_ref):
     token_of(token_ref)
     mine = pl.program_id(0) == mine_ref[0]
@@ -1306,11 +1319,7 @@
     def gather_parts(value):
         return [value] + [turn(value, by) for by in range(1, half)]
 
-    ids = jnp.concatenate(collect(gene_ids))
-    dead = jnp.where(ids != 0, 0.0, MASKED).astype(BF16)
-    dead_parts = [
-        jnp.broadcast_to(part[:, None], (part.shape[0], PAIR)) for part in gather_parts(dead)
-    ]
+    ids = collect(gene_ids)
     species, _ = own_and_other(species_flag)
     picked = jnp.where(species == 0, species_table[0], species_table[1])
     state = Tokens(collect(embedded), picked[None, :])
@@ -1318,8 +1327,19 @@
 
     kept = []
     for layer in range(LAYERS):
-        first = tuple(dead_parts) if layer == 0 else ()
-        h1, q, kv = qkv_forward(layer, state, norm_gain, norm_bias, w_qkv, first)
+        norm = (norm_gain, norm_bias, w_qkv)
+        if layer == 0:
+            own, away = (Tokens([array], state.shift) for array in state.arrays)
+            *some, token = qkv_forward(layer, own, *norm, (), state.rows)
+            masked = [jnp.where(part != 0, 0.0, MASKED) + token[0, 0] for part in ids]
+            dead = jnp.concatenate(masked).astype(BF16)
+            dead_parts = [
+                jnp.broadcast_to(part[:, None], (part.shape[0], PAIR))
+                for part in gather_parts(dead)
+            ]
+            h1, q, kv, _ = qkv_forward(layer, away, *norm, (dead,), state.rows, some)
+        else:
+            h1, q, kv, _ = qkv_forward(layer, state, *norm, ())
         kv_parts = gather_parts(kv)
         att, inverse, p = attend(q, kv_parts, dead_parts)
         last_one = layer == LAYERS - 1
@@ -1441,7 +1461,10 @@
             own_grad, small = qkv_backward(
                 layer, 0, F32, dq, dkv, own_x, norm_gain, w_qkv, dmid, small, species, last
             )
+            later = [one for one in moving if one.layer > 0 and one.results is of_qkv]
+            moving = [one for one in moving if one not in later]
             added, (small,) = fold(moving, (own_grad,), (small,))
+            moving += later
             last = (added,)
     small = SmallSum(small, sizes)
     moving.append(small)

time: 618 us -> 584 us (0.945)
  Pallas kernels: 472 us -> 451 us
  waiting for transfers between devices: 62.4 us -> 43.6 us
    ppermute x37, waiting for transfers between devices: 51.1 us -> 33.3 us  [exchange(): return lax.ppermute(value, axis, [(i, i ^ bit) for i in range(size)])]
    pallas_call x2, Pallas kernels: 91.5 us -> 74.9 us  [attend(): pl.pallas_call(functools.partial(attend_kernel, parts), grid=(pairs, rows...]
    pallas_call x4, Pallas kernels: 127 us -> 121 us  [attend_back(): pl.pallas_call(without(functools.partial(attend_back_kernel, parts), 5 +...]
    pallas_call x2 -> x3, Pallas kernels: 17.7 us -> 20.6 us  [qkv_forward(): pl.pallas_call(without(functools.partial(qkv_kernel, x, tile), x.count()...]
  transfers between devices with their start and end apart: 48 -> 48, of which waited for: 11 -> 16; matrix products, arithmetic and copies ran while one was open for 1% -> 2% of each run, Pallas kernels for 52% -> 54%
where the time goes in v3:
time: 584 us; the launch traced here: 575 us
  Pallas kernels  451 us (77%)
  waiting for transfers between devices  43.6 us (7%)
  starting transfers between devices  38.8 us (7%)
  local copies, waits for them, and re-layouts  22.1 us (4%)
  between operations  15.1 us (3%)
    pallas_call x4, Pallas kernels, attend_back(): pl.pallas_call(without(functools.partial(attend_back_kernel, parts), 5 +...  121 us
    pallas_call x2, Pallas kernels, feed_backward(): pl.pallas_call(without(functools.partial(feed_back_kernel, layer, grad, d...  81.8 us
    pallas_call x2, Pallas kernels, attend(): pl.pallas_call(functools.partial(attend_kernel, parts), grid=(pairs, rows...  74.9 us
    pallas_call x2, Pallas kernels, feed_forward(): pl.pallas_call(functools.partial(feed_kernel, x, tile, last), grid=(rows...  56.5 us
    pallas_call x2, Pallas kernels, qkv_gradients(): pl.pallas_call(without(functools.partial(qkv_grad_kernel, layer, groups,...  41.1 us
    pallas_call x10, Pallas kernels, fold(): pl.pallas_call(kernel, grid_spec=pltpu.PrefetchScalarGridSpec(num_scalar_...  39.7 us
    ppermute x37, starting transfers between devices, exchange(): return lax.ppermute(value, axis, [(i, i ^ bit) for i in range(size)])  37.4 us
    ppermute x37, waiting for transfers between devices, exchange(): return lax.ppermute(value, axis, [(i, i ^ bit) for i in range(size)])  33.3 us
  transfers between devices with their start and end apart: 48, of which 16 were waited for; matrix products, arithmetic and copies ran while one was open for 2% of the time, Pallas kernels for 54%

profile of v3, /device:TPU:0, one launch (start us, length us, event | category | flops | bytes accessed | tf_op | source)
XLA Modules:
  0.0 575.2 jit_solution(12012103666753021097)
XLA Ops:
  15.4 5.9 %norm_qkv.3 = (bf16[768,1024]{1,0:T(8,128)(2,1)}, bf16[1024,768]{1,0:T(8,128)(2,1)}, bf16[1024,1536]{1,0:T(8,128)(2,1)}, f32[8,128]{1,0:T(8,128)}) custom-call(bf16[512,768]{1,0:T(8,128)(2,1)} %get-tuple-element.292.refs_0_.refs_6_, f32[1,768]{1,0:T(1,128)} %broadcast_select_fusion.refs_1_.refs_2_.refs_8_.refs_7_, f32[2,2,768]{2,1,0:T(2,128)} %refs_8_.9, ...), custom_call_target="tpu_custom_call" | custom-call | flops 1811939328 | bytes 4718592 | tf_op jit(solution)/shard_map/norm_qkv/pallas_call | solution.py:168
  23.8 7.0 %collective-permute-done.1 = s32[512]{0:T(512)} collective-permute-done((s32[512]{0:T(512)}, s32[512]{0:T(512)}, u32[]{:S(2)}, u32[]{:S(2)}) %collective-permute-start.1) | collective-permute-done | bytes 2080 | tf_op jit(solution)/shard_map/ppermute | solution.py:1272
  32.7 5.8 %norm_qkv.4 = (bf16[768,1024]{1,0:T(8,128)(2,1)}, bf16[1024,768]{1,0:T(8,128)(2,1)}, bf16[1024,1536]{1,0:T(8,128)(2,1)}, f32[8,128]{1,0:T(8,128)}) custom-call(bf16[512,768]{1,0:T(8,128)(2,1)} %collective-permute-done.refs_0_.refs_1_.refs_7_, ...), custom_call_target="tpu_custom_call", output_to_operand_aliasing={{0}: (5, {}), {1}: (6, {}), {2}: (7, {})} | custom-call | flops 1811939328 | bytes 4718592 | tf_op jit(solution)/shard_map/norm_qkv/pallas_call | solution.py:168
  39.0 5.0 collective-permute-done.3
  47.0 37.2 %attend.2 = (bf16[1024,768]{1,0:T(8,128)(2,1)}, f32[1024,768]{1,0:T(8,128)}, bf16[12,1024,2048]{2,1,0:T(8,128)(2,1)}) custom-call(bf16[1024,768]{1,0:T(8,128)(2,1)} %get-tuple-element.153.refs_0_, bf16[1024,1536]{1,0:T(8,128)(2,1)} %get-tuple-element.154.refs_1_.refs_3_.refs_5_.refs_7_, ...), custom_call_target="tpu_custom_call" | custom-call | flops 25769803776 | bytes 50331648 | tf_op jit(solution)/shard_map/attend/pallas_call | solution.py:265
  84.2 27.5 %feed.2 = (f32[1024,768]{1,0:T(8,128)}, bf16[768,1024]{1,0:T(8,128)(2,1)}, bf16[768,1024]{1,0:T(8,128)(2,1)}, bf16[1024,3072]{1,0:T(8,128)(2,1)}, bf16[1024,3072]{1,0:T(8,128)(2,1)}, /*index=5*/f32[1024,768]{1,0:T(8,128)}) custom-call(bf16[512,768]{1,0:T(8,128)(2,1)} %get-tuple-element.292.refs_0_.refs_6_, ...), custom_call_target="tpu_custom_call" | custom-call | flops 10871635968 | bytes 34603008 | tf_op jit(solution)/shard_map/feed/pallas_call | solution.py:464
  111.7 9.0 %norm_qkv.5 = (bf16[768,1024]{1,0:T(8,128)(2,1)}, bf16[1024,768]{1,0:T(8,128)(2,1)}, bf16[1024,1536]{1,0:T(8,128)(2,1)}, f32[8,128]{1,0:T(8,128)}) custom-call(f32[1024,768]{1,0:T(8,128)} %get-tuple-element.156.refs_0_.refs_7_, f32[2,2,768]{2,1,0:T(2,128)} %refs_8_.9, f32[2,2,768]{2,1,0:T(2,128)} %refs_4_.7, bf16[2,768,2304]{2,1,0:T(8,128)(2,1)} %refs_9_.9), custom_call_target="tpu_custom_call" | custom-call | flops 3623878656 | bytes 9437184 | tf_op jit(solution)/shard_map/norm_qkv/pallas_call | solution.py:168
  126.7 37.6 %attend.3 = (bf16[1024,768]{1,0:T(8,128)(2,1)}, f32[1024,768]{1,0:T(8,128)}, bf16[12,1024,2048]{2,1,0:T(8,128)(2,1)}) custom-call(bf16[1024,768]{1,0:T(8,128)(2,1)} %get-tuple-element.157.refs_0_, bf16[1024,1536]{1,0:T(8,128)(2,1)} %get-tuple-element.158.refs_1_.refs_3_.refs_5_.refs_7_, ...), custom_call_target="tpu_custom_call" | custom-call | flops 25769803776 | bytes 50331648 | tf_op jit(solution)/shard_map/attend/pallas_call | solution.py:265
  164.3 29.0 %feed.3 = (f32[1024,768]{1,0:T(8,128)}, bf16[768,1024]{1,0:T(8,128)(2,1)}, bf16[768,1024]{1,0:T(8,128)(2,1)}, bf16[1024,3072]{1,0:T(8,128)(2,1)}, bf16[1024,3072...) custom-call(f32[1024,768]{1,0:T(8,128)} %get-tuple-element.156.refs_0_.refs_7_, ...), custom_call_target="tpu_custom_call" | custom-call | flops 10871635968 | bytes 34603008 | tf_op jit(solution)/shard_map/feed/pallas_call | solution.py:464
  193.9 40.4 %feed_back.2 = (bf16[8,2,96,960]{3,2,1,0:T(8,128)(2,1)}, bf16[8,2,96,960]{3,2,1,0:T(8,128)(2,1)}, bf16[8,2,192,384]{3,2,1,0:T(8,128)(2,1)}, bf16[8,2,192,384]{3,...) custom-call(s32[1]{0:T(128)} %bitcast.6.refs_0_, ...), custom_call_target="tpu_custom_call" | custom-call | flops 21743271936 | bytes 47185920 | tf_op jit(solution)/shard_map/feed_back/pallas_call | solution.py:653
  236.7 30.2 %attend_back.4 = (bf16[1024,384]{1,0:T(8,128)(2,1)}, bf16[2,1024,384]{2,1,0:T(8,128)(2,1)}, bf16[2,1024,384]{2,1,0:T(8,128)(2,1)}) custom-call(bf16[1024,768]{1,0:T(8,128)(2,1)} %get-tuple-element.157.refs_0_, f32[1024,768]{1,0:T(8,128)} %get-tuple-element.164.refs_1_, bf16[1024,768]{1,0:T(8,128)(2,1)} %get-tuple-element.159.refs_1_.refs_2_, ...), custom_call_target="tpu_custom_call" | custom-call | flops 25769803776 | bytes 25165824 | tf_op jit(solution)/shard_map/attend_back/pallas_call | solution.py:354
  266.9 6.8 %fold.10 = (bf16[16,1,1,96,960]{4,3,2,1,0:T(8,128)(2,1)}, bf16[16,1,1,192,384]{4,3,2,1,0:T(8,128)(2,1)}, f32[8,128]{1,0:T(8,128)}) custom-call(s32[1]{0:T(128)} %constant.167.clone.1.side_ref, bf16[16,1,1,96,960]{4,3,2,1,0:T(8,128)(2,1)} %bitcast.151, bf16[16,1,1,96,960]{4,3,2,1,0:T(8,128)(2,1)} %bitcast.11.refs_1_, bf16[16,1,1,192,384]{4,3,2,1,0:T(8,128)(2,1)} %bitcast.155, ...), custom_call_target="tpu_custom_call" | custom-call | flops 2655232 | bytes 15931392 | tf_op jit(solution)/shard_map/fold/pallas_call | solution.py:1246
  273.9 30.1 %attend_back.5 = (bf16[1024,384]{1,0:T(8,128)(2,1)}, bf16[2,1024,384]{2,1,0:T(8,128)(2,1)}, bf16[2,1024,384]{2,1,0:T(8,128)(2,1)}) custom-call(bf16[1024,768]{1,0:T(8,128)(2,1)} %get-tuple-element.157.refs_0_, f32[1024,768]{1,0:T(8,128)} %get-tuple-element.164.refs_1_, bf16[1024,768]{1,0:T(8,128)(2,1)} %get-tuple-element.159.refs_1_.refs_2_, ...), custom_call_target="tpu_custom_call" | custom-call | flops 25769803776 | bytes 25165824 | tf_op jit(solution)/shard_map/attend_back/pallas_call | solution.py:354
  307.8 21.7 %qkv_grad.2 = (bf16[8,2,96,576]{3,2,1,0:T(8,128)(2,1)}, bf16[8,2,96,576]{3,2,1,0:T(8,128)(2,1)}, f32[1024,768]{1,0:T(8,128)}, f32[16,768]{1,0:T(8,128)}) custom-call(s32[1]{0:T(128)} %bitcast.6.refs_0_, bf16[1024,384]{1,0:T(8,128)(2,1)} %get-tuple-element.172.refs_4_.refs_1_, bf16[1024,384]{1,0:T(8,128)(2,1)} %get-tuple-element.178.refs_2_.refs_14_, ...), custom_call_target="tpu_custom_call" | custom-call | flops 7247757312 | bytes 25165824 | tf_op jit(solution)/shard_map/qkv_grad/pallas_call | solution.py:816
  330.1 41.4 %feed_back.3 = (bf16[8,2,96,960]{3,2,1,0:T(8,128)(2,1)}, bf16[8,2,96,960]{3,2,1,0:T(8,128)(2,1)}, bf16[8,2,192,384]{3,2,1,0:T(8,128)(2,1)}, bf16[8,2,192,384]{3,...) custom-call(s32[1]{0:T(128)} %bitcast.6.refs_0_, ...), custom_call_target="tpu_custom_call" | custom-call | flops 21743271936 | bytes 47185920 | tf_op jit(solution)/shard_map/feed_back/pallas_call | solution.py:653
  379.2 30.3 %attend_back.6 = (bf16[1024,384]{1,0:T(8,128)(2,1)}, bf16[2,1024,384]{2,1,0:T(8,128)(2,1)}, bf16[2,1024,384]{2,1,0:T(8,128)(2,1)}) custom-call(bf16[1024,768]{1,0:T(8,128)(2,1)} %get-tuple-element.153.refs_0_, f32[1024,768]{1,0:T(8,128)} %get-tuple-element.163.refs_1_, bf16[1024,768]{1,0:T(8,128)(2,1)} %get-tuple-element.155.refs_3_.refs_2_, ...), custom_call_target="tpu_custom_call" | custom-call | flops 25769803776 | bytes 25165824 | tf_op jit(solution)/shard_map/attend_back/pallas_call | solution.py:354
  409.9 9.2 %fold.12 = (bf16[2,1,2,96,576]{4,3,2,1,0:T(8,128)(2,1)}, bf16[2,1,2,96,576]{4,3,2,1,0:T(8,128)(2,1)}, bf16[8,1,1,96,960]{4,3,2,1,0:T(8,128)(2,1)}, bf16[8,1,1,96...) custom-call(s32[7]{0:T(128)} %stack.39.side_ref, ...), custom_call_target="tpu_custom_call" | custom-call | flops 3097600 | bytes 18585600 | tf_op jit(solution)/shard_map/fold/pallas_call | solution.py:1246
  422.4 30.1 %attend_back.7 = (bf16[1024,384]{1,0:T(8,128)(2,1)}, bf16[2,1024,384]{2,1,0:T(8,128)(2,1)}, bf16[2,1024,384]{2,1,0:T(8,128)(2,1)}) custom-call(bf16[1024,768]{1,0:T(8,128)(2,1)} %get-tuple-element.153.refs_0_, f32[1024,768]{1,0:T(8,128)} %get-tuple-element.163.refs_1_, bf16[1024,768]{1,0:T(8,128)(2,1)} %get-tuple-element.155.refs_3_.refs_2_, ...), custom_call_target="tpu_custom_call" | custom-call | flops 25769803776 | bytes 25165824 | tf_op jit(solution)/shard_map/attend_back/pallas_call | solution.py:354
  456.0 5.1 fold.13
  466.6 19.4 %qkv_grad.3 = (bf16[8,2,96,576]{3,2,1,0:T(8,128)(2,1)}, bf16[8,2,96,576]{3,2,1,0:T(8,128)(2,1)}, bf16[512,768]{1,0:T(8,128)(2,1)}, f32[16,768]{1,0:T(8,128)}) custom-call(s32[1]{0:T(128)} %bitcast.6.refs_0_, bf16[1024,384]{1,0:T(8,128)(2,1)} %get-tuple-element.198.refs_12_.refs_1_.refs_0_, bf16[1024,384]{1,0:T(8,128)(2,1)} %get-tuple-element.206.refs_15_.refs_2_.refs_1_, ...), custom_call_target="tpu_custom_call" | custom-call | flops 7247757312 | bytes 25165824 | tf_op jit(solution)/shard_map/qkv_grad/pallas_call | solution.py:816
  493.9 8.0 %qkv_back.1 = (f32[512,768]{1,0:T(8,128)}, f32[16,768]{1,0:T(8,128)}) custom-call(bf16[1024,384]{1,0:T(8,128)(2,1)} %get-tuple-element.198.refs_12_.refs_1_.refs_0_, bf16[1024,384]{1,0:T(8,128)(2,1)} %get-tuple-element.206.refs_15_.refs_2_.refs_1_, bf16[2,1024,384]{2,1,0:T(8,128)(2,1)} %get-tuple-element.207.refs_3_.refs_2_, ...), custom_call_target="tpu_custom_call" | custom-call | flops 1811939328 | bytes 9437184 | tf_op jit(solution)/shard_map/qkv_back/pallas_call | solution.py:887
  501.9 4.3 collective-permute-done.25
  508.3 5.0 fold.15
  539.7 5.4 collective-permute-done.28
  (160 shorter events, 108.8 us)
Async XLA Ops:
  7.2 445.3 %reduce-scatter.7.cloned.1.call-start = ((), (), s32[]{:S(2)}) async-start(), calls=%async_computation.5 | async-start | bytes 2654208 | tf_op jit(solution)/shard_map/reduce_scatter | solution.py:1010
  9.9 22.7 %collective-permute-start = (bf16[512,768]{1,0:T(8,128)(2,1)}, bf16[512,768]{1,0:T(8,128)(2,1)}, u32[]{:S(2)}, u32[]{:S(2)}) collective-permute-start(bf16[512,768]{1,0:T(8,128)(2,1)} %get-tuple-element.291), channel_id=1, source_target_pairs={{0,2},{1,3},{2,0},{3,1},{4,6},{5,7},{6,4},{7,5},{8,10},{9,11},{10,... | collective-permute-start | bytes 2359304 | tf_op jit(solution)/shard_map/ppermute | solution.py:1272
  123.5 69.9 %collective-permute-start.6 = (bf16[512,768]{1,0:T(8,128)(2,1)}, bf16[512,768]{1,0:T(8,128)(2,1)}, u32[]{:S(2)}, u32[]{:S(2)}) collective-permute-start(bf16[512,768]{1,0:T(8,128)(2,1)} %get-tuple-element.289), channel_id=1, source_target_pairs={{0,2},{1,3},{2,0},{3,1},{4,6},{5,7},{6,4},{7,5},{8,10},{9,11},{10,... | collective-permute-start | bytes 2359304 | tf_op jit(solution)/shard_map/ppermute | solution.py:1272
  234.4 32.5 %collective-permute-start.7 = (bf16[16,96,960]{2,1,0:T(8,128)(2,1)}, bf16[16,96,960]{2,1,0:T(8,128)(2,1)}, u32[]{:S(2)}, u32[]{:S(2)}) collective-permute-start(bf16[16,96,960]{2,1,0:T(8,128)(2,1)} %bitcast.169), channel_id=1, source_target_pairs={{0,1},{1,0},{2,3},{3,2},{4,5},{5,4},{6,7},{7,6},{8,9},{9,8},{10,11... | collective-permute-start | bytes 8847368 | tf_op jit(solution)/shard_map/ppermute | solution.py:1272
  234.6 32.3 %collective-permute-start.8 = (bf16[16,192,384]{2,1,0:T(8,128)(2,1)}, bf16[16,192,384]{2,1,0:T(8,128)(2,1)}, u32[]{:S(2)}, u32[]{:S(2)}) collective-permute-start(bf16[16,192,384]{2,1,0:T(8,128)(2,1)} %bitcast.171), channel_id=1, source_target_pairs={{0,1},{1,0},{2,3},{3,2},{4,5},{5,4},{6,7},{7,6},{8,9},{9,8},{10,11... | collective-permute-start | bytes 7077896 | tf_op jit(solution)/shard_map/ppermute | solution.py:1272
  234.9 31.9 %collective-permute-start.5 = (bf16[512,768]{1,0:T(8,128)(2,1)}, bf16[512,768]{1,0:T(8,128)(2,1)}, u32[]{:S(2)}, u32[]{:S(2)}) collective-permute-start(bf16[512,768]{1,0:T(8,128)(2,1)} %get-tuple-element.161), channel_id=1, source_target_pairs={{0,2},{1,3},{2,0},{3,1},{4,6},{5,7},{6,4},{7,5},{8,10},{9,11},{10,... | collective-permute-start | bytes 2359304 | tf_op jit(solution)/shard_map/ppermute | solution.py:1272
  273.7 178.9 %reduce-scatter.5.cloned.1.call-start = ((), (), s32[]{:S(2)}) async-start(), calls=%async_computation.4 | async-start | bytes 3538944 | tf_op jit(solution)/shard_map/reduce_scatter | solution.py:1010
  273.8 30.7 %collective-permute-start.9 = (bf16[2,1024,384]{2,1,0:T(8,128)(2,1)}, bf16[2,1024,384]{2,1,0:T(8,128)(2,1)}, u32[]{:S(2)}, u32[]{:S(2)}) collective-permute-start(bf16[2,1024,384]{2,1,0:T(8,128)(2,1)} %get-tuple-element.180), channel_id=1, source_target_pairs={{0,1},{1,0},{2,3},{3,2},{4,5},{5,4},{6,7},{7,6},{8,9},{9,8},{10,11... | collective-permute-start | bytes 4718600 | tf_op jit(solution)/shard_map/ppermute | solution.py:1317
  304.5 221.2 %reduce-scatter.11.cloned.1.call-start = ((), (), s32[]{:S(2)}) async-start(), calls=%async_computation.7 | async-start | bytes 442368 | tf_op jit(solution)/shard_map/reduce_scatter | solution.py:1026
  329.5 44.3 %collective-permute-start.11 = (bf16[16,96,576]{2,1,0:T(8,128)(2,1)}, bf16[16,96,576]{2,1,0:T(8,128)(2,1)}, u32[]{:S(2)}, u32[]{:S(2)}) collective-permute-start(bf16[16,96,576]{2,1,0:T(8,128)(2,1)} %bitcast.172), channel_id=1, source_target_pairs={{0,1},{1,0},{2,3},{3,2},{4,5},{5,4},{6,7},{7,6},{8,9},{9,8},{10,11... | collective-permute-start | bytes 5308424 | tf_op jit(solution)/shard_map/ppermute | solution.py:1272
  371.4 38.4 %collective-permute-start.13 = (bf16[16,96,960]{2,1,0:T(8,128)(2,1)}, bf16[16,96,960]{2,1,0:T(8,128)(2,1)}, u32[]{:S(2)}, u32[]{:S(2)}) collective-permute-start(bf16[16,96,960]{2,1,0:T(8,128)(2,1)} %bitcast.168), channel_id=1, source_target_pairs={{0,1},{1,0},{2,3},{3,2},{4,5},{5,4},{6,7},{7,6},{8,9},{9,8},{10,11... | collective-permute-start | bytes 8847368 | tf_op jit(solution)/shard_map/ppermute | solution.py:1272
  373.4 36.2 %collective-permute-start.14 = (bf16[16,192,384]{2,1,0:T(8,128)(2,1)}, bf16[16,192,384]{2,1,0:T(8,128)(2,1)}, u32[]{:S(2)}, u32[]{:S(2)}) collective-permute-start(bf16[16,192,384]{2,1,0:T(8,128)(2,1)} %bitcast.170), channel_id=1, source_target_pairs={{0,1},{1,0},{2,3},{3,2},{4,5},{5,4},{6,7},{7,6},{8,9},{9,8},{10,11... | collective-permute-start | bytes 7077896 | tf_op jit(solution)/shard_map/ppermute | solution.py:1272
  377.7 32.1 %collective-permute-start.12 = (bf16[4,1,2,96,576]{4,3,2,1,0:T(8,128)(2,1)}, bf16[4,1,2,96,576]{4,3,2,1,0:T(8,128)(2,1)}, u32[]{:S(2)}, u32[]{:S(2)}) collective-permute-start(bf16[4,1,2,96,576]{4,3,2,1,0:T(8,128)(2,1)} %get-tuple-element.200), channel_id=1, source_target_pairs={{0,4},{4,0},{8,12},{12,8},{16,20},{20,16},{24,28},{28,24},{1,5},{5... | collective-permute-start | bytes 2654216 | tf_op jit(solution)/shard_map/ppermute | solution.py:1272
  409.6 43.0 %collective-permute-start.15 = (bf16[2,1024,384]{2,1,0:T(8,128)(2,1)}, bf16[2,1024,384]{2,1,0:T(8,128)(2,1)}, u32[]{:S(2)}, u32[]{:S(2)}) collective-permute-start(bf16[2,1024,384]{2,1,0:T(8,128)(2,1)} %get-tuple-element.208), channel_id=1, source_target_pairs={{0,1},{1,0},{2,3},{3,2},{4,5},{5,4},{6,7},{7,6},{8,9},{9,8},{10,11... | collective-permute-start | bytes 4718600 | tf_op jit(solution)/shard_map/ppermute | solution.py:1317
  419.1 36.9 %collective-permute-start.17 = (bf16[8,1,1,96,960]{4,3,2,1,0:T(8,128)(2,1)}, bf16[8,1,1,96,960]{4,3,2,1,0:T(8,128)(2,1)}, u32[]{:S(2)}, u32[]{:S(2)}) collective-permute-start(bf16[8,1,1,96,960]{4,3,2,1,0:T(8,128)(2,1)} %get-tuple-element.213), channel_id=1, source_target_pairs={{0,2},{1,3},{2,0},{3,1},{4,6},{5,7},{6,4},{7,5},{8,10},{9,11},{10,... | collective-permute-start | bytes 4423688 | tf_op jit(solution)/shard_map/ppermute | solution.py:1272
  419.8 32.7 %collective-permute-start.18 = (bf16[4,1,2,192,384]{4,3,2,1,0:T(8,128)(2,1)}, bf16[4,1,2,192,384]{4,3,2,1,0:T(8,128)(2,1)}, u32[]{:S(2)}, u32[]{:S(2)}) collective-permute-start(bf16[4,1,2,192,384]{4,3,2,1,0:T(8,128)(2,1)} %get-tuple-element.215), channel_id=1, source_target_pairs={{0,4},{4,0},{8,12},{12,8},{16,20},{20,16},{24,28},{28,24},{1,5},{5... | collective-permute-start | bytes 3538952 | tf_op jit(solution)/shard_map/ppermute | solution.py:1272
  421.0 31.5 %collective-permute-start.16 = (bf16[2,1,2,96,576]{4,3,2,0,1:T(8,128)(2,1)}, bf16[2,1,2,96,576]{4,3,2,0,1:T(8,128)(2,1)}, u32[]{:S(2)}, u32[]{:S(2)}) collective-permute-start(bf16[2,1,2,96,576]{4,3,2,0,1:T(8,128)(2,1)} %bitcast.175), channel_id=1, source_target_pairs={{0,8},{4,12},{8,0},{12,4},{16,24},{20,28},{24,16},{28,20},{1,9},{5... | collective-permute-start | bytes 1327112 | tf_op jit(solution)/shard_map/ppermute | solution.py:1272
  461.1 24.9 %collective-permute-start.21 = (bf16[4,1,1,96,960]{4,3,2,1,0:T(8,128)(2,1)}, bf16[4,1,1,96,960]{4,3,2,1,0:T(8,128)(2,1)}, u32[]{:S(2)}, u32[]{:S(2)}) collective-permute-start(bf16[4,1,1,96,960]{4,3,2,1,0:T(8,128)(2,1)} %get-tuple-element.228), channel_id=1, source_target_pairs={{0,4},{4,0},{8,12},{12,8},{16,20},{20,16},{24,28},{28,24},{1,5},{5... | collective-permute-start | bytes 2211848 | tf_op jit(solution)/shard_map/ppermute | solution.py:1272
  462.3 23.7 %collective-permute-start.22 = (bf16[2,1,2,192,384]{4,3,2,0,1:T(8,128)(2,1)}, bf16[2,1,2,192,384]{4,3,2,0,1:T(8,128)(2,1)}, u32[]{:S(2)}, u32[]{:S(2)}) collective-permute-start(bf16[2,1,2,192,384]{4,3,2,0,1:T(8,128)(2,1)} %bitcast.173), channel_id=1, source_target_pairs={{0,8},{4,12},{8,0},{12,4},{16,24},{20,28},{24,16},{28,20},{1,9},{5... | collective-permute-start | bytes 1769480 | tf_op jit(solution)/shard_map/ppermute | solution.py:1272
  464.0 22.0 %collective-permute-start.20 = (bf16[1,1,2,96,576]{4,3,2,1,0:T(8,128)(2,1)}, bf16[1,1,2,96,576]{4,3,2,1,0:T(8,128)(2,1)}, u32[]{:S(2)}, u32[]{:S(2)}) collective-permute-start(bf16[1,1,2,96,576]{4,3,2,1,0:T(8,128)(2,1)} %get-tuple-element.226), channel_id=1, source_target_pairs={{0,16},{4,20},{8,24},{12,28},{16,0},{20,4},{24,8},{28,12},{1,17},{... | collective-permute-start | bytes 663560 | tf_op jit(solution)/shard_map/ppermute | solution.py:1272
  489.9 18.4 %collective-permute-start.26 = (bf16[16,96,576]{2,1,0:T(8,128)(2,1)}, bf16[16,96,576]{2,1,0:T(8,128)(2,1)}, u32[]{:S(2)}, u32[]{:S(2)}) collective-permute-start(bf16[16,96,576]{2,1,0:T(8,128)(2,1)} %bitcast.156), channel_id=1, source_target_pairs={{0,1},{1,0},{2,3},{3,2},{4,5},{5,4},{6,7},{7,6},{8,9},{9,8},{10,11... | collective-permute-start | bytes 5308424 | tf_op jit(solution)/shard_map/ppermute | solution.py:1272
  490.0 35.6 %reduce-scatter.9.cloned.1.call-start = ((), (), s32[]{:S(2)}) async-start(), calls=%async_computation.6 | async-start | bytes 589824 | tf_op jit(solution)/shard_map/reduce_scatter | solution.py:1026
  490.1 18.2 %collective-permute-start.24 = (bf16[2,1,1,96,960]{4,3,0,2,1:T(8,128)(2,1)}, bf16[2,1,1,96,960]{4,3,0,2,1:T(8,128)(2,1)}, u32[]{:S(2)}, u32[]{:S(2)}) collective-permute-start(bf16[2,1,1,96,960]{4,3,0,2,1:T(8,128)(2,1)} %bitcast.176), channel_id=1, source_target_pairs={{0,8},{4,12},{8,0},{12,4},{16,24},{20,28},{24,16},{28,20},{1,9},{5... | collective-permute-start | bytes 1105928 | tf_op jit(solution)/shard_map/ppermute | solution.py:1272
  490.6 31.2 %collective-permute-start.23 = (bf16[512,768]{1,0:T(8,128)(2,1)}, bf16[512,768]{1,0:T(8,128)(2,1)}, u32[]{:S(2)}, u32[]{:S(2)}) collective-permute-start(bf16[512,768]{1,0:T(8,128)(2,1)} %get-tuple-element.236), channel_id=1, source_target_pairs={{0,2},{1,3},{2,0},{3,1},{4,6},{5,7},{6,4},{7,5},{8,10},{9,11},{10,... | collective-permute-start | bytes 2359304 | tf_op jit(solution)/shard_map/ppermute | solution.py:1272
  (42 other events, 296.1 us)
Sparse Core Ops, SparseCore 0:
  273.9 69.3 reduce-scatter.6
  346.8 83.7 reduce-scatter.4
  490.1 13.1 reduce-scatter.10
  505.4 13.6 reduce-scatter.8
